TPU v7x, 32 devices: a whole 2x2x4 slice. The times are simulated.
32 devices in a mesh: tok: 2 (over core), row: 4 (over y, x), col: 4 (over z).
Axes of the slice: x: 2, y: 2, z: 4, core: 2. Of those that a mesh axis runs over, the one named last changes fastest.
Arguments:
- hidden: bfloat16 [1024, 5120], P('tok', ('row', 'col')), may hold values from -6 to 6
- gains: float32 [2, 5120], P('tok', ('row', 'col')), may hold values from 0.25 to 1.75
- weights: bfloat16 [2, 5120, 2048], P('tok', 'row', 'col'), may hold values from -6 to 6
- lengths: int32 [2], replicated, may hold values from 1 to 512, 768 in all
Outputs:
- merged: float32 [5120, 2048], P(('row', 'tok'), 'col')
Inputs may be any that keep to these rules, and one draw needn't show every extreme that they name: The largest entry of lengths is exactly 512.
All inputs are finite; a program needn't handle non-finite values.
Results may differ from a plain program's by a relative error of at most 0.0054.
Values may be sent and summed in bfloat16 or wider, within the bound.
No kernel may reach another device: no remote copies, remote signals or barrier semaphores. Data moves between devices by JAX's collectives and lax.ppermute only.
A program may use at most 64 MiB of HBM per device.

v0:
```python
import jax
import jax.numpy as jnp
from jax import lax
from jax.sharding import PartitionSpec as P

ITERS = 4


MIXING = 0.9
EPSILON = 1e-06


def body(hidden, gains, weights, lengths):
    row_devices = lax.axis_size("row")
    col_devices = lax.axis_size("col")
    tok_devices = lax.axis_size("tok")
    slots, width_dev = hidden.shape
    model_width = width_dev * row_devices * col_devices
    sub_rows = model_width // (row_devices * tok_devices)
    length = lengths[lax.axis_index("tok")]
    values = hidden.astype(jnp.float32)
    squares = lax.psum(jnp.sum(values * values, axis=1), ("row", "col"))
    inverse_rms = lax.rsqrt(squares / model_width + EPSILON)
    live_mask = (jnp.arange(slots, dtype=jnp.int32) < length).astype(jnp.float32)
    normed = (values * (inverse_rms * live_mask)[:, None] * gains[0][None, :]).astype(jnp.bfloat16)
    row_block = lax.all_gather(normed, "col", axis=1, tiled=True)
    gram_term = lax.dot_general(
        lax.all_gather(normed, ("row", "col"), axis=1, tiled=True),
        normed,
        (((0,), (0,)), ((), ())),
        preferred_element_type=jnp.float32,
    )
    gram_term = gram_term.reshape(row_devices, tok_devices, sub_rows, width_dev)
    gram_term = jnp.transpose(gram_term, (1, 0, 2, 3)).reshape(model_width, width_dev)
    gram_share = lax.psum_scatter(gram_term, "tok", scatter_dimension=0, tiled=True)
    operator = lax.all_gather(gram_share, "col", axis=1, tiled=True)
    diag_block = lax.dynamic_slice(
        operator,
        (lax.axis_index("row") * sub_rows, lax.axis_index("tok") * sub_rows),
        (sub_rows, sub_rows),
    )
    diagonal = jnp.diagonal(diag_block)
    w_local = weights[0]
    partial_value = jnp.dot(row_block, w_local, preferred_element_type=jnp.float32)
    outputs = lax.psum(partial_value, "row").astype(jnp.bfloat16)
    squared = jnp.sum(jnp.square(row_block.astype(jnp.float32)), axis=0)
    product = lax.dot_general(
        row_block, outputs, (((0,), (0,)), ((), ())), preferred_element_type=jnp.float32
    )
    weight_rows = w_local.astype(jnp.float32)
    right = lax.psum_scatter(
        MIXING * product + (1.0 - MIXING) * squared[:, None] * weight_rows,
        "tok",
        scatter_dimension=0,
        tiled=True,
    )

    def column_norms(residual):
        return lax.psum(jnp.sum(residual * residual, axis=0), ("tok", "row"))

    merged = jnp.zeros_like(right)
    residual = right
    direction = right
    norm_now = column_norms(residual)
    for step in range(ITERS):
        gathered = lax.all_gather(direction, "row", axis=0, tiled=True)
        operate_product = lax.dot_general(
            operator,
            gathered,
            (((0,), (0,)), ((), ())),
            precision=lax.Precision.HIGHEST,
            preferred_element_type=jnp.float32,
        )
        summed = lax.psum_scatter(operate_product, "tok", scatter_dimension=0, tiled=True)
        image = MIXING * summed + (1.0 - MIXING) * diagonal[:, None] * direction
        curvature = lax.psum(jnp.sum(direction * image, axis=0), ("tok", "row"))
        step_size = norm_now / curvature
        merged = merged + step_size[None, :] * direction
        residual = residual - step_size[None, :] * image
        norm_next = column_norms(residual)
        direction = residual + (norm_next / norm_now)[None, :] * direction
        norm_now = norm_next
    return merged


def solution(mesh):
    return jax.shard_map(
        body,
        mesh=mesh,
        in_specs=(P("tok", ("row", "col")), P("tok", ("row", "col")), P("tok", "row", "col"), P()),
        out_specs=P(("row", "tok"), "col"),
        check_vma=False,
    )
```

profile of v0, /device:TPU:0, one launch (start us, length us, event | category | flops | bytes accessed | tf_op | source)
XLA Modules:
  0.0 983.9 jit_solution(15010314310392883414)
XLA Ops:
  7.7 43.7 %psum.70 = f32[512]{0:T(512)S(1)} all-reduce(f32[512]{0:T(512)S(1)} %fusion.3), channel_id=1, replica_groups=mesh['tok'=2,'row'=4,'col'=4] {'row','col'}, use_global_device_ids=true, to_apply=%region_1.0 | all-reduce | flops 512 | bytes 4096 | tf_op jit(solution)/shard_map/psum | solution.py:22
  56.7 28.3 %all-gather.8.cloned.1.call-done = bf16[512,1280]{0,1:T(8,128)(2,1)} async-done(((bf16[512,320]{0,1:T(8,128)(2,1)}), bf16[512,1280]{0,1:T(8,128)(2,1)}) %all-gather.8.cloned.1.call-update) | async-done | bytes 1310736 | tf_op jit(solution)/shard_map/all_gather | solution.py:26
  88.5 53.1 %all-reduce.2 = bf16[512,512]{1,0:T(8,128)(2,1)S(1)} all-reduce(f32[512,512]{1,0:T(8,128)} %fusion.1), channel_id=1, replica_groups=mesh['tok'=2,'row'=4,'col'=4] {'row'}, use_global_device_ids=true, to_apply=%region_2.0 | all-reduce | flops 262144 | bytes 1572864 | tf_op jit(solution)/shard_map/psum | solution.py:45
  144.1 39.0 %all-gather.10.cloned.1.call-done = bf16[512,5120]{0,1:T(8,128)(2,1)} async-done(((bf16[512,320]{0,1:T(8,128)(2,1)}), bf16[512,5120]{0,1:T(8,128)(2,1)}) %all-gather.10.cloned.1.call-update) | async-done | bytes 5242896 | tf_op jit(solution)/shard_map/all_gather | solution.py:28
  216.1 12.9 %reduce-scatter.9.cloned.1.call-done = f32[2560,320]{0,1:T(8,128)} async-done(((f32[5120,320]{0,1:T(8,128)}), f32[2560,320]{0,1:T(8,128)}) %reduce-scatter.9.cloned.1.call-update) | async-done | bytes 3276816 | tf_op jit(solution)/shard_map/reduce_scatter | solution.py:35
  229.2 64.1 %all-gather.14.cloned.1.call-done = f32[2560,512]{1,0:T(8,128)} async-done(((f32[640,512]{1,0:T(8,128)}), f32[2560,512]{1,0:T(8,128)}) %all-gather.14.cloned.1.call-update) | async-done | bytes 5242896 | tf_op jit(solution)/shard_map/all_gather | solution.py:66
  293.3 228.2 %all-gather.12.cloned.1.call-done = f32[2560,1280]{0,1:T(8,128)} async-done(((f32[2560,320]{0,1:T(8,128)}), f32[2560,1280]{0,1:T(8,128)}) %all-gather.12.cloned.1.call-update) | async-done | bytes 13107216 | tf_op jit(solution)/shard_map/all_gather | solution.py:36
  521.5 25.1 %fusion.8 = f32[1280,512]{1,0:T(8,128)} fusion(f32[2560,1280]{0,1:T(8,128)} %all-gather.12.cloned.1.call-done, f32[2560,512]{1,0:T(8,128)} %all-gather.14.cloned.1.call-done), kind=kOutput, calls=%fused_computation.37 | convolution fusion | flops 20132659200 | bytes 20971520 | tf_op jit(solution)/shard_map/dot_general | solution.py:67
  558.7 14.3 %all-reduce = (f32[512]{0:T(512)S(1)}, f32[512]{0:T(512)S(1)}) all-reduce(f32[512]{0:T(512)S(1)} %get-tuple-element.6, f32[512]{0:T(512)S(1)} %get-tuple-element.5), channel_id=1, replica_groups=mesh['tok'=2,'row'=4,'col'=4] {'tok','row'}, use_global_device_ids=true, to_apply=%region_6.7 | all-reduce | flops 1024 | bytes 8192 | tf_op jit(solution)/shard_map/psum | solution.py:59
  573.4 14.2 %psum.74 = f32[512]{0:T(512)S(1)} all-reduce(f32[512]{0:T(512)S(1)} %multiply_reduce_fusion.6), channel_id=1, replica_groups=mesh['tok'=2,'row'=4,'col'=4] {'tok','row'}, use_global_device_ids=true, to_apply=%region_12.13 | all-reduce | flops 512 | bytes 4096 | tf_op jit(solution)/shard_map/psum | solution.py:59
  589.1 61.7 %all-gather.16.cloned.1.call-done = f32[2560,512]{1,0:T(8,128)} async-done(((f32[640,512]{1,0:T(8,128)}), f32[2560,512]{1,0:T(8,128)}) %all-gather.16.cloned.1.call-update) | async-done | bytes 5242896 | tf_op jit(solution)/shard_map/all_gather | solution.py:66
  650.8 25.1 %fusion.9 = f32[1280,512]{1,0:T(8,128)} fusion(f32[2560,1280]{0,1:T(8,128)} %all-gather.12.cloned.1.call-done, f32[2560,512]{1,0:T(8,128)} %all-gather.16.cloned.1.call-done), kind=kOutput, calls=%fused_computation.38 | convolution fusion | flops 20132659200 | bytes 20971520 | tf_op jit(solution)/shard_map/dot_general | solution.py:67
  676.0 10.3 %reduce-scatter.13.cloned.1.call-done = f32[640,512]{1,0:T(8,128)} async-done(((f32[1280,512]{1,0:T(8,128)}), f32[640,512]{1,0:T(8,128)}) %reduce-scatter.13.cloned.1.call-update) | async-done | bytes 1310736 | tf_op jit(solution)/shard_map/reduce_scatter | solution.py:74
  687.9 14.8 %psum.75 = f32[512]{0:T(512)S(1)} all-reduce(f32[512]{0:T(512)S(1)} %multiply_reduce_fusion.5), channel_id=1, replica_groups=mesh['tok'=2,'row'=4,'col'=4] {'tok','row'}, use_global_device_ids=true, to_apply=%region_15.16 | all-reduce | flops 512 | bytes 4096 | tf_op jit(solution)/shard_map/psum | solution.py:76
  706.1 14.2 %psum.76 = f32[512]{0:T(512)S(1)} all-reduce(f32[512]{0:T(512)S(1)} %get-tuple-element.9), channel_id=1, replica_groups=mesh['tok'=2,'row'=4,'col'=4] {'tok','row'}, use_global_device_ids=true, to_apply=%region_17.18 | all-reduce | flops 512 | bytes 4096 | tf_op jit(solution)/shard_map/psum | solution.py:59
  723.0 63.2 %all-gather.18.cloned.1.call-done = f32[2560,512]{1,0:T(8,128)} async-done(((f32[640,512]{1,0:T(8,128)}), f32[2560,512]{1,0:T(8,128)}) %all-gather.18.cloned.1.call-update) | async-done | bytes 5242896 | tf_op jit(solution)/shard_map/all_gather | solution.py:66
  786.2 25.1 %fusion.10 = f32[1280,512]{1,0:T(8,128)} fusion(f32[2560,1280]{0,1:T(8,128)} %all-gather.12.cloned.1.call-done, f32[2560,512]{1,0:T(8,128)} %all-gather.18.cloned.1.call-done), kind=kOutput, calls=%fused_computation.39 | convolution fusion | flops 20132659200 | bytes 20971520 | tf_op jit(solution)/shard_map/dot_general | solution.py:67
  811.4 10.3 %reduce-scatter.15.cloned.1.call-done = f32[640,512]{1,0:T(8,128)} async-done(((f32[1280,512]{1,0:T(8,128)}), f32[640,512]{1,0:T(8,128)}) %reduce-scatter.15.cloned.1.call-update) | async-done | bytes 1310736 | tf_op jit(solution)/shard_map/reduce_scatter | solution.py:74
  823.7 14.6 %psum.77 = f32[512]{0:T(512)S(1)} all-reduce(f32[512]{0:T(512)S(1)} %multiply_reduce_fusion.3), channel_id=1, replica_groups=mesh['tok'=2,'row'=4,'col'=4] {'tok','row'}, use_global_device_ids=true, to_apply=%region_20.21 | all-reduce | flops 512 | bytes 4096 | tf_op jit(solution)/shard_map/psum | solution.py:76
  840.8 14.2 %psum.78 = f32[512]{0:T(512)S(1)} all-reduce(f32[512]{0:T(512)S(1)} %multiply_reduce_fusion.2), channel_id=1, replica_groups=mesh['tok'=2,'row'=4,'col'=4] {'tok','row'}, use_global_device_ids=true, to_apply=%region_22.23 | all-reduce | flops 512 | bytes 4096 | tf_op jit(solution)/shard_map/psum | solution.py:59
  858.6 63.2 %all-gather.20.cloned.1.call-done = f32[2560,512]{1,0:T(8,128)} async-done(((f32[640,512]{1,0:T(8,128)}), f32[2560,512]{1,0:T(8,128)}) %all-gather.20.cloned.1.call-update) | async-done | bytes 5242896 | tf_op jit(solution)/shard_map/all_gather | solution.py:66
  921.8 25.1 %fusion.11 = f32[1280,512]{1,0:T(8,128)} fusion(f32[2560,1280]{0,1:T(8,128)} %all-gather.12.cloned.1.call-done, f32[2560,512]{1,0:T(8,128)} %all-gather.20.cloned.1.call-done), kind=kOutput, calls=%fused_computation.40 | convolution fusion | flops 20132659200 | bytes 20971520 | tf_op jit(solution)/shard_map/dot_general | solution.py:67
  947.0 10.3 %reduce-scatter.17.cloned.1.call-done = f32[640,512]{1,0:T(8,128)} async-done(((f32[1280,512]{1,0:T(8,128)}), f32[640,512]{1,0:T(8,128)}) %reduce-scatter.17.cloned.1.call-update) | async-done | bytes 1310736 | tf_op jit(solution)/shard_map/reduce_scatter | solution.py:74
  959.3 14.6 %psum.79 = f32[512]{0:T(512)S(1)} all-reduce(f32[512]{0:T(512)S(1)} %multiply_reduce_fusion.1), channel_id=1, replica_groups=mesh['tok'=2,'row'=4,'col'=4] {'tok','row'}, use_global_device_ids=true, to_apply=%region_25.26 | all-reduce | flops 512 | bytes 4096 | tf_op jit(solution)/shard_map/psum | solution.py:76
  (76 shorter events, 80.8 us)
Async XLA Ops:
  6.5 78.4 %copy-start.5 = (bf16[1,1280,512]{2,1,0:T(8,128)(2,1)S(1)}, bf16[1,1280,512]{2,1,0:T(8,128)(2,1)}, u32[]{:S(2)}) copy-start(bf16[1,1280,512]{2,1,0:T(8,128)(2,1)} %param.6) | copy-start | bytes 3932164
  6.5 78.4 %all-gather.8.cloned.1.call-start = ((), (), s32[]{:S(2)}) async-start(), calls=%async_computation.6 | async-start | bytes 1638400 | tf_op jit(solution)/shard_map/all_gather | solution.py:26
  55.9 127.3 %all-gather.10.cloned.1.call-start = ((), (), s32[]{:S(2)}) async-start(), calls=%async_computation.8 | async-start | bytes 5570560 | tf_op jit(solution)/shard_map/all_gather | solution.py:28
  56.6 158.9 %reduce-scatter.7.cloned.1.call-start = ((), (), s32[]{:S(2)}) async-start(), calls=%async_computation.7 | async-start | bytes 3932160 | tf_op jit(solution)/shard_map/reduce_scatter | solution.py:51
  84.9 3.3 copy-start.4
  144.0 39.1 %copy-start.3 = (bf16[512,320]{0,1:T(8,128)(2,1)S(1)}, bf16[512,320]{0,1:T(8,128)(2,1)}, u32[]{:S(2)}) copy-start(bf16[512,320]{0,1:T(8,128)(2,1)} %fusion.5) | copy-start | bytes 983044
  144.1 84.9 %reduce-scatter.9.cloned.1.call-start = ((), (), s32[]{:S(2)}) async-start(), calls=%async_computation.9 | async-start | bytes 9830400 | tf_op jit(solution)/shard_map/reduce_scatter | solution.py:35
  215.4 77.8 %all-gather.14.cloned.1.call-start = ((), (), s32[]{:S(2)}) async-start(), calls=%async_computation.11 | async-start | bytes 6553600 | tf_op jit(solution)/shard_map/all_gather | solution.py:66
  216.0 305.5 %all-gather.12.cloned.1.call-start = ((), (), s32[]{:S(2)}) async-start(), calls=%async_computation.10 | async-start | bytes 16384000 | tf_op jit(solution)/shard_map/all_gather | solution.py:36
  229.0 328.0 %reduce-scatter.11.cloned.1.call-start = ((), (), s32[]{:S(2)}) async-start(), calls=%async_computation.12 | async-start | bytes 3932160 | tf_op jit(solution)/shard_map/reduce_scatter | solution.py:74
  546.6 104.2 %all-gather.16.cloned.1.call-start = ((), (), s32[]{:S(2)}) async-start(), calls=%async_computation.13 | async-start | bytes 6553600 | tf_op jit(solution)/shard_map/all_gather | solution.py:66
  551.5 5.5 copy-start
  557.0 16.0 %copy-start.2 = (f32[640,512]{1,0:T(8,128)S(1)}, f32[640,512]{1,0:T(8,128)}, u32[]{:S(2)}) copy-start(f32[640,512]{1,0:T(8,128)} %reduce-scatter.11.cloned.1.call-done) | copy-start | bytes 3932164
  589.0 97.3 %reduce-scatter.13.cloned.1.call-start = ((), (), s32[]{:S(2)}) async-start(), calls=%async_computation.14 | async-start | bytes 3932160 | tf_op jit(solution)/shard_map/reduce_scatter | solution.py:74
  675.9 10.4 %copy-start.1 = (f32[640,512]{1,0:T(8,128)S(1)}, f32[640,512]{1,0:T(8,128)}, u32[]{:S(2)}) copy-start(f32[640,512]{1,0:T(8,128)} %multiply_add_fusion.5) | copy-start | bytes 3932164
  676.0 110.3 %all-gather.18.cloned.1.call-start = ((), (), s32[]{:S(2)}) async-start(), calls=%async_computation.15 | async-start | bytes 6553600 | tf_op jit(solution)/shard_map/all_gather | solution.py:66
  723.0 98.7 %reduce-scatter.15.cloned.1.call-start = ((), (), s32[]{:S(2)}) async-start(), calls=%async_computation.16 | async-start | bytes 3932160 | tf_op jit(solution)/shard_map/reduce_scatter | solution.py:74
  811.4 110.4 %all-gather.20.cloned.1.call-start = ((), (), s32[]{:S(2)}) async-start(), calls=%async_computation.17 | async-start | bytes 6553600 | tf_op jit(solution)/shard_map/all_gather | solution.py:66
  858.6 98.7 %reduce-scatter.17.cloned.1.call-start = ((), (), s32[]{:S(2)}) async-start(), calls=%async_computation.18 | async-start | bytes 3932160 | tf_op jit(solution)/shard_map/reduce_scatter | solution.py:74
Sparse Core Ops, SparseCore 0:
  56.0 28.8 all-gather.7
  87.6 95.4 all-gather.9
  185.4 8.7 reduce-scatter.6
  215.6 13.3 reduce-scatter.8
  230.6 62.5 all-gather.13
  294.7 226.7 all-gather.11
  546.8 8.3 reduce-scatter.10
  589.2 61.5 all-gather.15
  676.1 10.1 reduce-scatter.12
  723.1 63.0 all-gather.17
  811.5 10.1 reduce-scatter.14
  858.7 63.0 all-gather.19
  947.1 10.1 reduce-scatter.16
where the time goes:
time: 985 us; the launch traced here: 984 us
  waiting for transfers between devices  593 us (60%)
  blocking collectives  198 us (20%)
  matrix products  113 us (11%)
  local copies, waits for them, and re-layouts  36.3 us (4%)
  other arithmetic  29.4 us (3%)
  between operations  13.4 us (1%)
    all_gather x4, waiting for transfers between devices, body(): gathered = lax.all_gather(direction, 'row', axis=0, tiled=True)  252 us
    all_gather x1, waiting for transfers between devices, body(): operator = lax.all_gather(gram_share, 'col', axis=1, tiled=True)  228 us
    dot_general x4, matrix products, body(): lax.dot_general(operator, gathered, (((0,), (0,)), ((), ())), precision=l...  101 us
    psum x4, blocking collectives, column_norms(): return lax.psum(jnp.sum(residual * residual, axis=0), ('tok', 'row'))  56.8 us
    psum x1, blocking collectives, body(): outputs = lax.psum(partial_value, 'row').astype(jnp.bfloat16)  53.1 us
    psum x3, blocking collectives, body(): curvature = lax.psum(jnp.sum(direction * image, axis=0), ('tok', 'row'))  44 us
    psum x1, blocking collectives, body(): squares = lax.psum(jnp.sum(values * values, axis=1), ('row', 'col'))  43.7 us
    all_gather x1, waiting for transfers between devices, body(): lax.all_gather(normed, ('row', 'col'), axis=1, tiled=True)  39 us
  transfers between devices with their start and end apart: 13, of which 11 were waited for; matrix products, arithmetic and copies ran while one was open for 5% of the time, Pallas kernels for 0%

commit v1 on v0

v1 whole, which is shorter than its diff:
```python
import functools

import jax
import jax.numpy as jnp
from jax import lax
from jax.experimental import pallas as pl
from jax.experimental.pallas import tpu as pltpu
from jax.sharding import PartitionSpec as P

ITERS = 4

MIXING = 0.9
EPSILON = 1e-06

LANES = 128
CHUNK = 512
MOST_TOKENS = 1024
TABLE_OUT = 0


def two_terms(value):
    high = value.astype(jnp.bfloat16).astype(jnp.float32)
    return jnp.concatenate([high, value - high], axis=0).astype(jnp.bfloat16)


def over_features(left, tokens, found):
    slots = tokens.shape[1]
    if slots <= MOST_TOKENS:
        found[...] = jnp.dot(left[...], tokens[...], preferred_element_type=jnp.float32)
        return

    def some(step, carry):
        lanes = pl.ds(pl.multiple_of(step * CHUNK, CHUNK), CHUNK)
        found[:, lanes] = jnp.dot(left[...], tokens[:, lanes], preferred_element_type=jnp.float32)
        return carry

    lax.fori_loop(0, slots // CHUNK, some, 0)


def over_tokens(left, tokens, part):
    slots = tokens.shape[1]
    product = functools.partial(
        lax.dot_general, dimension_numbers=(((1,), (1,)), ((), ())), preferred_element_type=jnp.float32
    )
    if slots <= MOST_TOKENS:
        return product(left[...], tokens[part, :])

    def some(step, total):
        lanes = pl.ds(pl.multiple_of(step * CHUNK, CHUNK), CHUNK)
        return total + product(left[:, lanes], tokens[part, lanes])

    return lax.fori_loop(0, slots // CHUNK, some, jnp.zeros((left.shape[0], CHUNK), jnp.float32))


def solve_kernel(owners, models, block, copies, places, table_ref, live_ref, owner_ref, squares_ref, gains_ref, *refs):
    pieces = refs[:len(copies)]
    weight_pieces = refs[len(copies):len(copies) + len(places)]
    out_refs = refs[len(copies) + len(places):-12]
    tokens, weights, squared, diagonal, residual, direction, merged, terms, values, outputs, seen, sems = refs[-12:]
    width, slots = tokens.shape
    columns = residual.shape[0]
    started = []
    for piece, parts in zip(pieces, copies):
        for source, entry, part, lanes in parts:
            start = pl.multiple_of(table_ref[entry] * block, 16)
            lane = pl.multiple_of(table_ref[part] * lanes, LANES)
            copy = pltpu.make_async_copy(
                piece.at[source],
                tokens.at[pl.ds(start, block), pl.ds(lane, lanes)],
                sems.at[0],
            )
            copy.start()
            started.append(copy)
    for piece, (entry, part) in zip(weight_pieces, places):
        held, row_width = piece.shape
        lane = pl.multiple_of(table_ref[entry] * row_width, LANES)
        row = pl.multiple_of(table_ref[part] * held, held)
        copy = pltpu.make_async_copy(
            piece, weights.at[pl.ds(row, held), pl.ds(lane, row_width)], sems.at[1]
        )
        copy.start()
        started.append(copy)
    for copy in started:
        copy.wait()

    inverse_rms = lax.rsqrt(squares_ref[...] / width + EPSILON) * live_ref[...]

    def norm_rows(step, carry):
        start = pl.multiple_of(step * LANES, LANES)
        gains = gains_ref[pl.ds(start, LANES), :]
        sums = [jnp.zeros((LANES, LANES), jnp.float32) for _ in range(models)]
        for tile, owner in enumerate(owners):
            lanes = slice(tile * LANES, (tile + 1) * LANES)
            value = tokens[pl.ds(start, LANES), lanes].astype(jnp.float32)
            if owner < 0:
                gain = jnp.where(owner_ref[:, lanes] > 0, gains[:, 1:2], gains[:, 0:1])
            else:
                gain = gains[:, owner:owner + 1]
            normed = (value * inverse_rms[:, lanes] * gain).astype(jnp.bfloat16)
            tokens[pl.ds(start, LANES), lanes] = normed
            value = normed.astype(jnp.float32)
            value = value * value
            if owner < 0:
                theirs = value * owner_ref[:, lanes]
                sums[0] = sums[0] + (value - theirs)
                sums[1] = sums[1] + theirs
            else:
                sums[owner] = sums[owner] + value
        sums = [jnp.sum(part.T, axis=0, keepdims=True) for part in sums]
        for model in range(models):
            squared[model:model + 1, pl.ds(start, LANES)] = sums[model]
        diagonal[:, pl.ds(start, LANES)] = functools.reduce(jnp.add, sums)
        return carry

    lax.fori_loop(0, width // LANES, norm_rows, 0)

    over_features(weights, tokens, values)
    picked = []
    for tile, owner in enumerate(owners):
        lanes = slice(tile * LANES, (tile + 1) * LANES)
        if owner < 0:
            picked.append(jnp.where(owner_ref[:, lanes] > 0, values[columns:2 * columns, lanes], values[:columns, lanes]))
        else:
            picked.append(values[owner * columns:(owner + 1) * columns, lanes])
    outputs[...] = jnp.concatenate(picked, axis=1).astype(jnp.bfloat16)

    norm_now = jnp.zeros((columns, 1), jnp.float32)
    for start in range(0, width, CHUNK):
        part = slice(start, start + CHUNK)
        weighted = jnp.zeros((columns, CHUNK), jnp.float32)
        for model in range(models):
            rows = weights[model * columns:(model + 1) * columns, part].astype(jnp.float32)
            weighted = weighted + squared[model:model + 1, part] * rows
        right = MIXING * over_tokens(outputs, tokens, part) + (1.0 - MIXING) * weighted
        residual[:, part] = right
        direction[:, part] = jnp.zeros_like(right)
        merged[:, part] = jnp.zeros_like(right)
        norm_now = norm_now + jnp.sum(right * right, axis=1, keepdims=True)

    def step_of(scale, norm_now):
        weighted = jnp.zeros((columns, 1), jnp.float32)
        for start in range(0, width, CHUNK):
            part = slice(start, start + CHUNK)
            value = residual[:, part] + scale * direction[:, part]
            direction[:, part] = value
            terms[:, part] = two_terms(value)
            weighted = weighted + jnp.sum(diagonal[:, part] * value * value, axis=1, keepdims=True)
        both = values.at[:2 * columns]
        over_features(terms, tokens, both)
        both = both[:columns] + both[columns:]
        seen[...] = two_terms(both)
        curvature = MIXING * jnp.sum(both * both, axis=1, keepdims=True) + (1.0 - MIXING) * weighted
        return norm_now / curvature

    def iterate(_, carry):
        scale, norm_now = carry
        step_size = step_of(scale, norm_now)
        norm_next = jnp.zeros((columns, 1), jnp.float32)
        for start in range(0, width, CHUNK):
            part = slice(start, start + CHUNK)
            both = over_tokens(seen, tokens, part)
            along = direction[:, part]
            image = MIXING * (both[:columns] + both[columns:]) + (1.0 - MIXING) * diagonal[:, part] * along
            merged[:, part] = merged[:, part] + step_size * along
            value = residual[:, part] - step_size * image
            residual[:, part] = value
            norm_next = norm_next + jnp.sum(value * value, axis=1, keepdims=True)
        return norm_next / norm_now, norm_next

    scale, norm_now = lax.fori_loop(0, ITERS - 1, iterate, (jnp.zeros((columns, 1), jnp.float32), norm_now))
    step_size = step_of(scale, norm_now)
    merged[...] = merged[...] + step_size * direction[...]
    for number, out_ref in enumerate(out_refs):
        sub_rows = out_ref.shape[1]
        if len(out_refs) > 1:
            start = pl.multiple_of(table_ref[TABLE_OUT + number] * sub_rows, LANES)
            out_ref[...] = merged[:, pl.ds(start, sub_rows)].astype(out_ref.dtype)
        else:
            out_ref[...] = merged[...].astype(out_ref.dtype)


def place_kernel(table_ref, *refs):
    pieces, out_ref, sem = refs[:-2], refs[-2], refs[-1]
    started = []
    for number, piece in enumerate(pieces):
        copy = pltpu.make_async_copy(piece, out_ref.at[table_ref[number]], sem.at[0])
        copy.start()
        started.append(copy)
    for copy in started:
        copy.wait()


def pick_kernel(table_ref, whole_ref, *refs):
    sem = refs[-1]
    started = []
    for number, out_ref in enumerate(refs[:-1]):
        copy = pltpu.make_async_copy(whole_ref.at[table_ref[number]], out_ref, sem.at[0])
        copy.start()
        started.append(copy)
    for copy in started:
        copy.wait()


def body(hidden, gains, weights, lengths):
    rows = lax.axis_size("row")
    cols = lax.axis_size("col")
    toks = lax.axis_size("tok")
    row, col, tok = lax.axis_index("row"), lax.axis_index("col"), lax.axis_index("tok")
    slots, block = hidden.shape
    width = block * rows * cols
    models = toks * gains.shape[0]
    row_width, col_width = weights.shape[1:]
    columns = col_width // (rows * toks)
    sub_rows = row_width // toks
    features = hidden.T
    positions = jnp.arange(slots, dtype=jnp.int32)
    paired = toks == 2 and rows == 4
    any_space = pl.BlockSpec(memory_space=pl.ANY)
    scalars = pl.BlockSpec(memory_space=pltpu.SMEM)
    in_vmem = pl.BlockSpec(memory_space=pltpu.VMEM)
    dma = [pltpu.SemaphoreType.DMA((1,))]

    def swap(value, flip):
        pairs = [
            (t * rows + r, (t ^ flip % 2) * rows + (r ^ flip // 2)) for t in range(toks) for r in range(rows)
        ]
        return lax.ppermute(value, ("tok", "row"), pairs)

    sent = weights[0].T.reshape(rows * toks, columns, row_width)
    if paired:
        near_first = (0, 2, 4, 6, 3, 5, 7, 1)
        partners = jnp.stack([(row * toks + tok) ^ flip for flip in near_first]).astype(jnp.int32)
        picked = pl.pallas_call(
            pick_kernel,
            out_shape=[jax.ShapeDtypeStruct((columns, row_width), jnp.bfloat16)] * len(near_first),
            in_specs=[scalars, any_space],
            out_specs=[any_space] * len(near_first),
            scratch_shapes=dma,
        )(partners, sent)
        weight_pieces = [picked[0]] + [swap(x, flip) for x, flip in zip(picked[1:], near_first[1:])]

        half, quarter = slots // 2, slots // 4
        held = half + quarter
        lower, upper = features[:, half:held], features[:, held:]
        given = swap(upper, 1)
        mirror = jnp.eye(quarter, dtype=jnp.bfloat16)[::-1]
        turned = jnp.dot(jnp.where(tok == 0, given, lower), mirror, preferred_element_type=jnp.float32)
        place = jnp.arange(half, dtype=jnp.int32)
        of_second = place >= lengths[0] - half
        ours = lax.dynamic_slice(of_second, (tok * quarter,), (quarter,))
        mixed = jnp.where(ours[None, :], turned.astype(jnp.bfloat16), jnp.where(tok == 0, lower, given))
        piece = jnp.concatenate([features[:, :half], mixed], axis=1)
        line = [piece]
        for shift in range(1, cols):
            line.append(lax.ppermute(piece, "col", [(i, (i + shift) % cols) for i in range(cols)]))
        table = list(partners) + [tok, 1 - tok, row] + [row ^ 1, row ^ 2, row ^ 3]
        origin = {}
        mine, homes = [], []
        for back in range(cols):
            by_near, by_far = swap(line[back], 2), swap(line[back], 4)
            across = swap(by_far, 2) if back % 2 == 0 else swap(by_near, 4)
            for flip, value in enumerate((line[back], by_near, by_far, across)):
                mine.append(value)
                homes.append(len(table))
                table.append((row ^ flip) * cols + (col - back + cols) % cols)
        theirs = [swap(value, 1) for value in mine]
        pieces = [value[None] for value in mine + theirs]
        base = len(partners)
        copies = [[(0, home, base, held)] for home in homes] + [[(0, home, base + 1, held)] for home in homes]
        places = []
        for flip in near_first:
            places.append((base + 2 + flip // 2, base + flip % 2))
        owners = (0, 0, -1, 1, 1, -1)
        late = jnp.where(of_second, slots - 1 - place < lengths[1], half + place < lengths[0])
        live = jnp.concatenate([
            positions[:half] < lengths[0], late[:quarter], positions[:half] < lengths[1], late[quarter:]
        ])
        lane_owner = jnp.concatenate([
            jnp.zeros(half, bool), of_second[:quarter], jnp.ones(half, bool), of_second[quarter:]
        ])
    else:
        own_weights = lax.all_to_all(sent, ("row", "tok"), 0, 0, tiled=True)
        own_weights = own_weights.reshape(rows, models * columns, row_width)
        weight_pieces = [own_weights.transpose(1, 0, 2).reshape(models * columns, width)]
        places = [(0, 0)]
        piece, held = features, slots
        everything = lax.all_gather(features, ("row", "col"), axis=0, tiled=False)
        pieces = [lax.all_gather(everything, "tok", axis=0, tiled=True)]
        tiles = slots // LANES
        owners = tuple(m for m in range(models) for _ in range(tiles))
        table = list(range(max(models, rows * cols)))
        copies = [[
            (m * rows * cols + b, b, m, slots) for m in range(models) for b in range(rows * cols)
        ]]
        live = (positions[None, :] < lengths[:, None]).reshape(-1)
        lane_owner = jnp.zeros(models * slots, bool)
    slots_held = toks * held

    floats = piece.astype(jnp.float32)
    squares = jnp.sum(floats * floats, axis=0)
    spread = lax.dynamic_update_slice(
        jnp.zeros((rows * cols, block), jnp.float32), gains, (row * cols + col, 0)
    ).reshape(width)
    shared = lax.dynamic_update_slice(
        jnp.zeros((toks, held + width), jnp.float32), jnp.concatenate([squares, spread])[None], (tok, 0)
    )
    shared = lax.psum(shared, ("tok", "row", "col"))
    every_gain = shared[:, held:].T
    squares = shared[:, :held].reshape(1, slots_held)

    if paired:
        out_shape = [jax.ShapeDtypeStruct((columns, sub_rows), jnp.bfloat16)] * (rows * toks)
    else:
        out_shape = [jax.ShapeDtypeStruct((columns, width), jnp.bfloat16)]
    found = pl.pallas_call(
        functools.partial(solve_kernel, owners, models, block, copies, places),
        out_shape=out_shape,
        in_specs=[scalars] + [in_vmem] * 4 + [any_space] * (len(pieces) + len(weight_pieces)),
        out_specs=[in_vmem] * len(out_shape),
        scratch_shapes=[
            pltpu.VMEM((width, slots_held), jnp.bfloat16),
            pltpu.VMEM((models * columns, width), jnp.bfloat16),
            pltpu.VMEM((models, width), jnp.float32),
            pltpu.VMEM((1, width), jnp.float32),
            pltpu.VMEM((columns, width), jnp.float32),
            pltpu.VMEM((columns, width), jnp.float32),
            pltpu.VMEM((columns, width), jnp.float32),
            pltpu.VMEM((2 * columns, width), jnp.bfloat16),
            pltpu.VMEM((max(models, 2) * columns, slots_held), jnp.float32),
            pltpu.VMEM((columns, slots_held), jnp.bfloat16),
            pltpu.VMEM((2 * columns, slots_held), jnp.bfloat16),
            pltpu.SemaphoreType.DMA((2,)),
        ],
        compiler_params=pltpu.CompilerParams(vmem_limit_bytes=width * slots_held * 2 + (18 << 20)),
    )(
        jnp.stack([jnp.asarray(x, jnp.int32) for x in table]),
        live.astype(jnp.float32)[None, :],
        lane_owner.astype(jnp.float32)[None, :],
        squares,
        every_gain,
        *pieces,
        *weight_pieces,
    )
    if paired:
        arrived = [found[0]] + [swap(x, flip) for x, flip in zip(found[1:], near_first[1:])]
        back = pl.pallas_call(
            place_kernel,
            out_shape=jax.ShapeDtypeStruct((rows * toks, columns, sub_rows), jnp.bfloat16),
            in_specs=[scalars] + [any_space] * len(arrived),
            out_specs=any_space,
            scratch_shapes=dma,
        )(partners, *arrived)
    else:
        found = found[0].reshape(columns, rows * toks, sub_rows).transpose(1, 0, 2)
        back = lax.all_to_all(found, ("row", "tok"), 0, 0, tiled=True)
    return back.reshape(col_width, sub_rows).T.astype(jnp.float32)


def solution(mesh):
    return jax.shard_map(
        body,
        mesh=mesh,
        in_specs=(P("tok", ("row", "col")), P("tok", ("row", "col")), P("tok", "row", "col"), P()),
        out_specs=P(("row", "tok"), "col"),
        check_vma=False,
    )
```

time: 985 us -> 308 us (0.31)
  waiting for transfers between devices: 593 us -> 30.5 us
  blocking collectives: 198 us -> 79.9 us
  matrix products: 113 us -> 0.16 us
  Pallas kernels: 0 us -> 94.6 us
  starting transfers between devices: 0.67 us -> 36.4 us
  other arithmetic: 29.4 us -> 2.55 us
  local copies, waits for them, and re-layouts: 36.3 us -> 61.2 us
  between operations: 13.4 us -> 1.12 us
    all_gather x7 -> x0, waiting for transfers between devices: 548 us -> none  [the longest x4 252 us: body(): gathered = lax.all_gather(direction, 'row', axis=0, tiled=True)]
    psum x9 -> x1, blocking collectives: 198 us -> 79.9 us  [body(): shared = lax.psum(shared, ('tok', 'row', 'col'))]
    dot_general x7 -> x1, matrix products: 113 us -> 0.16 us  [body(): jnp.dot(jnp.where(tok == 0, given, lower), mirror, preferred_element_type...]
    pallas_call x0 -> x3, Pallas kernels: none -> 94.6 us  [the longest x1 41.5 us: body(): pl.pallas_call(pick_kernel, out_shape=[jax.ShapeDtypeStruct((columns, row...]
    reduce_scatter x6 -> x0, waiting for transfers between devices: 43.8 us -> none  [the longest x4 30.9 us: body(): lax.psum_scatter(operate_product, 'tok', scatter_dimension=0, tiled=True)]
    ppermute x0 -> x46, starting transfers between devices: none -> 36.4 us  [the longest x43 27.9 us: swap(): return lax.ppermute(value, ('tok', 'row'), pairs)]
    unnamed x13 -> x117, local copies, waits for them, and re-layouts: 2.11 us -> 37.9 us
    ppermute x0 -> x46, waiting for transfers between devices: none -> 30.5 us  [the longest x43 26.3 us: swap(): return lax.ppermute(value, ('tok', 'row'), pairs)]
  transfers between devices with their start and end apart: 13 -> 46, of which waited for: 11 -> 18; matrix products, arithmetic and copies ran while one was open for 5% -> 7% of each run, Pallas kernels for 0% -> 0%
where the time goes in v1:
time: 308 us; the launch traced here: 306 us
  Pallas kernels  94.6 us (31%)
  blocking collectives  79.9 us (26%)
  local copies, waits for them, and re-layouts  61.2 us (20%)
  starting transfers between devices  36.4 us (12%)
  waiting for transfers between devices  30.5 us (10%)
    psum x1, blocking collectives, body(): shared = lax.psum(shared, ('tok', 'row', 'col'))  79.9 us
    pallas_call x1, Pallas kernels, body(): pl.pallas_call(pick_kernel, out_shape=[jax.ShapeDtypeStruct((columns, row...  41.5 us
    unnamed x117, local copies, waits for them, and re-layouts  37.9 us
    pallas_call x1, Pallas kernels, body(): pl.pallas_call(functools.partial(solve_kernel, owners, models, block, cop...  31.5 us
    ppermute x43, starting transfers between devices, swap(): return lax.ppermute(value, ('tok', 'row'), pairs)  27.9 us
    ppermute x43, waiting for transfers between devices, swap(): return lax.ppermute(value, ('tok', 'row'), pairs)  26.3 us
    pallas_call x1, Pallas kernels, body(): pl.pallas_call(place_kernel, out_shape=jax.ShapeDtypeStruct((rows * toks,...  21.6 us
    ppermute x3, starting transfers between devices, body(): lax.ppermute(piece, 'col', [(i, (i + shift) % cols) for i in range(cols)])  8.47 us
  transfers between devices with their start and end apart: 46, of which 18 were waited for; matrix products, arithmetic and copies ran while one was open for 7% of the time, Pallas kernels for 0%

profile of v1, /device:TPU:0, one launch (start us, length us, event | category | flops | bytes accessed | tf_op | source)
XLA Modules:
  0.0 306.4 jit_solution(11333287185900535153)
XLA Ops:
  0.0 2.5 copy.9
  3.2 41.5 %shard_map.46 = (bf16[64,1280]{1,0:T(8,128)(2,1)}, bf16[64,1280]{1,0:T(8,128)(2,1)}, bf16[64,1280]{1,0:T(8,128)(2,1)}, bf16[64,1280]{1,0:T(8,128)(2,1)}, bf16[64...) custom-call(s32[8]{0:T(128)} %stack.104.table_ref, ...), custom_call_target="tpu_custom_call" | custom-call | tf_op jit(solution)/shard_map/pallas_call | solution.py:233
  44.6 3.0 collective-permute-start.32
  50.9 2.1 collective-permute-start.4
  58.4 1.6 collective-permute-start.38
  60.7 2.6 collective-permute-start.8
  65.0 3.8 %collective-permute-start.12 = (bf16[320,384]{1,0:T(8,128)(2,1)S(1)}, bf16[320,384]{1,0:T(8,128)(2,1)S(1)}, u32[]{:S(2)}, u32[]{:S(2)}) collective-permute-start(bf16[320,384]{1,0:T(8,128)(2,1)S(1)} %get-tuple-element.37), channel_id=1, source_target_pairs={{0,3},{1,0},{2,1},{3,2},{4,7},{5,4},{6,5},{7,6},{8,11},{9,8},{10,9... | collective-permute-start | bytes 737288 | tf_op jit(solution)/shard_map/ppermute | solution.py:255
  72.3 3.4 %collective-permute-done.8 = bf16[320,384]{1,0:T(8,128)(2,1)S(1)} collective-permute-done((bf16[320,384]{1,0:T(8,128)(2,1)S(1)}, bf16[320,384]{1,0:T(8,128)(2,1)S(1)}, u32[]{:S(2)}, u32[]{:S(2)}) %collective-permute-start.8) | collective-permute-done | bytes 245792 | tf_op jit(solution)/shard_map/ppermute | solution.py:255
  78.0 1.5 collective-permute-start.10
  82.8 2.8 collective-permute-done.5
  87.2 3.6 %collective-permute-done.13 = bf16[320,384]{1,0:T(8,128)(2,1)S(1)} collective-permute-done((bf16[320,384]{1,0:T(8,128)(2,1)S(1)}, bf16[320,384]{1,0:T(8,128)(2,1)S(1)}, u32[]{:S(2)}, u32[]{:S(2)}) %collective-permute-start.13) | collective-permute-done | bytes 245792 | tf_op jit(solution)/shard_map/ppermute | solution.py:227
  92.0 4.0 %collective-permute-done.9 = bf16[320,384]{1,0:T(8,128)(2,1)S(1)} collective-permute-done((bf16[320,384]{1,0:T(8,128)(2,1)S(1)}, bf16[320,384]{1,0:T(8,128)(2,1)S(1)}, u32[]{:S(2)}, u32[]{:S(2)}) %collective-permute-start.9) | collective-permute-done | bytes 245792 | tf_op jit(solution)/shard_map/ppermute | solution.py:227
  107.0 2.6 collective-permute-done.7
  111.5 2.9 collective-permute-done.15
  115.2 3.4 %broadcast_in_dim.160 = f32[1,5504]{0,1:T(8,128)} reshape(f32[5504]{0:T(1024)S(1)} %pad_maximum_fusion.1) | data formatting | bytes 44032 | tf_op jit(solution)/shard_map/broadcast_in_dim | solution.py:305
  118.7 1.8 broadcast_in_dim.124
  120.4 8.0 %dynamic_update_slice.7 = f32[2,5504]{0,1:T(8,128)} dynamic-update-slice(f32[2,5504]{0,1:T(8,128)} %broadcast_in_dim.124, f32[1,5504]{0,1:T(8,128)} %broadcast_in_dim.160, s32[]{:T(128)S(6)} %select_n.83, s32[]{:T(128)} %constant.90.clone.1) | dynamic-update-slice | bytes 44036 | tf_op jit(solution)/shard_map/dynamic_update_slice | solution.py:304
  128.4 79.9 %psum.7 = f32[2,5504]{0,1:T(8,128)} all-reduce(f32[2,5504]{0,1:T(8,128)} %dynamic_update_slice.7), channel_id=1, replica_groups=mesh['tok'=2,'row'=4,'col'=4] {'tok','row','col'}, use_global_device_ids=true, to_apply=%region_1.2 | all-reduce | flops 11008 | bytes 88064 | tf_op jit(solution)/shard_map/psum | solution.py:307
  212.2 1.9 slice_bitcast_fusion.gains_ref
  214.1 1.6 slice.57
  238.3 31.5 %shard_map.47 = (bf16[64,640]{1,0:T(8,128)(2,1)S(1)}, bf16[64,640]{1,0:T(8,128)(2,1)S(1)}, bf16[64,640]{1,0:T(8,128)(2,1)S(1)}, bf16[64,640]{1,0:T(8,128)(2,1)S(...) custom-call(s32[30]{0:T(128)S(1)} %stack.127.table_ref, ...), custom_call_target="tpu_custom_call" | custom-call | tf_op jit(solution)/shard_map/pallas_call | solution.py:315
  276.6 1.7 collective-permute-done.40.refs_2_
  279.5 2.0 collective-permute-done.44.refs_6_
  282.1 21.6 %shard_map.48 = bf16[8,64,640]{2,1,0:T(8,128)(2,1)} custom-call(s32[8]{0:T(128)} %stack.104.table_ref, bf16[64,640]{1,0:T(8,128)(2,1)} %copy-done.47, bf16[64,640]{1,0:T(8,128)(2,1)} %copy-done.49, bf16[64,640]{1,0:T(8,128)(2,1)} %copy-done.50, bf16[64,640]{1,0:T(8,128)(2,1)} %copy-done.51, bf16[64,640]{1,0:T(8,128)(2,1)} %copy-done.52, ...), custom_call_target="tpu_custom_call" | custom-call | tf_op jit(solution)/shard_map/pallas_call | solution.py:346
  (225 shorter events, 73.9 us)
Async XLA Ops:
  44.6 9.6 %collective-permute-start.32 = (bf16[64,1280]{1,0:T(8,128)(2,1)}, bf16[64,1280]{1,0:T(8,128)(2,1)S(1)}, u32[]{:S(2)}, u32[]{:S(2)}) collective-permute-start(bf16[64,1280]{1,0:T(8,128)(2,1)} %get-tuple-element.22), channel_id=1, source_target_pairs={{0,4},{4,0},{8,12},{12,8},{16,20},{20,16},{24,28},{28,24},{1,5},{5... | collective-permute-start | bytes 491528 | tf_op jit(solution)/shard_map/ppermute | solution.py:227
  47.7 9.4 %collective-permute-start.33 = (bf16[64,1280]{1,0:T(8,128)(2,1)}, bf16[64,1280]{1,0:T(8,128)(2,1)S(1)}, u32[]{:S(2)}, u32[]{:S(2)}) collective-permute-start(bf16[64,1280]{1,0:T(8,128)(2,1)} %get-tuple-element.23), channel_id=1, source_target_pairs={{0,8},{4,12},{8,0},{12,4},{16,24},{20,28},{24,16},{28,20},{1,9},{5... | collective-permute-start | bytes 491528 | tf_op jit(solution)/shard_map/ppermute | solution.py:227
  50.9 21.4 %collective-permute-start.4 = (bf16[320,384]{1,0:T(8,128)(2,1)S(1)}, bf16[320,384]{1,0:T(8,128)(2,1)S(1)}, u32[]{:S(2)}, u32[]{:S(2)}) collective-permute-start(bf16[320,384]{1,0:T(8,128)(2,1)S(1)} %get-tuple-element.37), channel_id=1, source_target_pairs={{0,1},{1,2},{2,3},{3,0},{4,5},{5,6},{6,7},{7,4},{8,9},{9,10},{10,1... | collective-permute-start | bytes 737288 | tf_op jit(solution)/shard_map/ppermute | solution.py:255
  55.0 9.4 %collective-permute-start.36 = (bf16[64,1280]{1,0:T(8,128)(2,1)}, bf16[64,1280]{1,0:T(8,128)(2,1)S(1)}, u32[]{:S(2)}, u32[]{:S(2)}) collective-permute-start(bf16[64,1280]{1,0:T(8,128)(2,1)} %get-tuple-element.26), channel_id=1, source_target_pairs={{0,24},{4,28},{8,16},{12,20},{16,8},{20,12},{24,0},{28,4},{1,25},{... | collective-permute-start | bytes 491528 | tf_op jit(solution)/shard_map/ppermute | solution.py:227
  57.7 11.1 %collective-permute-start.37 = (bf16[64,1280]{1,0:T(8,128)(2,1)}, bf16[64,1280]{1,0:T(8,128)(2,1)S(1)}, u32[]{:S(2)}, u32[]{:S(2)}) collective-permute-start(bf16[64,1280]{1,0:T(8,128)(2,1)} %get-tuple-element.27), channel_id=1, source_target_pairs={{0,28},{4,24},{8,20},{12,16},{16,12},{20,8},{24,4},{28,0},{1,29},{... | collective-permute-start | bytes 491528 | tf_op jit(solution)/shard_map/ppermute | solution.py:227
  58.4 12.3 %collective-permute-start.38 = (bf16[64,1280]{1,0:T(8,128)(2,1)}, bf16[64,1280]{1,0:T(8,128)(2,1)S(1)}, u32[]{:S(2)}, u32[]{:S(2)}) collective-permute-start(bf16[64,1280]{1,0:T(8,128)(2,1)} %get-tuple-element.28), channel_id=1, source_target_pairs={{0,16},{4,20},{8,24},{12,28},{16,0},{20,4},{24,8},{28,12},{1,17},{... | collective-permute-start | bytes 491528 | tf_op jit(solution)/shard_map/ppermute | solution.py:227
  60.7 15.0 %collective-permute-start.8 = (bf16[320,384]{1,0:T(8,128)(2,1)S(1)}, bf16[320,384]{1,0:T(8,128)(2,1)S(1)}, u32[]{:S(2)}, u32[]{:S(2)}) collective-permute-start(bf16[320,384]{1,0:T(8,128)(2,1)S(1)} %get-tuple-element.37), channel_id=1, source_target_pairs={{0,2},{1,3},{2,0},{3,1},{4,6},{5,7},{6,4},{7,5},{8,10},{9,11},{10,... | collective-permute-start | bytes 737288 | tf_op jit(solution)/shard_map/ppermute | solution.py:255
  65.0 13.0 %collective-permute-start.12 = (bf16[320,384]{1,0:T(8,128)(2,1)S(1)}, bf16[320,384]{1,0:T(8,128)(2,1)S(1)}, u32[]{:S(2)}, u32[]{:S(2)}) collective-permute-start(bf16[320,384]{1,0:T(8,128)(2,1)S(1)} %get-tuple-element.37), channel_id=1, source_target_pairs={{0,3},{1,0},{2,1},{3,2},{4,7},{5,4},{6,5},{7,6},{8,11},{9,8},{10,9... | collective-permute-start | bytes 737288 | tf_op jit(solution)/shard_map/ppermute | solution.py:255
  69.5 10.1 %collective-permute-start.2 = (bf16[320,384]{1,0:T(8,128)(2,1)S(1)}, bf16[320,384]{1,0:T(8,128)(2,1)S(1)}, u32[]{:S(2)}, u32[]{:S(2)}) collective-permute-start(bf16[320,384]{1,0:T(8,128)(2,1)S(1)} %get-tuple-element.37), channel_id=1, source_target_pairs={{0,8},{4,12},{8,0},{12,4},{16,24},{20,28},{24,16},{28,20},{1,9},{5... | collective-permute-start | bytes 737288 | tf_op jit(solution)/shard_map/ppermute | solution.py:227
  71.4 8.9 %collective-permute-start.1 = (bf16[320,384]{1,0:T(8,128)(2,1)S(1)}, bf16[320,384]{1,0:T(8,128)(2,1)S(1)}, u32[]{:S(2)}, u32[]{:S(2)}) collective-permute-start(bf16[320,384]{1,0:T(8,128)(2,1)S(1)} %get-tuple-element.37), channel_id=1, source_target_pairs={{0,4},{4,0},{8,12},{12,8},{16,20},{20,16},{24,28},{28,24},{1,5},{5... | collective-permute-start | bytes 737288 | tf_op jit(solution)/shard_map/ppermute | solution.py:227
  75.7 9.9 %collective-permute-start.5 = (bf16[320,384]{1,0:T(8,128)(2,1)S(1)}, bf16[320,384]{1,0:T(8,128)(2,1)S(1)}, u32[]{:S(2)}, u32[]{:S(2)}) collective-permute-start(bf16[320,384]{1,0:T(8,128)(2,1)S(1)} %collective-permute-done.4), channel_id=1, source_target_pairs={{0,4},{4,0},{8,12},{12,8},{16,20},{20,16},{24,28},{28,24},{1,5},{5... | collective-permute-start | bytes 737288 | tf_op jit(solution)/shard_map/ppermute | solution.py:227
  79.5 11.3 %collective-permute-start.13 = (bf16[320,384]{1,0:T(8,128)(2,1)S(1)}, bf16[320,384]{1,0:T(8,128)(2,1)S(1)}, u32[]{:S(2)}, u32[]{:S(2)}) collective-permute-start(bf16[320,384]{1,0:T(8,128)(2,1)S(1)} %collective-permute-done.12), channel_id=1, source_target_pairs={{0,4},{4,0},{8,12},{12,8},{16,20},{20,16},{24,28},{28,24},{1,5},{5... | collective-permute-start | bytes 737288 | tf_op jit(solution)/shard_map/ppermute | solution.py:227
  80.3 11.8 %collective-permute-start.6 = (bf16[320,384]{1,0:T(8,128)(2,1)S(1)}, bf16[320,384]{1,0:T(8,128)(2,1)S(1)}, u32[]{:S(2)}, u32[]{:S(2)}) collective-permute-start(bf16[320,384]{1,0:T(8,128)(2,1)S(1)} %collective-permute-done.4), channel_id=1, source_target_pairs={{0,8},{4,12},{8,0},{12,4},{16,24},{20,28},{24,16},{28,20},{1,9},{5... | collective-permute-start | bytes 737288 | tf_op jit(solution)/shard_map/ppermute | solution.py:227
  81.2 14.8 %collective-permute-start.9 = (bf16[320,384]{1,0:T(8,128)(2,1)S(1)}, bf16[320,384]{1,0:T(8,128)(2,1)S(1)}, u32[]{:S(2)}, u32[]{:S(2)}) collective-permute-start(bf16[320,384]{1,0:T(8,128)(2,1)S(1)} %collective-permute-done.8), channel_id=1, source_target_pairs={{0,4},{4,0},{8,12},{12,8},{16,20},{20,16},{24,28},{28,24},{1,5},{5... | collective-permute-start | bytes 737288 | tf_op jit(solution)/shard_map/ppermute | solution.py:227
  85.6 12.5 %collective-permute-start.14 = (bf16[320,384]{1,0:T(8,128)(2,1)S(1)}, bf16[320,384]{1,0:T(8,128)(2,1)}, u32[]{:S(2)}, u32[]{:S(2)}) collective-permute-start(bf16[320,384]{1,0:T(8,128)(2,1)S(1)} %collective-permute-done.12), channel_id=1, source_target_pairs={{0,8},{4,12},{8,0},{12,4},{16,24},{20,28},{24,16},{28,20},{1,9},{5... | collective-permute-start | bytes 737288 | tf_op jit(solution)/shard_map/ppermute | solution.py:227
  86.8 13.2 %collective-permute-start.3 = (bf16[320,384]{1,0:T(8,128)(2,1)S(1)}, bf16[320,384]{1,0:T(8,128)(2,1)}, u32[]{:S(2)}, u32[]{:S(2)}) collective-permute-start(bf16[320,384]{1,0:T(8,128)(2,1)S(1)} %collective-permute-done.2), channel_id=1, source_target_pairs={{0,4},{4,0},{8,12},{12,8},{16,20},{20,16},{24,28},{28,24},{1,5},{5... | collective-permute-start | bytes 737288 | tf_op jit(solution)/shard_map/ppermute | solution.py:227
  90.8 9.9 %collective-permute-start.20 = (bf16[320,384]{1,0:T(8,128)(2,1)S(1)}, bf16[320,384]{1,0:T(8,128)(2,1)S(1)}, u32[]{:S(2)}, u32[]{:S(2)}) collective-permute-start(bf16[320,384]{1,0:T(8,128)(2,1)S(1)} %collective-permute-done.4), channel_id=1, source_target_pairs={{0,16},{4,20},{8,24},{12,28},{16,0},{20,4},{24,8},{28,12},{1,17},{... | collective-permute-start | bytes 737288 | tf_op jit(solution)/shard_map/ppermute | solution.py:227
  92.0 9.4 %collective-permute-start.24 = (bf16[320,384]{1,0:T(8,128)(2,1)S(1)}, bf16[320,384]{1,0:T(8,128)(2,1)S(1)}, u32[]{:S(2)}, u32[]{:S(2)}) collective-permute-start(bf16[320,384]{1,0:T(8,128)(2,1)S(1)} %collective-permute-done.8), channel_id=1, source_target_pairs={{0,16},{4,20},{8,24},{12,28},{16,0},{20,4},{24,8},{28,12},{1,17},{... | collective-permute-start | bytes 737288 | tf_op jit(solution)/shard_map/ppermute | solution.py:227
  104.3 10.1 %collective-permute-start.15 = (bf16[320,384]{1,0:T(8,128)(2,1)S(1)}, bf16[320,384]{1,0:T(8,128)(2,1)}, u32[]{:S(2)}, u32[]{:S(2)}) collective-permute-start(bf16[320,384]{1,0:T(8,128)(2,1)S(1)} %collective-permute-done.13), channel_id=1, source_target_pairs={{0,8},{4,12},{8,0},{12,4},{16,24},{20,28},{24,16},{28,20},{1,9},{5... | collective-permute-start | bytes 737288 | tf_op jit(solution)/shard_map/ppermute | solution.py:227
  105.0 103.3 %collective-permute-start.21 = (bf16[320,384]{1,0:T(8,128)(2,1)S(1)}, bf16[320,384]{1,0:T(8,128)(2,1)S(1)}, u32[]{:S(2)}, u32[]{:S(2)}) collective-permute-start(bf16[320,384]{1,0:T(8,128)(2,1)S(1)} %collective-permute-done.5), channel_id=1, source_target_pairs={{0,16},{4,20},{8,24},{12,28},{16,0},{20,4},{24,8},{28,12},{1,17},{... | collective-permute-start | bytes 737288 | tf_op jit(solution)/shard_map/ppermute | solution.py:227
  105.8 103.3 %collective-permute-start.26 = (bf16[320,384]{1,0:T(8,128)(2,1)S(1)}, bf16[320,384]{1,0:T(8,128)(2,1)S(1)}, u32[]{:S(2)}, u32[]{:S(2)}) collective-permute-start(bf16[320,384]{1,0:T(8,128)(2,1)S(1)} %collective-permute-done.10), channel_id=1, source_target_pairs={{0,16},{4,20},{8,24},{12,28},{16,0},{20,4},{24,8},{28,12},{1,17},{... | collective-permute-start | bytes 737288 | tf_op jit(solution)/shard_map/ppermute | solution.py:227
  109.6 100.7 %collective-permute-start.29 = (bf16[320,384]{1,0:T(8,128)(2,1)S(1)}, bf16[320,384]{1,0:T(8,128)(2,1)S(1)}, u32[]{:S(2)}, u32[]{:S(2)}) collective-permute-start(bf16[320,384]{1,0:T(8,128)(2,1)S(1)} %collective-permute-done.13), channel_id=1, source_target_pairs={{0,16},{4,20},{8,24},{12,28},{16,0},{20,4},{24,8},{28,12},{1,17},{... | collective-permute-start | bytes 737288 | tf_op jit(solution)/shard_map/ppermute | solution.py:227
  110.3 100.6 %collective-permute-start.22 = (bf16[320,384]{1,0:T(8,128)(2,1)S(1)}, bf16[320,384]{1,0:T(8,128)(2,1)S(1)}, u32[]{:S(2)}, u32[]{:S(2)}) collective-permute-start(bf16[320,384]{1,0:T(8,128)(2,1)S(1)} %collective-permute-done.6), channel_id=1, source_target_pairs={{0,16},{4,20},{8,24},{12,28},{16,0},{20,4},{24,8},{28,12},{1,17},{... | collective-permute-start | bytes 737288 | tf_op jit(solution)/shard_map/ppermute | solution.py:227
  114.4 97.7 %collective-permute-start.25 = (bf16[320,384]{1,0:T(8,128)(2,1)S(1)}, bf16[320,384]{1,0:T(8,128)(2,1)}, u32[]{:S(2)}, u32[]{:S(2)}) collective-permute-start(bf16[320,384]{1,0:T(8,128)(2,1)S(1)} %collective-permute-done.9), channel_id=1, source_target_pairs={{0,16},{4,20},{8,24},{12,28},{16,0},{20,4},{24,8},{28,12},{1,17},{... | collective-permute-start | bytes 737288 | tf_op jit(solution)/shard_map/ppermute | solution.py:227
  (80 other events, 424.9 us)

commit v2 on v1

v2 whole, which is shorter than its diff:
```python
import functools

import jax
import jax.numpy as jnp
from jax import lax
from jax.experimental import pallas as pl
from jax.experimental.pallas import tpu as pltpu
from jax.sharding import PartitionSpec as P

ITERS = 4

MIXING = 0.9
EPSILON = 1e-06

LANES = 128
CHUNK = 512
MOST_TOKENS = 1024
NEAR_FIRST = (0, 2, 4, 6, 3, 5, 7, 1)


def two_terms(value):
    high = value.astype(jnp.bfloat16).astype(jnp.float32)
    return jnp.concatenate([high, value - high], axis=0).astype(jnp.bfloat16)


def over_features(left, tokens, found):
    slots = tokens.shape[1]
    if slots <= MOST_TOKENS:
        found[...] = jnp.dot(left[...], tokens[...], preferred_element_type=jnp.float32)
        return

    def some(step, carry):
        lanes = pl.ds(pl.multiple_of(step * CHUNK, CHUNK), CHUNK)
        found[:, lanes] = jnp.dot(left[...], tokens[:, lanes], preferred_element_type=jnp.float32)
        return carry

    lax.fori_loop(0, slots // CHUNK, some, 0)


def over_tokens(left, tokens, part):
    slots = tokens.shape[1]
    product = functools.partial(
        lax.dot_general, dimension_numbers=(((1,), (1,)), ((), ())), preferred_element_type=jnp.float32
    )
    if slots <= MOST_TOKENS:
        return product(left[...], tokens[part, :])

    def some(step, total):
        lanes = pl.ds(pl.multiple_of(step * CHUNK, CHUNK), CHUNK)
        return total + product(left[:, lanes], tokens[part, lanes])

    return lax.fori_loop(0, slots // CHUNK, some, jnp.zeros((left.shape[0], CHUNK), jnp.float32))


def in_pair_order(lengths_ref, width):
    half, quarter = width // 3, width // 6
    lane = lax.broadcasted_iota(jnp.int32, (1, width), 1)
    part = jnp.where(lane >= width // 2, 1, 0)
    spot = lane - part * (width // 2)
    place = spot - half + part * quarter
    late = spot >= half
    second = jnp.where(late, jnp.where(place >= lengths_ref[0] - half, 1, 0), part)
    position = jnp.where(late, jnp.where(second == 1, 2 * half - 1 - place, half + place), spot)
    length = jnp.where(second == 1, lengths_ref[1], lengths_ref[0])
    return jnp.where(position < length, 1.0, 0.0), second.astype(jnp.float32)


def solve_kernel(owners, models, block, copies, places, lengths_ref, *refs):
    riding = len(copies) > 1
    if not riding:
        live_ref, squares_ref, gains_ref, refs = refs[0], refs[1], refs[2], refs[3:]
    pieces = refs[:len(copies)]
    weight_pieces = refs[len(copies):len(copies) + len(places)]
    out_refs = refs[len(copies) + len(places):-14]
    (tokens, weights, squared, diagonal, residual, direction, merged, terms, values, outputs, seen, extras, gains_held,
     sems) = refs[-14:]
    width, slots = tokens.shape
    columns = residual.shape[0]
    blocks = width // block
    started = []
    if riding:
        row, col, tok = lax.axis_index("row"), lax.axis_index("col"), lax.axis_index("tok")
        cols = lax.axis_size("col")
        row_devices = lax.axis_size("row")
    for piece, parts in zip(pieces, copies):
        for source, entry, part, lanes, first, held in parts:
            if riding:
                flip, back = entry
                entry = (row ^ flip) * cols + lax.rem(col - back + cols, cols)
                part = tok ^ part
            start = pl.multiple_of(entry * block + first, 16)
            lane = pl.multiple_of(part * lanes, LANES)
            copy = pltpu.make_async_copy(
                piece.at[source, pl.ds(0, held)],
                tokens.at[pl.ds(start, held), pl.ds(lane, lanes)],
                sems.at[0],
            )
            copy.start()
            started.append(copy)
            if piece.shape[1] > held:
                copy = pltpu.make_async_copy(
                    piece.at[source, pl.ds(held, 16)],
                    extras.at[part * blocks + entry],
                    sems.at[0],
                )
                copy.start()
                started.append(copy)
    for piece, place in zip(weight_pieces, places):
        moves = [(piece, weights)]
        if riding:
            row_width = piece.shape[1]
            lane = pl.multiple_of((row ^ place) * row_width, LANES)
            moves = [
                (
                    piece.at[pl.ds(part * columns, columns)],
                    weights.at[pl.ds(pl.multiple_of((tok ^ part) * columns, columns), columns), pl.ds(lane, row_width)],
                )
                for part in range(2)
            ]
        for source, target in moves:
            copy = pltpu.make_async_copy(source, target, sems.at[1])
            copy.start()
            started.append(copy)
    for copy in started:
        copy.wait()

    if riding:
        every = extras[...].astype(jnp.float32)
        sums = [jnp.sum(every[part * blocks:(part + 1) * blocks], axis=0) for part in range(models)]
        squares = jnp.concatenate([x[0:1] + x[1:2] + x[2:3] for x in sums], axis=1)
        turned = (every[:, 3] + every[:, 4] + every[:, 5]).T[:block]
        lane = lax.broadcasted_iota(jnp.int32, turned.shape, 1)
        side = lax.broadcasted_iota(jnp.int32, (block, LANES), 1)

        def hold_gains(step, carry):
            gain = [
                jnp.sum(jnp.where(lane == part * blocks + step, turned, 0.0), axis=1, keepdims=True)
                for part in range(models)
            ]
            gains_held[pl.ds(pl.multiple_of(step * block, block), block), :] = jnp.where(side == 0, gain[0], gain[1])
            return carry

        lax.fori_loop(0, blocks, hold_gains, 0)
        gains_ref = gains_held
        live, second = in_pair_order(lengths_ref, slots)
    else:
        squares, live = squares_ref[...], live_ref[...]
    inverse_rms = lax.rsqrt(squares / width + EPSILON) * live

    def norm_rows(step, carry):
        start = pl.multiple_of(step * LANES, LANES)
        gains = gains_ref[pl.ds(start, LANES), :]
        sums = [jnp.zeros((LANES, LANES), jnp.float32) for _ in range(models)]
        for tile, owner in enumerate(owners):
            lanes = slice(tile * LANES, (tile + 1) * LANES)
            value = tokens[pl.ds(start, LANES), lanes].astype(jnp.float32)
            if owner < 0:
                gain = jnp.where(second[:, lanes] > 0, gains[:, 1:2], gains[:, 0:1])
            else:
                gain = gains[:, owner:owner + 1]
            normed = (value * inverse_rms[:, lanes] * gain).astype(jnp.bfloat16)
            tokens[pl.ds(start, LANES), lanes] = normed
            value = normed.astype(jnp.float32)
            value = value * value
            if owner < 0:
                theirs = value * second[:, lanes]
                sums[0] = sums[0] + (value - theirs)
                sums[1] = sums[1] + theirs
            else:
                sums[owner] = sums[owner] + value
        sums = [jnp.sum(part.T, axis=0, keepdims=True) for part in sums]
        for model in range(models):
            squared[model:model + 1, pl.ds(start, LANES)] = sums[model]
        diagonal[:, pl.ds(start, LANES)] = functools.reduce(jnp.add, sums)
        return carry

    lax.fori_loop(0, width // LANES, norm_rows, 0, unroll=4 if riding else 1)

    over_features(weights, tokens, values)
    picked = []
    for tile, owner in enumerate(owners):
        lanes = slice(tile * LANES, (tile + 1) * LANES)
        if owner < 0:
            picked.append(jnp.where(second[:, lanes] > 0, values[columns:2 * columns, lanes], values[:columns, lanes]))
        else:
            picked.append(values[owner * columns:(owner + 1) * columns, lanes])
    outputs[...] = jnp.concatenate(picked, axis=1).astype(jnp.bfloat16)

    norm_now = jnp.zeros((columns, 1), jnp.float32)
    for start in range(0, width, CHUNK):
        part = slice(start, start + CHUNK)
        weighted = jnp.zeros((columns, CHUNK), jnp.float32)
        for model in range(models):
            rows = weights[model * columns:(model + 1) * columns, part].astype(jnp.float32)
            weighted = weighted + squared[model:model + 1, part] * rows
        right = MIXING * over_tokens(outputs, tokens, part) + (1.0 - MIXING) * weighted
        residual[:, part] = right
        direction[:, part] = jnp.zeros_like(right)
        merged[:, part] = jnp.zeros_like(right)
        norm_now = norm_now + jnp.sum(right * right, axis=1, keepdims=True)

    def step_of(scale, norm_now):
        weighted = jnp.zeros((columns, 1), jnp.float32)
        for start in range(0, width, CHUNK):
            part = slice(start, start + CHUNK)
            value = residual[:, part] + scale * direction[:, part]
            direction[:, part] = value
            terms[:, part] = two_terms(value)
            weighted = weighted + jnp.sum(diagonal[:, part] * value * value, axis=1, keepdims=True)
        both = values.at[:2 * columns]
        over_features(terms, tokens, both)
        both = both[:columns] + both[columns:]
        seen[...] = two_terms(both)
        curvature = MIXING * jnp.sum(both * both, axis=1, keepdims=True) + (1.0 - MIXING) * weighted
        return norm_now / curvature

    def iterate(_, carry):
        scale, norm_now = carry
        step_size = step_of(scale, norm_now)
        norm_next = jnp.zeros((columns, 1), jnp.float32)
        for start in range(0, width, CHUNK):
            part = slice(start, start + CHUNK)
            both = over_tokens(seen, tokens, part)
            along = direction[:, part]
            image = MIXING * (both[:columns] + both[columns:]) + (1.0 - MIXING) * diagonal[:, part] * along
            merged[:, part] = merged[:, part] + step_size * along
            value = residual[:, part] - step_size * image
            residual[:, part] = value
            norm_next = norm_next + jnp.sum(value * value, axis=1, keepdims=True)
        return norm_next / norm_now, norm_next

    scale, norm_now = lax.fori_loop(0, ITERS - 1, iterate, (jnp.zeros((columns, 1), jnp.float32), norm_now))
    step_size = step_of(scale, norm_now)
    merged[...] = merged[...] + step_size * direction[...]
    for number, out_ref in enumerate(out_refs):
        sub_rows = out_ref.shape[1]
        if len(out_refs) > 1:
            flip = NEAR_FIRST[number]
            sub_block = (row ^ flip // 2) * 2 + (tok ^ flip % 2)
            start = pl.multiple_of(sub_block * sub_rows, LANES)
            out_ref[...] = merged[:, pl.ds(start, sub_rows)].astype(out_ref.dtype)
        else:
            out_ref[...] = merged[...].astype(out_ref.dtype)


def three_terms(value):
    high = value.astype(jnp.bfloat16).astype(jnp.float32)
    rest = value - high
    middle = rest.astype(jnp.bfloat16).astype(jnp.float32)
    return [high, middle, rest - middle]


def piece_kernel(lengths_ref, features_ref, given_ref, gains_ref, upper_ref, lower_ref, extra):
    block, slots = features_ref.shape
    half, quarter = slots // 2, slots // 4
    tok = lax.axis_index("tok")
    first = tok == 0
    lower = features_ref[:, half:half + quarter].astype(jnp.float32)
    given = given_ref[...].astype(jnp.float32)
    row = lax.broadcasted_iota(jnp.int32, (quarter, quarter), 0)
    lane = lax.broadcasted_iota(jnp.int32, (quarter, quarter), 1)
    mirror = jnp.where(row + lane == quarter - 1, 1.0, 0.0).astype(jnp.bfloat16)
    turned = jnp.dot(
        jnp.where(first, given, lower).astype(jnp.bfloat16), mirror, preferred_element_type=jnp.float32
    )
    place = lax.broadcasted_iota(jnp.int32, (block, quarter), 1) + tok * quarter
    mixed = jnp.where(place >= lengths_ref[0] - half, turned, jnp.where(first, lower, given))
    kept = features_ref[:, :half]
    cut = lower_ref.shape[0]
    upper_ref[:cut, :half] = kept[:cut]
    upper_ref[:cut, half:] = mixed[:cut].astype(jnp.bfloat16)
    lower_ref[:, :half] = kept[cut:]
    lower_ref[:, half:] = mixed[cut:].astype(jnp.bfloat16)
    kept = kept.astype(jnp.float32)
    extra[...] = jnp.zeros_like(extra)
    for number, value in enumerate(three_terms(jnp.sum(kept * kept, axis=0, keepdims=True))):
        extra[number:number + 1, :half] = value
    for number, value in enumerate(three_terms(jnp.sum(mixed * mixed, axis=0, keepdims=True))):
        extra[number:number + 1, half:] = value
    for number, value in enumerate(three_terms(gains_ref[...])):
        extra[3 + number:4 + number, :block] = value
    upper_ref[cut:, :] = extra[...].astype(jnp.bfloat16)


def send_kernel(weights_ref, own_ref, other_ref, turned):
    row, tok = lax.axis_index("row"), lax.axis_index("tok")
    for start in range(0, weights_ref.shape[1], LANES):
        value = weights_ref[:, start:start + LANES].astype(jnp.float32)
        turned[start:start + LANES, :] = value.T.astype(jnp.bfloat16)
    rows, held, _ = own_ref.shape
    for flip in range(rows):
        for out_ref, core in ((own_ref, tok), (other_ref, 1 - tok)):
            start = pl.multiple_of(((row ^ flip) * 2 + core) * held, held)
            out_ref[flip] = turned[pl.ds(start, held), :]


def join_kernel(own_ref, given_ref, *refs):
    for flip, out_ref in enumerate(refs):
        held = own_ref.shape[1]
        out_ref[:held] = own_ref[flip]
        out_ref[held:] = given_ref[flip]


def gather_kernel(*refs):
    out_ref, ordered = refs[-2:]
    row, tok = lax.axis_index("row"), lax.axis_index("tok")
    for flip, piece in zip(NEAR_FIRST, refs[:-2]):
        held = piece.shape[0]
        start = pl.multiple_of(((row ^ flip // 2) * 2 + (tok ^ flip % 2)) * held, held)
        ordered[pl.ds(start, held), :] = piece[...].astype(jnp.float32)
    for start in range(0, out_ref.shape[1], LANES):
        out_ref[:, start:start + LANES] = ordered[start:start + LANES, :].T


def body(hidden, gains, weights, lengths):
    rows = lax.axis_size("row")
    cols = lax.axis_size("col")
    toks = lax.axis_size("tok")
    slots, block = hidden.shape
    width = block * rows * cols
    models = toks * gains.shape[0]
    row_width, col_width = weights.shape[1:]
    columns = col_width // (rows * toks)
    sub_rows = row_width // toks
    features = hidden.T
    paired = toks == 2 and rows == 4
    any_space = pl.BlockSpec(memory_space=pl.ANY)
    small = pltpu.CompilerParams(vmem_limit_bytes=10 << 20)
    scalars = pl.BlockSpec(memory_space=pltpu.SMEM)
    in_vmem = pl.BlockSpec(memory_space=pltpu.VMEM)

    def swap(value, flip):
        pairs = [
            (t * rows + r, (t ^ flip % 2) * rows + (r ^ flip // 2)) for t in range(toks) for r in range(rows)
        ]
        return lax.ppermute(value, ("tok", "row"), pairs)

    if paired:
        half, quarter = slots // 2, slots // 4
        held = half + quarter
        given = swap(features[:, held:], 1)
        own, other = pl.pallas_call(
            send_kernel,
            out_shape=[jax.ShapeDtypeStruct((rows, columns, row_width), jnp.bfloat16)] * 2,
            in_specs=[in_vmem],
            out_specs=[in_vmem] * 2,
            scratch_shapes=[pltpu.VMEM((col_width, row_width), jnp.bfloat16)],
            compiler_params=small,
        )(weights[0])
        joined = pl.pallas_call(
            join_kernel,
            out_shape=[jax.ShapeDtypeStruct((toks * columns, row_width), jnp.bfloat16)] * rows,
            in_specs=[in_vmem] * 2,
            out_specs=[in_vmem] * rows,
            compiler_params=small,
        )(own, swap(other, 1))
        weight_pieces = [swap(value, 2 * flip) if flip else value for flip, value in enumerate(joined)]
        places = list(range(rows))
        cut = block // 2
        upper, lower = pl.pallas_call(
            piece_kernel,
            out_shape=[
                jax.ShapeDtypeStruct((cut + 16, held), jnp.bfloat16), jax.ShapeDtypeStruct((cut, held), jnp.bfloat16)
            ],
            in_specs=[scalars, in_vmem, in_vmem, in_vmem],
            out_specs=[in_vmem] * 2,
            scratch_shapes=[pltpu.VMEM((16, held), jnp.float32)],
            compiler_params=small,
        )(lengths, features, given, gains)
        up = [(i, (i + 1) % cols) for i in range(cols)]
        lines = [[upper], [lower]]
        for _ in range(cols - 1):
            for line in lines:
                line.append(lax.ppermute(line[-1], "col", up))
        lines, weight_pieces = lax.optimization_barrier((lines, weight_pieces))
        pieces, copies = [], []
        for first, line in ((0, lines[0]), (cut, lines[1])):
            value = jnp.stack(line)
            by_near, by_far = swap(value, 2), swap(value, 4)
            across = swap(by_near, 4) if first else swap(by_far, 2)
            for flip, found in enumerate((value, by_near, by_far, across)):
                for part, arrived in enumerate((found, swap(found, 1))):
                    pieces.append(arrived)
                    copies.append([(i, (flip, i), part, held, first, cut) for i in range(cols)])
        owners = (0, 0, -1, 1, 1, -1)
        small_inputs = []
    else:
        sent = weights[0].T.reshape(rows * toks, columns, row_width)
        own_weights = lax.all_to_all(sent, ("row", "tok"), 0, 0, tiled=True)
        own_weights = own_weights.reshape(rows, models * columns, row_width)
        weight_pieces = [own_weights.transpose(1, 0, 2).reshape(models * columns, width)]
        places = [(0, 0)]
        held = slots
        everything = lax.all_gather(features, ("row", "col"), axis=0, tiled=False)
        pieces = [lax.all_gather(everything, "tok", axis=0, tiled=True)]
        tiles = slots // LANES
        owners = tuple(m for m in range(models) for _ in range(tiles))
        copies = [[
            (m * rows * cols + b, b, m, slots, 0, block) for m in range(models) for b in range(rows * cols)
        ]]
        live = jnp.arange(slots, dtype=jnp.int32)[None, :] < lengths[:, None]
        floats = features.astype(jnp.float32)
        squares = lax.psum(jnp.sum(floats * floats, axis=0), ("row", "col"))
        every_gain = lax.all_gather(gains[0], ("row", "col"), axis=0, tiled=True)
        small_inputs = [
            live.reshape(1, -1).astype(jnp.float32),
            lax.all_gather(squares, "tok", axis=0, tiled=True)[None, :],
            lax.all_gather(every_gain, "tok", axis=0, tiled=False).T,
        ]
    slots_held = toks * held

    if paired:
        out_shape = [jax.ShapeDtypeStruct((columns, sub_rows), jnp.bfloat16)] * (rows * toks)
    else:
        out_shape = [jax.ShapeDtypeStruct((columns, width), jnp.bfloat16)]
    found = pl.pallas_call(
        functools.partial(solve_kernel, owners, models, block, copies, places),
        out_shape=out_shape,
        in_specs=[scalars] + [in_vmem] * len(small_inputs) + [any_space] * (len(pieces) + len(weight_pieces)),
        out_specs=[in_vmem] * len(out_shape),
        scratch_shapes=[
            pltpu.VMEM((width, slots_held), jnp.bfloat16),
            pltpu.VMEM((models * columns, width), jnp.bfloat16),
            pltpu.VMEM((models, width), jnp.float32),
            pltpu.VMEM((1, width), jnp.float32),
            pltpu.VMEM((columns, width), jnp.float32),
            pltpu.VMEM((columns, width), jnp.float32),
            pltpu.VMEM((columns, width), jnp.float32),
            pltpu.VMEM((2 * columns, width), jnp.bfloat16),
            pltpu.VMEM((max(models, 2) * columns, slots_held), jnp.float32),
            pltpu.VMEM((columns, slots_held), jnp.bfloat16),
            pltpu.VMEM((2 * columns, slots_held), jnp.bfloat16),
            pltpu.VMEM((models * rows * cols, 16, slots_held // models) if paired else (8, 16, LANES), jnp.bfloat16),
            pltpu.VMEM((width if paired else 8, LANES), jnp.float32),
            pltpu.SemaphoreType.DMA((2,)),
        ],
        compiler_params=pltpu.CompilerParams(vmem_limit_bytes=width * slots_held * 2 + (18 << 20)),
    )(
        lengths,
        *small_inputs,
        *pieces,
        *weight_pieces,
    )
    if paired:
        arrived = [found[0]] + [swap(x, flip) for x, flip in zip(found[1:], NEAR_FIRST[1:])]
        return pl.pallas_call(
            gather_kernel,
            out_shape=jax.ShapeDtypeStruct((sub_rows, col_width), jnp.float32),
            in_specs=[in_vmem] * len(arrived),
            out_specs=in_vmem,
            scratch_shapes=[pltpu.VMEM((col_width, sub_rows), jnp.float32)],
            compiler_params=small,
        )(*arrived)
    found = found[0].reshape(columns, rows * toks, sub_rows).transpose(1, 0, 2)
    back = lax.all_to_all(found, ("row", "tok"), 0, 0, tiled=True)
    return back.reshape(col_width, sub_rows).T.astype(jnp.float32)


def solution(mesh):
    return jax.shard_map(
        body,
        mesh=mesh,
        in_specs=(P("tok", ("row", "col")), P("tok", ("row", "col")), P("tok", "row", "col"), P()),
        out_specs=P(("row", "tok"), "col"),
        check_vma=False,
    )
```

time: 308 us -> 117 us (0.38)
  blocking collectives: 79.9 us -> 0 us
  Pallas kernels: 94.6 us -> 34.1 us
  local copies, waits for them, and re-layouts: 61.2 us -> 1.35 us
  waiting for transfers between devices: 30.5 us -> 57.5 us
  starting transfers between devices: 36.4 us -> 24.2 us
    psum x1 -> x0, blocking collectives: 79.9 us -> none  [body(): shared = lax.psum(shared, ('tok', 'row', 'col'))]
    pallas_call x2 -> x4, Pallas kernels: 63.1 us -> 2.89 us  [the longest x1 1.56 us: body(): pl.pallas_call(gather_kernel, out_shape=jax.ShapeDtypeStruct((sub_rows, c...]
    unnamed x117 -> x8, local copies, waits for them, and re-layouts: 37.9 us -> 1.34 us
    ppermute x43 -> x26, waiting for transfers between devices: 26.3 us -> 39.8 us  [swap(): return lax.ppermute(value, ('tok', 'row'), pairs)]
    ppermute x3 -> x6, waiting for transfers between devices: 4.23 us -> 17.7 us  [body(): line.append(lax.ppermute(line[-1], 'col', up))]
    ppermute x43 -> x26, starting transfers between devices: 27.9 us -> 19.2 us  [swap(): return lax.ppermute(value, ('tok', 'row'), pairs)]
    dynamic_update_slice x2 -> x0, local copies, waits for them, and re-layouts: 8.07 us -> none  [the longest x1 8.02 us: body(): lax.dynamic_update_slice(jnp.zeros((toks, held + width), jnp.float32), jn...]
    broadcast_in_dim x5 -> x0, local copies, waits for them, and re-layouts: 5.2 us -> none  [the longest x1 3.41 us: body(): jnp.concatenate([squares, spread])[None]]
  transfers between devices with their start and end apart: 46 -> 32, of which waited for: 18 -> 14; matrix products, arithmetic and copies ran while one was open for 7% -> 0% of each run, Pallas kernels for 0% -> 1%
where the time goes in v2:
time: 117 us
  waiting for transfers between devices  57.5 us (49%)
  Pallas kernels  34.1 us (29%)
  starting transfers between devices  24.2 us (21%)
  local copies, waits for them, and re-layouts  1.35 us (1%)
    ppermute x26, waiting for transfers between devices, swap(): return lax.ppermute(value, ('tok', 'row'), pairs)  39.8 us
    pallas_call x1, Pallas kernels, body(): pl.pallas_call(functools.partial(solve_kernel, owners, models, block, cop...  31.2 us
    ppermute x26, starting transfers between devices, swap(): return lax.ppermute(value, ('tok', 'row'), pairs)  19.2 us
    ppermute x6, waiting for transfers between devices, body(): line.append(lax.ppermute(line[-1], 'col', up))  17.7 us
    ppermute x6, starting transfers between devices, body(): line.append(lax.ppermute(line[-1], 'col', up))  4.98 us
  transfers between devices with their start and end apart: 32, of which 14 were waited for; matrix products, arithmetic and copies ran while one was open for 0% of the time, Pallas kernels for 1%

profile of v2, /device:TPU:0, one launch (start us, length us, event | category | flops | bytes accessed | tf_op | source)
XLA Modules:
  0.0 117.3 jit_solution(2562961991538356498)
XLA Ops:
  0.0 1.3 %copy-done = bf16[1,1280,512]{2,1,0:T(8,128)(2,1)S(1)} copy-done((bf16[1,1280,512]{2,1,0:T(8,128)(2,1)S(1)}, bf16[1,1280,512]{2,1,0:T(8,128)(2,1)}, u32[]{:S(2)}) %copy-start) | copy-done | bytes 1310744
  2.8 1.4 %collective-permute-done.given_ref = bf16[320,128]{1,0:T(8,128)(2,1)S(1)} collective-permute-done((bf16[320,128]{1,0:T(8,128)(2,1)S(1)}, bf16[320,128]{1,0:T(8,128)(2,1)S(1)}, u32[]{:S(2)}, u32[]{:S(2)}) %collective-permute-start) | collective-permute-done | bytes 81952 | tf_op jit(solution)/shard_map/ppermute | solution.py:336
  5.0 3.0 %collective-permute-start.1 = (bf16[176,384]{1,0:T(8,128)(2,1)S(1)}, bf16[176,384]{1,0:T(8,128)(2,1)S(1)}, u32[]{:S(2)}, u32[]{:S(2)}) collective-permute-start(bf16[176,384]{1,0:T(8,128)(2,1)S(1)} %get-tuple-element.41), channel_id=1, source_target_pairs={{0,1},{1,2},{2,3},{3,0},{4,5},{5,6},{6,7},{7,4},{8,9},{9,10},{10,1... | collective-permute-start | bytes 405512 | tf_op jit(solution)/shard_map/ppermute | solution.py:374
  8.0 1.6 %collective-permute-start.4 = (bf16[160,384]{1,0:T(8,128)(2,1)S(1)}, bf16[160,384]{1,0:T(8,128)(2,1)S(1)}, u32[]{:S(2)}, u32[]{:S(2)}) collective-permute-start(bf16[160,384]{1,0:T(8,128)(2,1)S(1)} %get-tuple-element.45), channel_id=1, source_target_pairs={{0,1},{1,2},{2,3},{3,0},{4,5},{5,6},{6,7},{7,4},{8,9},{9,10},{10,1... | collective-permute-start | bytes 368648 | tf_op jit(solution)/shard_map/ppermute | solution.py:374
  9.6 1.6 %collective-permute-start.8 = (bf16[128,1280]{1,0:T(8,128)(2,1)S(1)}, bf16[128,1280]{1,0:T(8,128)(2,1)S(1)}, u32[]{:S(2)}, u32[]{:S(2)}) collective-permute-start(bf16[128,1280]{1,0:T(8,128)(2,1)S(1)} %get-tuple-element.38), channel_id=1, source_target_pairs={{0,4},{4,0},{8,12},{12,8},{16,20},{20,16},{24,28},{28,24},{1,5},{5... | collective-permute-start | bytes 983048 | tf_op jit(solution)/shard_map/ppermute | solution.py:336
  11.2 1.5 %collective-permute-start.9 = (bf16[128,1280]{1,0:T(8,128)(2,1)S(1)}, bf16[128,1280]{1,0:T(8,128)(2,1)S(1)}, u32[]{:S(2)}, u32[]{:S(2)}) collective-permute-start(bf16[128,1280]{1,0:T(8,128)(2,1)S(1)} %get-tuple-element.39), channel_id=1, source_target_pairs={{0,8},{4,12},{8,0},{12,4},{16,24},{20,28},{24,16},{28,20},{1,9},{5... | collective-permute-start | bytes 983048 | tf_op jit(solution)/shard_map/ppermute | solution.py:336
  13.2 1.2 %collective-permute-done.1 = bf16[176,384]{1,0:T(8,128)(2,1)S(1)} collective-permute-done((bf16[176,384]{1,0:T(8,128)(2,1)S(1)}, bf16[176,384]{1,0:T(8,128)(2,1)S(1)}, u32[]{:S(2)}, u32[]{:S(2)}) %collective-permute-start.1) | collective-permute-done | bytes 135200 | tf_op jit(solution)/shard_map/ppermute | solution.py:374
  14.8 1.7 %collective-permute-done.4 = bf16[160,384]{1,0:T(8,128)(2,1)S(1)} collective-permute-done((bf16[160,384]{1,0:T(8,128)(2,1)S(1)}, bf16[160,384]{1,0:T(8,128)(2,1)S(1)}, u32[]{:S(2)}, u32[]{:S(2)}) %collective-permute-start.4) | collective-permute-done | bytes 122912 | tf_op jit(solution)/shard_map/ppermute | solution.py:374
  16.5 5.3 %collective-permute-done.2 = bf16[176,384]{1,0:T(8,128)(2,1)S(1)} collective-permute-done((bf16[176,384]{1,0:T(8,128)(2,1)S(1)}, bf16[176,384]{1,0:T(8,128)(2,1)S(1)}, u32[]{:S(2)}, u32[]{:S(2)}) %collective-permute-start.2) | collective-permute-done | bytes 135200 | tf_op jit(solution)/shard_map/ppermute | solution.py:374
  21.8 2.1 %collective-permute-done.5 = bf16[160,384]{1,0:T(8,128)(2,1)S(1)} collective-permute-done((bf16[160,384]{1,0:T(8,128)(2,1)S(1)}, bf16[160,384]{1,0:T(8,128)(2,1)S(1)}, u32[]{:S(2)}, u32[]{:S(2)}) %collective-permute-start.5) | collective-permute-done | bytes 122912 | tf_op jit(solution)/shard_map/ppermute | solution.py:374
  24.0 7.3 %collective-permute-done.6 = bf16[160,384]{1,0:T(8,128)(2,1)S(1)} collective-permute-done((bf16[160,384]{1,0:T(8,128)(2,1)S(1)}, bf16[160,384]{1,0:T(8,128)(2,1)S(1)}, u32[]{:S(2)}, u32[]{:S(2)}) %collective-permute-start.6) | collective-permute-done | bytes 122912 | tf_op jit(solution)/shard_map/ppermute | solution.py:374
  31.4 1.8 %collective-permute-start.14 = (bf16[4,176,384]{2,1,0:T(8,128)(2,1)S(1)}, bf16[4,176,384]{2,1,0:T(8,128)(2,1)S(1)}, u32[]{:S(2)}, u32[]{:S(2)}) collective-permute-start(bf16[4,176,384]{2,1,0:T(8,128)(2,1)S(1)} %pad_maximum_fusion.refs_0_), channel_id=1, source_target_pairs={{0,8},{4,12},{8,0},{12,4},{16,24},{20,28},{24,16},{28,20},{1,9},{5... | collective-permute-start | bytes 1622024 | tf_op jit(solution)/shard_map/ppermute | solution.py:336
  33.6 1.7 %collective-permute-start.19 = (bf16[4,160,384]{2,1,0:T(8,128)(2,1)S(1)}, bf16[4,160,384]{2,1,0:T(8,128)(2,1)S(1)}, u32[]{:S(2)}, u32[]{:S(2)}) collective-permute-start(bf16[4,160,384]{2,1,0:T(8,128)(2,1)S(1)} %pad_maximum_fusion.1.refs_8_), channel_id=1, source_target_pairs={{0,4},{4,0},{8,12},{12,8},{16,20},{20,16},{24,28},{28,24},{1,5},{5... | collective-permute-start | bytes 1474568 | tf_op jit(solution)/shard_map/ppermute | solution.py:336
  35.7 19.4 %collective-permute-done.21.refs_12_ = bf16[4,160,384]{2,1,0:T(8,128)(2,1)S(1)} collective-permute-done((bf16[4,160,384]{2,1,0:T(8,128)(2,1)S(1)}, bf16[4,160,384]{2,1,0:T(8,128)(2,1)S(1)}, u32[]{:S(2)}, u32[]{:S(2)}) %collective-permute-start.21) | collective-permute-done | bytes 491552 | tf_op jit(solution)/shard_map/ppermute | solution.py:336
  56.3 1.5 %collective-permute-start.23 = (bf16[4,160,384]{2,1,0:T(8,128)(2,1)S(1)}, bf16[4,160,384]{2,1,0:T(8,128)(2,1)S(1)}, u32[]{:S(2)}, u32[]{:S(2)}) collective-permute-start(bf16[4,160,384]{2,1,0:T(8,128)(2,1)S(1)} %collective-permute-done.19.refs_10_), channel_id=1, source_target_pairs={{0,8},{4,12},{8,0},{12,4},{16,24},{20,28},{24,16},{28,20},{1,9},{5... | collective-permute-start | bytes 1474568 | tf_op jit(solution)/shard_map/ppermute | solution.py:336
  58.4 11.4 %collective-permute-done.16.refs_6_ = bf16[4,176,384]{2,1,0:T(8,128)(2,1)S(1)} collective-permute-done((bf16[4,176,384]{2,1,0:T(8,128)(2,1)S(1)}, bf16[4,176,384]{2,1,0:T(8,128)(2,1)S(1)}, u32[]{:S(2)}, u32[]{:S(2)}) %collective-permute-start.16) | collective-permute-done | bytes 540704 | tf_op jit(solution)/shard_map/ppermute | solution.py:336
  70.4 2.0 %collective-permute-done.20.refs_11_ = bf16[4,160,384]{2,1,0:T(8,128)(2,1)S(1)} collective-permute-done((bf16[4,160,384]{2,1,0:T(8,128)(2,1)S(1)}, bf16[4,160,384]{2,1,0:T(8,128)(2,1)S(1)}, u32[]{:S(2)}, u32[]{:S(2)}) %collective-permute-start.20) | collective-permute-done | bytes 491552 | tf_op jit(solution)/shard_map/ppermute | solution.py:336
  73.1 31.2 %shard_map.49 = (bf16[64,640]{1,0:T(8,128)(2,1)S(1)}, bf16[64,640]{1,0:T(8,128)(2,1)S(1)}, bf16[64,640]{1,0:T(8,128)(2,1)S(1)}, bf16[64,640]{1,0:T(8,128)(2,1)S(...) custom-call(s32[2]{0:T(128)S(1)} %copy-done.2, ...), custom_call_target="tpu_custom_call" | custom-call | tf_op jit(solution)/shard_map/pallas_call | solution.py:416
  104.4 1.0 collective-permute-start.25
  105.4 1.5 %collective-permute-start.26 = (bf16[64,640]{1,0:T(8,128)(2,1)S(1)}, bf16[64,640]{1,0:T(8,128)(2,1)S(1)}, u32[]{:S(2)}, u32[]{:S(2)}) collective-permute-start(bf16[64,640]{1,0:T(8,128)(2,1)S(1)} %get-tuple-element.55), channel_id=1, source_target_pairs={{0,8},{4,12},{8,0},{12,4},{16,24},{20,28},{24,16},{28,20},{1,9},{5... | collective-permute-start | bytes 245768 | tf_op jit(solution)/shard_map/ppermute | solution.py:336
  107.9 2.2 %collective-permute-start.29 = (bf16[64,640]{1,0:T(8,128)(2,1)S(1)}, bf16[64,640]{1,0:T(8,128)(2,1)S(1)}, u32[]{:S(2)}, u32[]{:S(2)}) collective-permute-start(bf16[64,640]{1,0:T(8,128)(2,1)S(1)} %get-tuple-element.58), channel_id=1, source_target_pairs={{0,24},{4,28},{8,16},{12,20},{16,8},{20,12},{24,0},{28,4},{1,25},{... | collective-permute-start | bytes 245768 | tf_op jit(solution)/shard_map/ppermute | solution.py:336
  111.4 1.9 %collective-permute-done.27.refs_3_ = bf16[64,640]{1,0:T(8,128)(2,1)S(1)} collective-permute-done((bf16[64,640]{1,0:T(8,128)(2,1)S(1)}, bf16[64,640]{1,0:T(8,128)(2,1)S(1)}, u32[]{:S(2)}, u32[]{:S(2)}) %collective-permute-start.27) | collective-permute-done | bytes 81952 | tf_op jit(solution)/shard_map/ppermute | solution.py:336
  114.2 1.6 %collective-permute-done.30.refs_6_ = bf16[64,640]{1,0:T(8,128)(2,1)S(1)} collective-permute-done((bf16[64,640]{1,0:T(8,128)(2,1)S(1)}, bf16[64,640]{1,0:T(8,128)(2,1)S(1)}, u32[]{:S(2)}, u32[]{:S(2)}) %collective-permute-start.30) | collective-permute-done | bytes 81952 | tf_op jit(solution)/shard_map/ppermute | solution.py:336
  115.8 1.6 %shard_map.50 = f32[640,512]{1,0:T(8,128)} custom-call(bf16[64,640]{1,0:T(8,128)(2,1)S(1)} %get-tuple-element.53.refs_0_, bf16[64,640]{1,0:T(8,128)(2,1)S(1)} %collective-permute-done.25.refs_1_, bf16[64,640]{1,0:T(8,128)(2,1)S(1)} %collective-permute-done.26.refs_2_, bf16[64,640]{1,0:T(8,128)(2,1)S(1)} %collective-permute-done.27.refs_3_, ...), custom_call_target="tpu_custom_call" | custom-call | tf_op jit(solution)/shard_map/pallas_call | solution.py:446
  (56 shorter events, 10.3 us)
Async XLA Ops:
  1.8 7.7 %collective-permute-start.7 = (bf16[4,64,1280]{2,1,0:T(8,128)(2,1)S(1)}, bf16[4,64,1280]{2,1,0:T(8,128)(2,1)S(1)}, u32[]{:S(2)}, u32[]{:S(2)}) collective-permute-start(bf16[4,64,1280]{2,1,0:T(8,128)(2,1)S(1)} %get-tuple-element.36), channel_id=1, source_target_pairs={{0,16},{4,20},{8,24},{12,28},{16,0},{20,4},{24,8},{28,12},{1,17},{... | collective-permute-start | bytes 1966088 | tf_op jit(solution)/shard_map/ppermute | solution.py:336
  5.0 9.4 %collective-permute-start.1 = (bf16[176,384]{1,0:T(8,128)(2,1)S(1)}, bf16[176,384]{1,0:T(8,128)(2,1)S(1)}, u32[]{:S(2)}, u32[]{:S(2)}) collective-permute-start(bf16[176,384]{1,0:T(8,128)(2,1)S(1)} %get-tuple-element.41), channel_id=1, source_target_pairs={{0,1},{1,2},{2,3},{3,0},{4,5},{5,6},{6,7},{7,4},{8,9},{9,10},{10,1... | collective-permute-start | bytes 405512 | tf_op jit(solution)/shard_map/ppermute | solution.py:374
  8.0 8.5 %collective-permute-start.4 = (bf16[160,384]{1,0:T(8,128)(2,1)S(1)}, bf16[160,384]{1,0:T(8,128)(2,1)S(1)}, u32[]{:S(2)}, u32[]{:S(2)}) collective-permute-start(bf16[160,384]{1,0:T(8,128)(2,1)S(1)} %get-tuple-element.45), channel_id=1, source_target_pairs={{0,1},{1,2},{2,3},{3,0},{4,5},{5,6},{6,7},{7,4},{8,9},{9,10},{10,1... | collective-permute-start | bytes 368648 | tf_op jit(solution)/shard_map/ppermute | solution.py:374
  9.6 21.7 %collective-permute-start.8 = (bf16[128,1280]{1,0:T(8,128)(2,1)S(1)}, bf16[128,1280]{1,0:T(8,128)(2,1)S(1)}, u32[]{:S(2)}, u32[]{:S(2)}) collective-permute-start(bf16[128,1280]{1,0:T(8,128)(2,1)S(1)} %get-tuple-element.38), channel_id=1, source_target_pairs={{0,4},{4,0},{8,12},{12,8},{16,20},{20,16},{24,28},{28,24},{1,5},{5... | collective-permute-start | bytes 983048 | tf_op jit(solution)/shard_map/ppermute | solution.py:336
  11.2 20.1 %collective-permute-start.9 = (bf16[128,1280]{1,0:T(8,128)(2,1)S(1)}, bf16[128,1280]{1,0:T(8,128)(2,1)S(1)}, u32[]{:S(2)}, u32[]{:S(2)}) collective-permute-start(bf16[128,1280]{1,0:T(8,128)(2,1)S(1)} %get-tuple-element.39), channel_id=1, source_target_pairs={{0,8},{4,12},{8,0},{12,4},{16,24},{20,28},{24,16},{28,20},{1,9},{5... | collective-permute-start | bytes 983048 | tf_op jit(solution)/shard_map/ppermute | solution.py:336
  12.7 18.6 %collective-permute-start.10 = (bf16[128,1280]{1,0:T(8,128)(2,1)S(1)}, bf16[128,1280]{1,0:T(8,128)(2,1)S(1)}, u32[]{:S(2)}, u32[]{:S(2)}) collective-permute-start(bf16[128,1280]{1,0:T(8,128)(2,1)S(1)} %get-tuple-element.40), channel_id=1, source_target_pairs={{0,12},{4,8},{8,4},{12,0},{16,28},{20,24},{24,20},{28,16},{1,13},{... | collective-permute-start | bytes 983048 | tf_op jit(solution)/shard_map/ppermute | solution.py:336
  14.3 7.5 %collective-permute-start.2 = (bf16[176,384]{1,0:T(8,128)(2,1)S(1)}, bf16[176,384]{1,0:T(8,128)(2,1)S(1)}, u32[]{:S(2)}, u32[]{:S(2)}) collective-permute-start(bf16[176,384]{1,0:T(8,128)(2,1)S(1)} %collective-permute-done.1), channel_id=1, source_target_pairs={{0,1},{1,2},{2,3},{3,0},{4,5},{5,6},{6,7},{7,4},{8,9},{9,10},{10,1... | collective-permute-start | bytes 405512 | tf_op jit(solution)/shard_map/ppermute | solution.py:374
  16.5 7.5 %collective-permute-start.5 = (bf16[160,384]{1,0:T(8,128)(2,1)S(1)}, bf16[160,384]{1,0:T(8,128)(2,1)S(1)}, u32[]{:S(2)}, u32[]{:S(2)}) collective-permute-start(bf16[160,384]{1,0:T(8,128)(2,1)S(1)} %collective-permute-done.4), channel_id=1, source_target_pairs={{0,1},{1,2},{2,3},{3,0},{4,5},{5,6},{6,7},{7,4},{8,9},{9,10},{10,1... | collective-permute-start | bytes 368648 | tf_op jit(solution)/shard_map/ppermute | solution.py:374
  21.8 9.4 %collective-permute-start.3 = (bf16[176,384]{1,0:T(8,128)(2,1)S(1)}, bf16[176,384]{1,0:T(8,128)(2,1)S(1)}, u32[]{:S(2)}, u32[]{:S(2)}) collective-permute-start(bf16[176,384]{1,0:T(8,128)(2,1)S(1)} %collective-permute-done.2), channel_id=1, source_target_pairs={{0,1},{1,2},{2,3},{3,0},{4,5},{5,6},{6,7},{7,4},{8,9},{9,10},{10,1... | collective-permute-start | bytes 405512 | tf_op jit(solution)/shard_map/ppermute | solution.py:374
  24.0 7.3 %collective-permute-start.6 = (bf16[160,384]{1,0:T(8,128)(2,1)S(1)}, bf16[160,384]{1,0:T(8,128)(2,1)S(1)}, u32[]{:S(2)}, u32[]{:S(2)}) collective-permute-start(bf16[160,384]{1,0:T(8,128)(2,1)S(1)} %collective-permute-done.5), channel_id=1, source_target_pairs={{0,1},{1,2},{2,3},{3,0},{4,5},{5,6},{6,7},{7,4},{8,9},{9,10},{10,1... | collective-permute-start | bytes 368648 | tf_op jit(solution)/shard_map/ppermute | solution.py:374
  31.4 23.7 %collective-permute-start.14 = (bf16[4,176,384]{2,1,0:T(8,128)(2,1)S(1)}, bf16[4,176,384]{2,1,0:T(8,128)(2,1)S(1)}, u32[]{:S(2)}, u32[]{:S(2)}) collective-permute-start(bf16[4,176,384]{2,1,0:T(8,128)(2,1)S(1)} %pad_maximum_fusion.refs_0_), channel_id=1, source_target_pairs={{0,8},{4,12},{8,0},{12,4},{16,24},{20,28},{24,16},{28,20},{1,9},{5... | collective-permute-start | bytes 1622024 | tf_op jit(solution)/shard_map/ppermute | solution.py:336
  33.3 21.8 %collective-permute-start.21 = (bf16[4,160,384]{2,1,0:T(8,128)(2,1)S(1)}, bf16[4,160,384]{2,1,0:T(8,128)(2,1)S(1)}, u32[]{:S(2)}, u32[]{:S(2)}) collective-permute-start(bf16[4,160,384]{2,1,0:T(8,128)(2,1)S(1)} %pad_maximum_fusion.1.refs_8_), channel_id=1, source_target_pairs={{0,8},{4,12},{8,0},{12,4},{16,24},{20,28},{24,16},{28,20},{1,9},{5... | collective-permute-start | bytes 1474568 | tf_op jit(solution)/shard_map/ppermute | solution.py:336
  33.6 22.5 %collective-permute-start.19 = (bf16[4,160,384]{2,1,0:T(8,128)(2,1)S(1)}, bf16[4,160,384]{2,1,0:T(8,128)(2,1)S(1)}, u32[]{:S(2)}, u32[]{:S(2)}) collective-permute-start(bf16[4,160,384]{2,1,0:T(8,128)(2,1)S(1)} %pad_maximum_fusion.1.refs_8_), channel_id=1, source_target_pairs={{0,4},{4,0},{8,12},{12,8},{16,20},{20,16},{24,28},{28,24},{1,5},{5... | collective-permute-start | bytes 1474568 | tf_op jit(solution)/shard_map/ppermute | solution.py:336
  35.3 21.0 %collective-permute-start.18 = (bf16[4,160,384]{2,1,0:T(8,128)(2,1)S(1)}, bf16[4,160,384]{2,1,0:T(8,128)(2,1)S(1)}, u32[]{:S(2)}, u32[]{:S(2)}) collective-permute-start(bf16[4,160,384]{2,1,0:T(8,128)(2,1)S(1)} %pad_maximum_fusion.1.refs_8_), channel_id=1, source_target_pairs={{0,16},{4,20},{8,24},{12,28},{16,0},{20,4},{24,8},{28,12},{1,17},{... | collective-permute-start | bytes 1474568 | tf_op jit(solution)/shard_map/ppermute | solution.py:336
  35.3 22.5 %collective-permute-start.12 = (bf16[4,176,384]{2,1,0:T(8,128)(2,1)S(1)}, bf16[4,176,384]{2,1,0:T(8,128)(2,1)S(1)}, u32[]{:S(2)}, u32[]{:S(2)}) collective-permute-start(bf16[4,176,384]{2,1,0:T(8,128)(2,1)S(1)} %pad_maximum_fusion.refs_0_), channel_id=1, source_target_pairs={{0,4},{4,0},{8,12},{12,8},{16,20},{20,16},{24,28},{28,24},{1,5},{5... | collective-permute-start | bytes 1622024 | tf_op jit(solution)/shard_map/ppermute | solution.py:336
  55.1 14.7 %collective-permute-start.16 = (bf16[4,176,384]{2,1,0:T(8,128)(2,1)S(1)}, bf16[4,176,384]{2,1,0:T(8,128)(2,1)S(1)}, u32[]{:S(2)}, u32[]{:S(2)}) collective-permute-start(bf16[4,176,384]{2,1,0:T(8,128)(2,1)S(1)} %collective-permute-done.14.refs_4_), channel_id=1, source_target_pairs={{0,4},{4,0},{8,12},{12,8},{16,20},{20,16},{24,28},{28,24},{1,5},{5... | collective-permute-start | bytes 1622024 | tf_op jit(solution)/shard_map/ppermute | solution.py:336
  56.1 13.7 %collective-permute-start.22 = (bf16[4,160,384]{2,1,0:T(8,128)(2,1)S(1)}, bf16[4,160,384]{2,1,0:T(8,128)(2,1)S(1)}, u32[]{:S(2)}, u32[]{:S(2)}) collective-permute-start(bf16[4,160,384]{2,1,0:T(8,128)(2,1)S(1)} %collective-permute-done.21.refs_12_), channel_id=1, source_target_pairs={{0,16},{4,20},{8,24},{12,28},{16,0},{20,4},{24,8},{28,12},{1,17},{... | collective-permute-start | bytes 1474568 | tf_op jit(solution)/shard_map/ppermute | solution.py:336
  56.3 14.0 %collective-permute-start.23 = (bf16[4,160,384]{2,1,0:T(8,128)(2,1)S(1)}, bf16[4,160,384]{2,1,0:T(8,128)(2,1)S(1)}, u32[]{:S(2)}, u32[]{:S(2)}) collective-permute-start(bf16[4,160,384]{2,1,0:T(8,128)(2,1)S(1)} %collective-permute-done.19.refs_10_), channel_id=1, source_target_pairs={{0,8},{4,12},{8,0},{12,4},{16,24},{20,28},{24,16},{28,20},{1,9},{5... | collective-permute-start | bytes 1474568 | tf_op jit(solution)/shard_map/ppermute | solution.py:336
  57.9 14.6 %collective-permute-start.15 = (bf16[4,176,384]{2,1,0:T(8,128)(2,1)S(1)}, bf16[4,176,384]{2,1,0:T(8,128)(2,1)S(1)}, u32[]{:S(2)}, u32[]{:S(2)}) collective-permute-start(bf16[4,176,384]{2,1,0:T(8,128)(2,1)S(1)} %collective-permute-done.14.refs_4_), channel_id=1, source_target_pairs={{0,16},{4,20},{8,24},{12,28},{16,0},{20,4},{24,8},{28,12},{1,17},{... | collective-permute-start | bytes 1622024 | tf_op jit(solution)/shard_map/ppermute | solution.py:336
  57.9 14.6 %collective-permute-start.13 = (bf16[4,176,384]{2,1,0:T(8,128)(2,1)S(1)}, bf16[4,176,384]{2,1,0:T(8,128)(2,1)S(1)}, u32[]{:S(2)}, u32[]{:S(2)}) collective-permute-start(bf16[4,176,384]{2,1,0:T(8,128)(2,1)S(1)} %collective-permute-done.12.refs_2_), channel_id=1, source_target_pairs={{0,16},{4,20},{8,24},{12,28},{16,0},{20,4},{24,8},{28,12},{1,17},{... | collective-permute-start | bytes 1622024 | tf_op jit(solution)/shard_map/ppermute | solution.py:336
  104.4 5.8 %collective-permute-start.25 = (bf16[64,640]{1,0:T(8,128)(2,1)S(1)}, bf16[64,640]{1,0:T(8,128)(2,1)S(1)}, u32[]{:S(2)}, u32[]{:S(2)}) collective-permute-start(bf16[64,640]{1,0:T(8,128)(2,1)S(1)} %get-tuple-element.54), channel_id=1, source_target_pairs={{0,4},{4,0},{8,12},{12,8},{16,20},{20,16},{24,28},{28,24},{1,5},{5... | collective-permute-start | bytes 245768 | tf_op jit(solution)/shard_map/ppermute | solution.py:336
  106.9 6.3 %collective-permute-start.27 = (bf16[64,640]{1,0:T(8,128)(2,1)S(1)}, bf16[64,640]{1,0:T(8,128)(2,1)S(1)}, u32[]{:S(2)}, u32[]{:S(2)}) collective-permute-start(bf16[64,640]{1,0:T(8,128)(2,1)S(1)} %get-tuple-element.56), channel_id=1, source_target_pairs={{0,12},{4,8},{8,4},{12,0},{16,28},{20,24},{24,20},{28,16},{1,13},{... | collective-permute-start | bytes 245768 | tf_op jit(solution)/shard_map/ppermute | solution.py:336
  107.9 6.3 %collective-permute-start.29 = (bf16[64,640]{1,0:T(8,128)(2,1)S(1)}, bf16[64,640]{1,0:T(8,128)(2,1)S(1)}, u32[]{:S(2)}, u32[]{:S(2)}) collective-permute-start(bf16[64,640]{1,0:T(8,128)(2,1)S(1)} %get-tuple-element.58), channel_id=1, source_target_pairs={{0,24},{4,28},{8,16},{12,20},{16,8},{20,12},{24,0},{28,4},{1,25},{... | collective-permute-start | bytes 245768 | tf_op jit(solution)/shard_map/ppermute | solution.py:336
  110.1 5.6 %collective-permute-start.30 = (bf16[64,640]{1,0:T(8,128)(2,1)S(1)}, bf16[64,640]{1,0:T(8,128)(2,1)S(1)}, u32[]{:S(2)}, u32[]{:S(2)}) collective-permute-start(bf16[64,640]{1,0:T(8,128)(2,1)S(1)} %get-tuple-element.59), channel_id=1, source_target_pairs={{0,28},{4,24},{8,20},{12,16},{16,12},{20,8},{24,4},{28,0},{1,29},{... | collective-permute-start | bytes 245768 | tf_op jit(solution)/shard_map/ppermute | solution.py:336
  (12 other events, 38.5 us)

commit v3 on v2

--- a/solution.py
+++ b/solution.py
@@ -52,11 +52,12 @@
     return lax.fori_loop(0, slots // CHUNK, some, jnp.zeros((left.shape[0], CHUNK), jnp.float32))
 
 
-def in_pair_order(lengths_ref, width):
+def in_pair_order(lengths_ref, tok, width):
     half, quarter = width // 3, width // 6
     lane = lax.broadcasted_iota(jnp.int32, (1, width), 1)
-    part = jnp.where(lane >= width // 2, 1, 0)
-    spot = lane - part * (width // 2)
+    low = lane < width // 2
+    part = jnp.where(low, tok, 1 - tok)
+    spot = jnp.where(low, lane, lane - width // 2)
     place = spot - half + part * quarter
     late = spot >= half
     second = jnp.where(late, jnp.where(place >= lengths_ref[0] - half, 1, 0), part)
@@ -65,46 +66,107 @@
     return jnp.where(position < length, 1.0, 0.0), second.astype(jnp.float32)
 
 
+def norm_pieces(block, copies, pieces, lengths_ref, tokens, squared, diagonal, gains, sums, extras):
+    width, slots = tokens.shape
+    row, col, tok = lax.axis_index("row"), lax.axis_index("col"), lax.axis_index("tok")
+    cols = lax.axis_size("col")
+    held = slots // 2
+    live, second = in_pair_order(lengths_ref, tok, slots)
+
+    def start_of(flip, back):
+        return ((row ^ flip) * cols + lax.rem(col - back + cols, cols)) * block
+
+    extras[...] = jnp.zeros_like(extras)
+    squares = [jnp.zeros((1, held), jnp.float32) for _ in range(2)]
+    riders = []
+    for number, (by_flip, flip, back, first, high) in enumerate(copies):
+        if pieces[2 * number].shape[1] > high:
+            for index in range(cols):
+                for part in range(2):
+                    rows = pieces[2 * number + part][index, high:high + 16, :].astype(jnp.float32)
+                    squares[part] = squares[part] + (rows[0:1] + rows[1:2] + rows[2:3])
+                    spot = 2 * len(riders) + part
+                    extras[spot:spot + 1, :] = rows[3:4] + rows[4:5] + rows[5:6]
+                riders.append((flip, back + index))
+    scale = lax.rsqrt(jnp.concatenate(squares, axis=1) / width + EPSILON) * live
+    turned = extras[...].T[:block]
+    side = lax.broadcasted_iota(jnp.int32, (block, LANES), 1)
+    for spot, (flip, back) in enumerate(riders):
+        gains[pl.ds(pl.multiple_of(start_of(flip, back), 64), block), :] = jnp.where(
+            side == 0, turned[:, 2 * spot:2 * spot + 1], turned[:, 2 * spot + 1:2 * spot + 2]
+        )
+
+    for number, (by_flip, flip, back, first, high) in enumerate(copies):
+        both = pieces[2 * number:2 * number + 2]
+
+        def norm_block(index, carry, both=both, by_flip=by_flip, flip=flip, back=back, first=first, high=high):
+            place = start_of(index, back) if by_flip else start_of(flip, back + index)
+            low = 0
+            while low < high:
+                size = min(80 if high % 80 == 0 else 64, high - low)
+                start = pl.multiple_of(place + first + low, 16)
+                gain = gains[pl.ds(start, size), :]
+                own, other = gain[:, 0:1], gain[:, 1:2]
+                gain_first = jnp.where(tok == 0, own, other)
+                gain_second = jnp.where(tok == 0, other, own)
+                sums_part = [jnp.zeros((size, LANES), jnp.float32) for _ in range(2)]
+                sums_model = [jnp.zeros((size, LANES), jnp.float32) for _ in range(2)]
+                for part in range(2):
+                    for tile in range(held // LANES):
+                        lanes = slice(part * held + tile * LANES, part * held + (tile + 1) * LANES)
+                        value = both[part][index, low:low + size, tile * LANES:(tile + 1) * LANES].astype(jnp.float32)
+                        mixed = tile == held // LANES - 1
+                        if mixed:
+                            factor = jnp.where(second[:, lanes] > 0, gain_second, gain_first)
+                        else:
+                            factor = (own, other)[part]
+                        normed = (value * scale[:, lanes] * factor).astype(jnp.bfloat16)
+                        tokens[pl.ds(start, size), lanes] = normed
+                        value = normed.astype(jnp.float32)
+                        value = value * value
+                        if mixed:
+                            theirs = value * second[:, lanes]
+                            sums_model[0] = sums_model[0] + (value - theirs)
+                            sums_model[1] = sums_model[1] + theirs
+                        else:
+                            sums_part[part] = sums_part[part] + value
+                total = [
+                    jnp.sum(sums_model[model] + jnp.where(tok == model, sums_part[0], sums_part[1]), axis=1, keepdims=True)
+                    for model in range(2)
+                ]
+                lane = lax.broadcasted_iota(jnp.int32, (size, LANES), 1)
+                sums[pl.ds(start, size), :] = jnp.where(lane == 0, total[0], total[1])
+                low += size
+            return carry
+
+        lax.fori_loop(0, cols, norm_block, 0)
+
+    def turn(step, carry):
+        start = pl.multiple_of(step * LANES, LANES)
+        rows = sums[pl.ds(start, LANES), :].T
+        squared[:, pl.ds(start, LANES)] = rows[0:2]
+        diagonal[:, pl.ds(start, LANES)] = rows[0:1] + rows[1:2]
+        return carry
+
+    lax.fori_loop(0, width // LANES, turn, 0, unroll=4)
+    return second
+
+
 def solve_kernel(owners, models, block, copies, places, lengths_ref, *refs):
     riding = len(copies) > 1
     if not riding:
         live_ref, squares_ref, gains_ref, refs = refs[0], refs[1], refs[2], refs[3:]
-    pieces = refs[:len(copies)]
-    weight_pieces = refs[len(copies):len(copies) + len(places)]
-    out_refs = refs[len(copies) + len(places):-14]
+    count = 2 * len(copies) if riding else len(copies)
+    pieces = refs[:count]
+    weight_pieces = refs[count:count + len(places)]
+    out_refs = refs[count + len(places):-15]
     (tokens, weights, squared, diagonal, residual, direction, merged, terms, values, outputs, seen, extras, gains_held,
-     sems) = refs[-14:]
+     sums_held, sems) = refs[-15:]
     width, slots = tokens.shape
     columns = residual.shape[0]
-    blocks = width // block
     started = []
     if riding:
-        row, col, tok = lax.axis_index("row"), lax.axis_index("col"), lax.axis_index("tok")
-        cols = lax.axis_size("col")
-        row_devices = lax.axis_size("row")
-    for piece, parts in zip(pieces, copies):
-        for source, entry, part, lanes, first, held in parts:
-            if riding:
-                flip, back = entry
-                entry = (row ^ flip) * cols + lax.rem(col - back + cols, cols)
-                part = tok ^ part
-            start = pl.multiple_of(entry * block + first, 16)
-            lane = pl.multiple_of(part * lanes, LANES)
-            copy = pltpu.make_async_copy(
-                piece.at[source, pl.ds(0, held)],
-                tokens.at[pl.ds(start, held), pl.ds(lane, lanes)],
-                sems.at[0],
-            )
-            copy.start()
-            started.append(copy)
-            if piece.shape[1] > held:
-                copy = pltpu.make_async_copy(
-                    piece.at[source, pl.ds(held, 16)],
-                    extras.at[part * blocks + entry],
-                    sems.at[0],
-                )
-                copy.start()
-                started.append(copy)
+        row, tok = lax.axis_index("row"), lax.axis_index("tok")
     for piece, place in zip(weight_pieces, places):
         moves = [(piece, weights)]
         if riding:
@@ -121,31 +183,16 @@
             copy = pltpu.make_async_copy(source, target, sems.at[1])
             copy.start()
             started.append(copy)
-    for copy in started:
-        copy.wait()
-
-    if riding:
-        every = extras[...].astype(jnp.float32)
-        sums = [jnp.sum(every[part * blocks:(part + 1) * blocks], axis=0) for part in range(models)]
-        squares = jnp.concatenate([x[0:1] + x[1:2] + x[2:3] for x in sums], axis=1)
-        turned = (every[:, 3] + every[:, 4] + every[:, 5]).T[:block]
-        lane = lax.broadcasted_iota(jnp.int32, turned.shape, 1)
-        side = lax.broadcasted_iota(jnp.int32, (block, LANES), 1)
-
-        def hold_gains(step, carry):
-            gain = [
-                jnp.sum(jnp.where(lane == part * blocks + step, turned, 0.0), axis=1, keepdims=True)
-                for part in range(models)
-            ]
-            gains_held[pl.ds(pl.multiple_of(step * block, block), block), :] = jnp.where(side == 0, gain[0], gain[1])
-            return carry
-
-        lax.fori_loop(0, blocks, hold_gains, 0)
-        gains_ref = gains_held
-        live, second = in_pair_order(lengths_ref, slots)
-    else:
-        squares, live = squares_ref[...], live_ref[...]
-    inverse_rms = lax.rsqrt(squares / width + EPSILON) * live
+    if not riding:
+        for piece, parts in zip(pieces, copies):
+            for source, entry, part, lanes in parts:
+                copy = pltpu.make_async_copy(
+                    piece.at[source],
+                    tokens.at[pl.ds(entry * block, block), pl.ds(part * lanes, lanes)],
+                    sems.at[0],
+                )
+                copy.start()
+                started.append(copy)
 
     def norm_rows(step, carry):
         start = pl.multiple_of(step * LANES, LANES)
@@ -154,37 +201,33 @@
         for tile, owner in enumerate(owners):
             lanes = slice(tile * LANES, (tile + 1) * LANES)
             value = tokens[pl.ds(start, LANES), lanes].astype(jnp.float32)
-            if owner < 0:
-                gain = jnp.where(second[:, lanes] > 0, gains[:, 1:2], gains[:, 0:1])
-            else:
-                gain = gains[:, owner:owner + 1]
-            normed = (value * inverse_rms[:, lanes] * gain).astype(jnp.bfloat16)
+            normed = (value * inverse_rms[:, lanes] * gains[:, owner:owner + 1]).astype(jnp.bfloat16)
             tokens[pl.ds(start, LANES), lanes] = normed
             value = normed.astype(jnp.float32)
-            value = value * value
-            if owner < 0:
-                theirs = value * second[:, lanes]
-                sums[0] = sums[0] + (value - theirs)
-                sums[1] = sums[1] + theirs
-            else:
-                sums[owner] = sums[owner] + value
+            sums[owner] = sums[owner] + value * value
         sums = [jnp.sum(part.T, axis=0, keepdims=True) for part in sums]
         for model in range(models):
             squared[model:model + 1, pl.ds(start, LANES)] = sums[model]
         diagonal[:, pl.ds(start, LANES)] = functools.reduce(jnp.add, sums)
         return carry
 
-    lax.fori_loop(0, width // LANES, norm_rows, 0, unroll=4 if riding else 1)
+    if riding:
+        second = norm_pieces(
+            block, copies, pieces, lengths_ref, tokens, squared, diagonal, gains_held, sums_held, extras
+        )
+    for copy in started:
+        copy.wait()
+    if not riding:
+        inverse_rms = lax.rsqrt(squares_ref[...] / width + EPSILON) * live_ref[...]
+        lax.fori_loop(0, width // LANES, norm_rows, 0)
 
     over_features(weights, tokens, values)
-    picked = []
-    for tile, owner in enumerate(owners):
-        lanes = slice(tile * LANES, (tile + 1) * LANES)
-        if owner < 0:
-            picked.append(jnp.where(second[:, lanes] > 0, values[columns:2 * columns, lanes], values[:columns, lanes]))
-        else:
-            picked.append(values[owner * columns:(owner + 1) * columns, lanes])
-    outputs[...] = jnp.concatenate(picked, axis=1).astype(jnp.bfloat16)
+    if riding:
+        outputs[...] = jnp.where(second > 0, values[columns:2 * columns, :], values[:columns, :]).astype(jnp.bfloat16)
+    else:
+        for tile, owner in enumerate(owners):
+            lanes = slice(tile * LANES, (tile + 1) * LANES)
+            outputs[:, lanes] = values[owner * columns:(owner + 1) * columns, lanes].astype(jnp.bfloat16)
 
     norm_now = jnp.zeros((columns, 1), jnp.float32)
     for start in range(0, width, CHUNK):
@@ -266,7 +309,7 @@
     place = lax.broadcasted_iota(jnp.int32, (block, quarter), 1) + tok * quarter
     mixed = jnp.where(place >= lengths_ref[0] - half, turned, jnp.where(first, lower, given))
     kept = features_ref[:, :half]
-    cut = lower_ref.shape[0]
+    cut = block - lower_ref.shape[0]
     upper_ref[:cut, :half] = kept[:cut]
     upper_ref[:cut, half:] = mixed[:cut].astype(jnp.bfloat16)
     lower_ref[:, :half] = kept[cut:]
@@ -354,13 +397,12 @@
             out_specs=[in_vmem] * rows,
             compiler_params=small,
         )(own, swap(other, 1))
-        weight_pieces = [swap(value, 2 * flip) if flip else value for flip, value in enumerate(joined)]
-        places = list(range(rows))
-        cut = block // 2
+        cut = block * 3 // 4
         upper, lower = pl.pallas_call(
             piece_kernel,
             out_shape=[
-                jax.ShapeDtypeStruct((cut + 16, held), jnp.bfloat16), jax.ShapeDtypeStruct((cut, held), jnp.bfloat16)
+                jax.ShapeDtypeStruct((cut + 16, held), jnp.bfloat16),
+                jax.ShapeDtypeStruct((block - cut, held), jnp.bfloat16),
             ],
             in_specs=[scalars, in_vmem, in_vmem, in_vmem],
             out_specs=[in_vmem] * 2,
@@ -368,21 +410,33 @@
             compiler_params=small,
         )(lengths, features, given, gains)
         up = [(i, (i + 1) % cols) for i in range(cols)]
-        lines = [[upper], [lower]]
+        line = [upper]
         for _ in range(cols - 1):
-            for line in lines:
-                line.append(lax.ppermute(line[-1], "col", up))
-        lines, weight_pieces = lax.optimization_barrier((lines, weight_pieces))
+            line.append(lax.ppermute(line[-1], "col", up))
+        by_near, by_far = swap(lower, 2), swap(lower, 4)
+        (by_near, by_far), joined = lax.optimization_barrier(((by_near, by_far), joined))
+        plane = [lower, by_near, by_far, swap(by_far, 2)]
+        weight_pieces = [swap(value, 2 * flip) if flip else value for flip, value in enumerate(joined)]
+        places = list(range(rows))
+        line, plane, weight_pieces = lax.optimization_barrier((line, plane, weight_pieces))
+        value = jnp.stack(line)
+        by_near, by_far = swap(value, 2), swap(value, 4)
+        middle = (cut + 16) // 2
+        crossed = [
+            (0, 0, value), (1, 0, by_near), (2, 0, by_far),
+            (3, 0, swap(by_far[:, :middle], 2)), (3, middle, swap(by_near[:, middle:], 4)),
+        ]
+        rounds = [jnp.stack(plane)]
+        for _ in range(cols - 1):
+            rounds.append(lax.ppermute(rounds[-1], "col", up))
         pieces, copies = [], []
-        for first, line in ((0, lines[0]), (cut, lines[1])):
-            value = jnp.stack(line)
-            by_near, by_far = swap(value, 2), swap(value, 4)
-            across = swap(by_near, 4) if first else swap(by_far, 2)
-            for flip, found in enumerate((value, by_near, by_far, across)):
-                for part, arrived in enumerate((found, swap(found, 1))):
-                    pieces.append(arrived)
-                    copies.append([(i, (flip, i), part, held, first, cut) for i in range(cols)])
-        owners = (0, 0, -1, 1, 1, -1)
+        for flip, first, found in crossed:
+            pieces += [found, swap(found, 1)]
+            copies.append((False, flip, 0, first, min(first + found.shape[1], cut) - first))
+        for back, found in enumerate(rounds):
+            pieces += [found, swap(found, 1)]
+            copies.append((True, 0, back, cut, block - cut))
+        owners = ()
         small_inputs = []
     else:
         sent = weights[0].T.reshape(rows * toks, columns, row_width)
@@ -396,7 +450,7 @@
         tiles = slots // LANES
         owners = tuple(m for m in range(models) for _ in range(tiles))
         copies = [[
-            (m * rows * cols + b, b, m, slots, 0, block) for m in range(models) for b in range(rows * cols)
+            (m * rows * cols + b, b, m, slots) for m in range(models) for b in range(rows * cols)
         ]]
         live = jnp.arange(slots, dtype=jnp.int32)[None, :] < lengths[:, None]
         floats = features.astype(jnp.float32)
@@ -416,7 +470,8 @@
     found = pl.pallas_call(
         functools.partial(solve_kernel, owners, models, block, copies, places),
         out_shape=out_shape,
-        in_specs=[scalars] + [in_vmem] * len(small_inputs) + [any_space] * (len(pieces) + len(weight_pieces)),
+        in_specs=[scalars] + [in_vmem] * len(small_inputs) + [in_vmem if paired else any_space] * len(pieces)
+        + [any_space] * len(weight_pieces),
         out_specs=[in_vmem] * len(out_shape),
         scratch_shapes=[
             pltpu.VMEM((width, slots_held), jnp.bfloat16),
@@ -430,7 +485,8 @@
             pltpu.VMEM((max(models, 2) * columns, slots_held), jnp.float32),
             pltpu.VMEM((columns, slots_held), jnp.bfloat16),
             pltpu.VMEM((2 * columns, slots_held), jnp.bfloat16),
-            pltpu.VMEM((models * rows * cols, 16, slots_held // models) if paired else (8, 16, LANES), jnp.bfloat16),
+            pltpu.VMEM((LANES, held if paired else LANES), jnp.float32),
+            pltpu.VMEM((width if paired else 8, LANES), jnp.float32),
             pltpu.VMEM((width if paired else 8, LANES), jnp.float32),
             pltpu.SemaphoreType.DMA((2,)),
         ],

time: 117 us -> 122 us (1.043)
  Pallas kernels: 34.1 us -> 41.2 us
  waiting for transfers between devices: 57.5 us -> 52.4 us
  starting transfers between devices: 24.2 us -> 26.1 us
    ppermute x0 -> x3, waiting for transfers between devices: none -> 22.7 us  [body(): rounds.append(lax.ppermute(rounds[-1], 'col', up))]
    ppermute x26 -> x28, waiting for transfers between devices: 39.8 us -> 17.8 us  [swap(): return lax.ppermute(value, ('tok', 'row'), pairs)]
    pallas_call x1, Pallas kernels: 31.2 us -> 38.3 us  [body(): pl.pallas_call(functools.partial(solve_kernel, owners, models, block, cop...]
    ppermute x6 -> x3, waiting for transfers between devices: 17.7 us -> 11.9 us  [body(): line.append(lax.ppermute(line[-1], 'col', up))]
    ppermute x26 -> x28, starting transfers between devices: 19.2 us -> 20.7 us  [swap(): return lax.ppermute(value, ('tok', 'row'), pairs)]
    ppermute x6 -> x3, starting transfers between devices: 4.98 us -> 4.28 us  [body(): line.append(lax.ppermute(line[-1], 'col', up))]
  transfers between devices with their start and end apart: 32 -> 34, of which waited for: 14 -> 17; matrix products, arithmetic and copies ran while one was open for 0% -> 0% of each run, Pallas kernels for 1% -> 1%
where the time goes in v3:
time: 122 us; the launch traced here: 121 us
  waiting for transfers between devices  52.4 us (43%)
  Pallas kernels  41.2 us (34%)
  starting transfers between devices  26.1 us (21%)
  local copies, waits for them, and re-layouts  1.43 us (1%)
    pallas_call x1, Pallas kernels, body(): pl.pallas_call(functools.partial(solve_kernel, owners, models, block, cop...  38.3 us
    ppermute x3, waiting for transfers between devices, body(): rounds.append(lax.ppermute(rounds[-1], 'col', up))  22.7 us
    ppermute x28, starting transfers between devices, swap(): return lax.ppermute(value, ('tok', 'row'), pairs)  20.7 us
    ppermute x28, waiting for transfers between devices, swap(): return lax.ppermute(value, ('tok', 'row'), pairs)  17.8 us
    ppermute x3, waiting for transfers between devices, body(): line.append(lax.ppermute(line[-1], 'col', up))  11.9 us
    ppermute x3, starting transfers between devices, body(): line.append(lax.ppermute(line[-1], 'col', up))  4.28 us
  transfers between devices with their start and end apart: 34, of which 17 were waited for; matrix products, arithmetic and copies ran while one was open for 0% of the time, Pallas kernels for 1%

profile of v3, /device:TPU:0, one launch (start us, length us, event | category | flops | bytes accessed | tf_op | source)
XLA Modules:
  0.0 121.4 jit_solution(12531644117094655255)
XLA Ops:
  0.0 1.3 %copy-done = bf16[1,1280,512]{2,1,0:T(8,128)(2,1)S(1)} copy-done((bf16[1,1280,512]{2,1,0:T(8,128)(2,1)S(1)}, bf16[1,1280,512]{2,1,0:T(8,128)(2,1)}, u32[]{:S(2)}) %copy-start) | copy-done | bytes 1310744
  2.8 1.4 %collective-permute-done.given_ref = bf16[320,128]{1,0:T(8,128)(2,1)S(1)} collective-permute-done((bf16[320,128]{1,0:T(8,128)(2,1)S(1)}, bf16[320,128]{1,0:T(8,128)(2,1)S(1)}, u32[]{:S(2)}, u32[]{:S(2)}) %collective-permute-start) | collective-permute-done | bytes 81952 | tf_op jit(solution)/shard_map/ppermute | solution.py:379
  5.0 3.0 %collective-permute-start.1 = (bf16[256,384]{1,0:T(8,128)(2,1)S(1)}, bf16[256,384]{1,0:T(8,128)(2,1)S(1)}, u32[]{:S(2)}, u32[]{:S(2)}) collective-permute-start(bf16[256,384]{1,0:T(8,128)(2,1)S(1)} %get-tuple-element.53), channel_id=1, source_target_pairs={{0,1},{1,2},{2,3},{3,0},{4,5},{5,6},{6,7},{7,4},{8,9},{9,10},{10,1... | collective-permute-start | bytes 589832 | tf_op jit(solution)/shard_map/ppermute | solution.py:415
  7.9 7.2 %collective-permute-done.1 = bf16[256,384]{1,0:T(8,128)(2,1)S(1)} collective-permute-done((bf16[256,384]{1,0:T(8,128)(2,1)S(1)}, bf16[256,384]{1,0:T(8,128)(2,1)S(1)}, u32[]{:S(2)}, u32[]{:S(2)}) %collective-permute-start.1) | collective-permute-done | bytes 196640 | tf_op jit(solution)/shard_map/ppermute | solution.py:415
  15.2 1.5 %collective-permute-start.5 = (bf16[80,384]{1,0:T(8,128)(2,1)S(1)}, bf16[80,384]{1,0:T(8,128)(2,1)S(1)}, u32[]{:S(2)}, u32[]{:S(2)}) collective-permute-start(bf16[80,384]{1,0:T(8,128)(2,1)S(1)} %get-tuple-element.57), channel_id=1, source_target_pairs={{0,8},{4,12},{8,0},{12,4},{16,24},{20,28},{24,16},{28,20},{1,9},{5... | collective-permute-start | bytes 184328 | tf_op jit(solution)/shard_map/ppermute | solution.py:379
  16.7 1.5 %collective-permute-start.4 = (bf16[80,384]{1,0:T(8,128)(2,1)S(1)}, bf16[80,384]{1,0:T(8,128)(2,1)S(1)}, u32[]{:S(2)}, u32[]{:S(2)}) collective-permute-start(bf16[80,384]{1,0:T(8,128)(2,1)S(1)} %get-tuple-element.57), channel_id=1, source_target_pairs={{0,4},{4,0},{8,12},{12,8},{16,20},{20,16},{24,28},{28,24},{1,5},{5... | collective-permute-start | bytes 184328 | tf_op jit(solution)/shard_map/ppermute | solution.py:379
  19.4 1.5 %collective-permute-done.4 = bf16[80,384]{1,0:T(8,128)(2,1)S(1)} collective-permute-done((bf16[80,384]{1,0:T(8,128)(2,1)S(1)}, bf16[80,384]{1,0:T(8,128)(2,1)S(1)}, u32[]{:S(2)}, u32[]{:S(2)}) %collective-permute-start.4) | collective-permute-done | bytes 61472 | tf_op jit(solution)/shard_map/ppermute | solution.py:379
  20.9 1.5 %collective-permute-start.8 = (bf16[128,1280]{1,0:T(8,128)(2,1)S(1)}, bf16[128,1280]{1,0:T(8,128)(2,1)S(1)}, u32[]{:S(2)}, u32[]{:S(2)}) collective-permute-start(bf16[128,1280]{1,0:T(8,128)(2,1)S(1)} %get-tuple-element.50), channel_id=1, source_target_pairs={{0,4},{4,0},{8,12},{12,8},{16,20},{20,16},{24,28},{28,24},{1,5},{5... | collective-permute-start | bytes 983048 | tf_op jit(solution)/shard_map/ppermute | solution.py:379
  22.9 1.5 %collective-permute-start.10 = (bf16[128,1280]{1,0:T(8,128)(2,1)S(1)}, bf16[128,1280]{1,0:T(8,128)(2,1)S(1)}, u32[]{:S(2)}, u32[]{:S(2)}) collective-permute-start(bf16[128,1280]{1,0:T(8,128)(2,1)S(1)} %get-tuple-element.52), channel_id=1, source_target_pairs={{0,12},{4,8},{8,4},{12,0},{16,28},{20,24},{24,20},{28,16},{1,13},{... | collective-permute-start | bytes 983048 | tf_op jit(solution)/shard_map/ppermute | solution.py:379
  24.4 1.3 %collective-permute-start.3 = (bf16[256,384]{1,0:T(8,128)(2,1)S(1)}, bf16[256,384]{1,0:T(8,128)(2,1)S(1)}, u32[]{:S(2)}, u32[]{:S(2)}) collective-permute-start(bf16[256,384]{1,0:T(8,128)(2,1)S(1)} %collective-permute-done.2), channel_id=1, source_target_pairs={{0,1},{1,2},{2,3},{3,0},{4,5},{5,6},{6,7},{7,4},{8,9},{9,10},{10,1... | collective-permute-start | bytes 589832 | tf_op jit(solution)/shard_map/ppermute | solution.py:415
  25.7 1.5 %collective-permute-start.7 = (bf16[80,384]{1,0:T(8,128)(2,1)S(1)}, bf16[80,384]{1,0:T(8,128)(2,1)S(1)}, u32[]{:S(2)}, u32[]{:S(2)}) collective-permute-start(bf16[80,384]{1,0:T(8,128)(2,1)S(1)} %collective-permute-done.5), channel_id=1, source_target_pairs={{0,4},{4,0},{8,12},{12,8},{16,20},{20,16},{24,28},{28,24},{1,5},{5... | collective-permute-start | bytes 184328 | tf_op jit(solution)/shard_map/ppermute | solution.py:379
  27.2 4.7 %collective-permute-done.3 = bf16[256,384]{1,0:T(8,128)(2,1)S(1)} collective-permute-done((bf16[256,384]{1,0:T(8,128)(2,1)S(1)}, bf16[256,384]{1,0:T(8,128)(2,1)S(1)}, u32[]{:S(2)}, u32[]{:S(2)}) %collective-permute-start.3) | collective-permute-done | bytes 196640 | tf_op jit(solution)/shard_map/ppermute | solution.py:415
  31.9 5.2 %collective-permute-done.7 = bf16[80,384]{1,0:T(8,128)(2,1)S(1)} collective-permute-done((bf16[80,384]{1,0:T(8,128)(2,1)S(1)}, bf16[80,384]{1,0:T(8,128)(2,1)S(1)}, u32[]{:S(2)}, u32[]{:S(2)}) %collective-permute-start.7) | collective-permute-done | bytes 61472 | tf_op jit(solution)/shard_map/ppermute | solution.py:379
  38.1 1.5 %collective-permute-start.12 = (bf16[4,256,384]{2,1,0:T(8,128)(2,1)S(1)}, bf16[4,256,384]{2,1,0:T(8,128)(2,1)S(1)}, u32[]{:S(2)}, u32[]{:S(2)}) collective-permute-start(bf16[4,256,384]{2,1,0:T(8,128)(2,1)S(1)} %pad_maximum_fusion.refs_0_), channel_id=1, source_target_pairs={{0,4},{4,0},{8,12},{12,8},{16,20},{20,16},{24,28},{28,24},{1,5},{5... | collective-permute-start | bytes 2359304 | tf_op jit(solution)/shard_map/ppermute | solution.py:379
  40.7 7.4 %collective-permute-done.21.refs_12_ = bf16[4,80,384]{2,1,0:T(8,128)(2,1)S(1)} collective-permute-done((bf16[4,80,384]{2,1,0:T(8,128)(2,1)S(1)}, bf16[4,80,384]{2,1,0:T(8,128)(2,1)S(1)}, u32[]{:S(2)}, u32[]{:S(2)}) %collective-permute-start.21) | collective-permute-done | bytes 245792 | tf_op jit(solution)/shard_map/ppermute | solution.py:431
  48.8 7.4 %collective-permute-done.23.refs_14_ = bf16[4,80,384]{2,1,0:T(8,128)(2,1)S(1)} collective-permute-done((bf16[4,80,384]{2,1,0:T(8,128)(2,1)S(1)}, bf16[4,80,384]{2,1,0:T(8,128)(2,1)S(1)}, u32[]{:S(2)}, u32[]{:S(2)}) %collective-permute-start.23) | collective-permute-done | bytes 245792 | tf_op jit(solution)/shard_map/ppermute | solution.py:431
  58.4 7.9 %collective-permute-done.25.refs_16_ = bf16[4,80,384]{2,1,0:T(8,128)(2,1)S(1)} collective-permute-done((bf16[4,80,384]{2,1,0:T(8,128)(2,1)S(1)}, bf16[4,80,384]{2,1,0:T(8,128)(2,1)S(1)}, u32[]{:S(2)}, u32[]{:S(2)}) %collective-permute-start.25) | collective-permute-done | bytes 245792 | tf_op jit(solution)/shard_map/ppermute | solution.py:431
  69.3 1.9 %collective-permute-done.26.refs_17_ = bf16[4,80,384]{2,1,0:T(8,128)(2,1)S(1)} collective-permute-done((bf16[4,80,384]{2,1,0:T(8,128)(2,1)S(1)}, bf16[4,80,384]{2,1,0:T(8,128)(2,1)S(1)}, u32[]{:S(2)}, u32[]{:S(2)}) %collective-permute-start.26) | collective-permute-done | bytes 245792 | tf_op jit(solution)/shard_map/ppermute | solution.py:379
  71.2 38.3 %shard_map.49 = (bf16[64,640]{1,0:T(8,128)(2,1)S(1)}, bf16[64,640]{1,0:T(8,128)(2,1)S(1)}, bf16[64,640]{1,0:T(8,128)(2,1)S(1)}, bf16[64,640]{1,0:T(8,128)(2,1)S(...) custom-call(s32[2]{0:T(128)S(1)} %copy-done.2, ...), custom_call_target="tpu_custom_call" | custom-call | tf_op jit(solution)/shard_map/pallas_call | solution.py:470
  111.0 2.1 %collective-permute-start.29 = (bf16[64,640]{1,0:T(8,128)(2,1)S(1)}, bf16[64,640]{1,0:T(8,128)(2,1)S(1)}, u32[]{:S(2)}, u32[]{:S(2)}) collective-permute-start(bf16[64,640]{1,0:T(8,128)(2,1)S(1)} %get-tuple-element.68), channel_id=1, source_target_pairs={{0,12},{4,8},{8,4},{12,0},{16,28},{20,24},{24,20},{28,16},{1,13},{... | collective-permute-start | bytes 245768 | tf_op jit(solution)/shard_map/ppermute | solution.py:379
  113.0 1.1 collective-permute-start.31
  116.4 1.4 %collective-permute-done.30.refs_4_ = bf16[64,640]{1,0:T(8,128)(2,1)S(1)} collective-permute-done((bf16[64,640]{1,0:T(8,128)(2,1)S(1)}, bf16[64,640]{1,0:T(8,128)(2,1)S(1)}, u32[]{:S(2)}, u32[]{:S(2)}) %collective-permute-start.30) | collective-permute-done | bytes 81952 | tf_op jit(solution)/shard_map/ppermute | solution.py:379
  117.8 2.1 %collective-permute-done.32.refs_6_ = bf16[64,640]{1,0:T(8,128)(2,1)S(1)} collective-permute-done((bf16[64,640]{1,0:T(8,128)(2,1)S(1)}, bf16[64,640]{1,0:T(8,128)(2,1)S(1)}, u32[]{:S(2)}, u32[]{:S(2)}) %collective-permute-start.32) | collective-permute-done | bytes 81952 | tf_op jit(solution)/shard_map/ppermute | solution.py:379
  119.8 1.6 %shard_map.50 = f32[640,512]{1,0:T(8,128)} custom-call(bf16[64,640]{1,0:T(8,128)(2,1)S(1)} %get-tuple-element.65.refs_0_, bf16[64,640]{1,0:T(8,128)(2,1)S(1)} %collective-permute-done.27.refs_1_, bf16[64,640]{1,0:T(8,128)(2,1)S(1)} %collective-permute-done.28.refs_2_, bf16[64,640]{1,0:T(8,128)(2,1)S(1)} %collective-permute-done.29.refs_3_, ...), custom_call_target="tpu_custom_call" | custom-call | tf_op jit(solution)/shard_map/pallas_call | solution.py:502
  (62 shorter events, 15.6 us)
Async XLA Ops:
  1.8 16.4 %collective-permute-start.6 = (bf16[4,64,1280]{2,1,0:T(8,128)(2,1)S(1)}, bf16[4,64,1280]{2,1,0:T(8,128)(2,1)S(1)}, u32[]{:S(2)}, u32[]{:S(2)}) collective-permute-start(bf16[4,64,1280]{2,1,0:T(8,128)(2,1)S(1)} %get-tuple-element.42), channel_id=1, source_target_pairs={{0,16},{4,20},{8,24},{12,28},{16,0},{20,4},{24,8},{28,12},{1,17},{... | collective-permute-start | bytes 1966088 | tf_op jit(solution)/shard_map/ppermute | solution.py:379
  5.0 10.2 %collective-permute-start.1 = (bf16[256,384]{1,0:T(8,128)(2,1)S(1)}, bf16[256,384]{1,0:T(8,128)(2,1)S(1)}, u32[]{:S(2)}, u32[]{:S(2)}) collective-permute-start(bf16[256,384]{1,0:T(8,128)(2,1)S(1)} %get-tuple-element.53), channel_id=1, source_target_pairs={{0,1},{1,2},{2,3},{3,0},{4,5},{5,6},{6,7},{7,4},{8,9},{9,10},{10,1... | collective-permute-start | bytes 589832 | tf_op jit(solution)/shard_map/ppermute | solution.py:415
  15.2 9.2 %collective-permute-start.2 = (bf16[256,384]{1,0:T(8,128)(2,1)S(1)}, bf16[256,384]{1,0:T(8,128)(2,1)S(1)}, u32[]{:S(2)}, u32[]{:S(2)}) collective-permute-start(bf16[256,384]{1,0:T(8,128)(2,1)S(1)} %collective-permute-done.1), channel_id=1, source_target_pairs={{0,1},{1,2},{2,3},{3,0},{4,5},{5,6},{6,7},{7,4},{8,9},{9,10},{10,1... | collective-permute-start | bytes 589832 | tf_op jit(solution)/shard_map/ppermute | solution.py:415
  20.9 16.2 %collective-permute-start.8 = (bf16[128,1280]{1,0:T(8,128)(2,1)S(1)}, bf16[128,1280]{1,0:T(8,128)(2,1)S(1)}, u32[]{:S(2)}, u32[]{:S(2)}) collective-permute-start(bf16[128,1280]{1,0:T(8,128)(2,1)S(1)} %get-tuple-element.50), channel_id=1, source_target_pairs={{0,4},{4,0},{8,12},{12,8},{16,20},{20,16},{24,28},{28,24},{1,5},{5... | collective-permute-start | bytes 983048 | tf_op jit(solution)/shard_map/ppermute | solution.py:379
  22.4 14.7 %collective-permute-start.9 = (bf16[128,1280]{1,0:T(8,128)(2,1)S(1)}, bf16[128,1280]{1,0:T(8,128)(2,1)S(1)}, u32[]{:S(2)}, u32[]{:S(2)}) collective-permute-start(bf16[128,1280]{1,0:T(8,128)(2,1)S(1)} %get-tuple-element.51), channel_id=1, source_target_pairs={{0,8},{4,12},{8,0},{12,4},{16,24},{20,28},{24,16},{28,20},{1,9},{5... | collective-permute-start | bytes 983048 | tf_op jit(solution)/shard_map/ppermute | solution.py:379
  22.9 14.2 %collective-permute-start.10 = (bf16[128,1280]{1,0:T(8,128)(2,1)S(1)}, bf16[128,1280]{1,0:T(8,128)(2,1)S(1)}, u32[]{:S(2)}, u32[]{:S(2)}) collective-permute-start(bf16[128,1280]{1,0:T(8,128)(2,1)S(1)} %get-tuple-element.52), channel_id=1, source_target_pairs={{0,12},{4,8},{8,4},{12,0},{16,28},{20,24},{24,20},{28,16},{1,13},{... | collective-permute-start | bytes 983048 | tf_op jit(solution)/shard_map/ppermute | solution.py:379
  24.4 7.5 %collective-permute-start.3 = (bf16[256,384]{1,0:T(8,128)(2,1)S(1)}, bf16[256,384]{1,0:T(8,128)(2,1)S(1)}, u32[]{:S(2)}, u32[]{:S(2)}) collective-permute-start(bf16[256,384]{1,0:T(8,128)(2,1)S(1)} %collective-permute-done.2), channel_id=1, source_target_pairs={{0,1},{1,2},{2,3},{3,0},{4,5},{5,6},{6,7},{7,4},{8,9},{9,10},{10,1... | collective-permute-start | bytes 589832 | tf_op jit(solution)/shard_map/ppermute | solution.py:415
  25.7 11.4 %collective-permute-start.7 = (bf16[80,384]{1,0:T(8,128)(2,1)S(1)}, bf16[80,384]{1,0:T(8,128)(2,1)S(1)}, u32[]{:S(2)}, u32[]{:S(2)}) collective-permute-start(bf16[80,384]{1,0:T(8,128)(2,1)S(1)} %collective-permute-done.5), channel_id=1, source_target_pairs={{0,4},{4,0},{8,12},{12,8},{16,20},{20,16},{24,28},{28,24},{1,5},{5... | collective-permute-start | bytes 184328 | tf_op jit(solution)/shard_map/ppermute | solution.py:379
  37.3 18.9 %collective-permute-start.14 = (bf16[4,256,384]{2,1,0:T(8,128)(2,1)S(1)}, bf16[4,256,384]{2,1,0:T(8,128)(2,1)S(1)}, u32[]{:S(2)}, u32[]{:S(2)}) collective-permute-start(bf16[4,256,384]{2,1,0:T(8,128)(2,1)S(1)} %pad_maximum_fusion.refs_0_), channel_id=1, source_target_pairs={{0,8},{4,12},{8,0},{12,4},{16,24},{20,28},{24,16},{28,20},{1,9},{5... | collective-permute-start | bytes 2359304 | tf_op jit(solution)/shard_map/ppermute | solution.py:379
  38.1 18.0 %collective-permute-start.12 = (bf16[4,256,384]{2,1,0:T(8,128)(2,1)S(1)}, bf16[4,256,384]{2,1,0:T(8,128)(2,1)S(1)}, u32[]{:S(2)}, u32[]{:S(2)}) collective-permute-start(bf16[4,256,384]{2,1,0:T(8,128)(2,1)S(1)} %pad_maximum_fusion.refs_0_), channel_id=1, source_target_pairs={{0,4},{4,0},{8,12},{12,8},{16,20},{20,16},{24,28},{28,24},{1,5},{5... | collective-permute-start | bytes 2359304 | tf_op jit(solution)/shard_map/ppermute | solution.py:379
  39.7 8.4 %collective-permute-start.21 = (bf16[4,80,384]{2,1,0:T(8,128)(2,1)S(1)}, bf16[4,80,384]{2,1,0:T(8,128)(2,1)S(1)}, u32[]{:S(2)}, u32[]{:S(2)}) collective-permute-start(bf16[4,80,384]{2,1,0:T(8,128)(2,1)S(1)} %pad_maximum_fusion.1.refs_10_), channel_id=1, source_target_pairs={{0,1},{1,2},{2,3},{3,0},{4,5},{5,6},{6,7},{7,4},{8,9},{9,10},{10,1... | collective-permute-start | bytes 737288 | tf_op jit(solution)/shard_map/ppermute | solution.py:431
  48.1 8.0 %collective-permute-start.23 = (bf16[4,80,384]{2,1,0:T(8,128)(2,1)S(1)}, bf16[4,80,384]{2,1,0:T(8,128)(2,1)S(1)}, u32[]{:S(2)}, u32[]{:S(2)}) collective-permute-start(bf16[4,80,384]{2,1,0:T(8,128)(2,1)S(1)} %collective-permute-done.21.refs_12_), channel_id=1, source_target_pairs={{0,1},{1,2},{2,3},{3,0},{4,5},{5,6},{6,7},{7,4},{8,9},{9,10},{10,1... | collective-permute-start | bytes 737288 | tf_op jit(solution)/shard_map/ppermute | solution.py:431
  48.2 8.6 %collective-permute-start.20 = (bf16[4,80,384]{2,1,0:T(8,128)(2,1)S(1)}, bf16[4,80,384]{2,1,0:T(8,128)(2,1)S(1)}, u32[]{:S(2)}, u32[]{:S(2)}) collective-permute-start(bf16[4,80,384]{2,1,0:T(8,128)(2,1)S(1)} %pad_maximum_fusion.1.refs_10_), channel_id=1, source_target_pairs={{0,16},{4,20},{8,24},{12,28},{16,0},{20,4},{24,8},{28,12},{1,17},{... | collective-permute-start | bytes 737288 | tf_op jit(solution)/shard_map/ppermute | solution.py:379
  48.2 20.6 %collective-permute-start.11 = (bf16[4,256,384]{2,1,0:T(8,128)(2,1)S(1)}, bf16[4,256,384]{2,1,0:T(8,128)(2,1)S(1)}, u32[]{:S(2)}, u32[]{:S(2)}) collective-permute-start(bf16[4,256,384]{2,1,0:T(8,128)(2,1)S(1)} %pad_maximum_fusion.refs_0_), channel_id=1, source_target_pairs={{0,16},{4,20},{8,24},{12,28},{16,0},{20,4},{24,8},{28,12},{1,17},{... | collective-permute-start | bytes 2359304 | tf_op jit(solution)/shard_map/ppermute | solution.py:379
  56.1 10.2 %collective-permute-start.25 = (bf16[4,80,384]{2,1,0:T(8,128)(2,1)S(1)}, bf16[4,80,384]{2,1,0:T(8,128)(2,1)S(1)}, u32[]{:S(2)}, u32[]{:S(2)}) collective-permute-start(bf16[4,80,384]{2,1,0:T(8,128)(2,1)S(1)} %collective-permute-done.23.refs_14_), channel_id=1, source_target_pairs={{0,1},{1,2},{2,3},{3,0},{4,5},{5,6},{6,7},{7,4},{8,9},{9,10},{10,1... | collective-permute-start | bytes 737288 | tf_op jit(solution)/shard_map/ppermute | solution.py:431
  56.2 10.2 %collective-permute-start.24 = (bf16[4,80,384]{2,1,0:T(8,128)(2,1)S(1)}, bf16[4,80,384]{2,1,0:T(8,128)(2,1)S(1)}, u32[]{:S(2)}, u32[]{:S(2)}) collective-permute-start(bf16[4,80,384]{2,1,0:T(8,128)(2,1)S(1)} %collective-permute-done.23.refs_14_), channel_id=1, source_target_pairs={{0,16},{4,20},{8,24},{12,28},{16,0},{20,4},{24,8},{28,12},{1,17},{... | collective-permute-start | bytes 737288 | tf_op jit(solution)/shard_map/ppermute | solution.py:379
  56.8 11.1 %collective-permute-start.16 = (bf16[4,128,384]{2,1,0:T(8,128)(2,1)S(1)}, bf16[4,128,384]{2,1,0:T(8,128)(2,1)S(1)}, u32[]{:S(2)}, u32[]{:S(2)}) collective-permute-start(bf16[4,128,384]{2,1,0:T(8,128)(2,1)S(1)} %slice.13), channel_id=1, source_target_pairs={{0,4},{4,0},{8,12},{12,8},{16,20},{20,16},{24,28},{28,24},{1,5},{5... | collective-permute-start | bytes 1179656 | tf_op jit(solution)/shard_map/ppermute | solution.py:379
  57.6 11.2 %collective-permute-start.18 = (bf16[4,128,384]{2,1,0:T(8,128)(2,1)S(1)}, bf16[4,128,384]{2,1,0:T(8,128)(2,1)S(1)}, u32[]{:S(2)}, u32[]{:S(2)}) collective-permute-start(bf16[4,128,384]{2,1,0:T(8,128)(2,1)S(1)} %slice.14), channel_id=1, source_target_pairs={{0,8},{4,12},{8,0},{12,4},{16,24},{20,28},{24,16},{28,20},{1,9},{5... | collective-permute-start | bytes 1179656 | tf_op jit(solution)/shard_map/ppermute | solution.py:379
  66.3 4.9 %collective-permute-start.15 = (bf16[4,256,384]{2,1,0:T(8,128)(2,1)S(1)}, bf16[4,256,384]{2,1,0:T(8,128)(2,1)S(1)}, u32[]{:S(2)}, u32[]{:S(2)}) collective-permute-start(bf16[4,256,384]{2,1,0:T(8,128)(2,1)S(1)} %collective-permute-done.14.refs_4_), channel_id=1, source_target_pairs={{0,16},{4,20},{8,24},{12,28},{16,0},{20,4},{24,8},{28,12},{1,17},{... | collective-permute-start | bytes 2359304 | tf_op jit(solution)/shard_map/ppermute | solution.py:379
  66.3 4.9 %collective-permute-start.13 = (bf16[4,256,384]{2,1,0:T(8,128)(2,1)S(1)}, bf16[4,256,384]{2,1,0:T(8,128)(2,1)S(1)}, u32[]{:S(2)}, u32[]{:S(2)}) collective-permute-start(bf16[4,256,384]{2,1,0:T(8,128)(2,1)S(1)} %collective-permute-done.12.refs_2_), channel_id=1, source_target_pairs={{0,16},{4,20},{8,24},{12,28},{16,0},{20,4},{24,8},{28,12},{1,17},{... | collective-permute-start | bytes 2359304 | tf_op jit(solution)/shard_map/ppermute | solution.py:379
  109.5 4.9 %collective-permute-start.27 = (bf16[64,640]{1,0:T(8,128)(2,1)S(1)}, bf16[64,640]{1,0:T(8,128)(2,1)S(1)}, u32[]{:S(2)}, u32[]{:S(2)}) collective-permute-start(bf16[64,640]{1,0:T(8,128)(2,1)S(1)} %get-tuple-element.66), channel_id=1, source_target_pairs={{0,4},{4,0},{8,12},{12,8},{16,20},{20,16},{24,28},{28,24},{1,5},{5... | collective-permute-start | bytes 245768 | tf_op jit(solution)/shard_map/ppermute | solution.py:379
  110.1 5.5 %collective-permute-start.28 = (bf16[64,640]{1,0:T(8,128)(2,1)S(1)}, bf16[64,640]{1,0:T(8,128)(2,1)S(1)}, u32[]{:S(2)}, u32[]{:S(2)}) collective-permute-start(bf16[64,640]{1,0:T(8,128)(2,1)S(1)} %get-tuple-element.67), channel_id=1, source_target_pairs={{0,8},{4,12},{8,0},{12,4},{16,24},{20,28},{24,16},{28,20},{1,9},{5... | collective-permute-start | bytes 245768 | tf_op jit(solution)/shard_map/ppermute | solution.py:379
  111.0 5.4 %collective-permute-start.29 = (bf16[64,640]{1,0:T(8,128)(2,1)S(1)}, bf16[64,640]{1,0:T(8,128)(2,1)S(1)}, u32[]{:S(2)}, u32[]{:S(2)}) collective-permute-start(bf16[64,640]{1,0:T(8,128)(2,1)S(1)} %get-tuple-element.68), channel_id=1, source_target_pairs={{0,12},{4,8},{8,4},{12,0},{16,28},{20,24},{24,20},{28,16},{1,13},{... | collective-permute-start | bytes 245768 | tf_op jit(solution)/shard_map/ppermute | solution.py:379
  114.4 5.5 %collective-permute-start.32 = (bf16[64,640]{1,0:T(8,128)(2,1)S(1)}, bf16[64,640]{1,0:T(8,128)(2,1)S(1)}, u32[]{:S(2)}, u32[]{:S(2)}) collective-permute-start(bf16[64,640]{1,0:T(8,128)(2,1)S(1)} %get-tuple-element.71), channel_id=1, source_target_pairs={{0,28},{4,24},{8,20},{12,16},{16,12},{20,8},{24,4},{28,0},{1,29},{... | collective-permute-start | bytes 245768 | tf_op jit(solution)/shard_map/ppermute | solution.py:379
  (14 other events, 42.9 us)

commit v4 on v2

--- a/solution.py
+++ b/solution.py
@@ -266,7 +266,7 @@
     place = lax.broadcasted_iota(jnp.int32, (block, quarter), 1) + tok * quarter
     mixed = jnp.where(place >= lengths_ref[0] - half, turned, jnp.where(first, lower, given))
     kept = features_ref[:, :half]
-    cut = lower_ref.shape[0]
+    cut = block - lower_ref.shape[0]
     upper_ref[:cut, :half] = kept[:cut]
     upper_ref[:cut, half:] = mixed[:cut].astype(jnp.bfloat16)
     lower_ref[:, :half] = kept[cut:]
@@ -294,11 +294,34 @@
             out_ref[flip] = turned[pl.ds(start, held), :]
 
 
-def join_kernel(own_ref, given_ref, *refs):
+def packed_rows(lower, width):
+    return -(-lower.shape[0] // (width // lower.shape[1]) // 16) * 16
+
+
+def join_kernel(own_ref, given_ref, lower_ref, *refs):
+    _, held, width = own_ref.shape
+    rows, lanes = lower_ref.shape
+    high = packed_rows(lower_ref, width)
     for flip, out_ref in enumerate(refs):
-        held = own_ref.shape[1]
         out_ref[:held] = own_ref[flip]
-        out_ref[held:] = given_ref[flip]
+        out_ref[held:2 * held] = given_ref[flip]
+        if flip:
+            out_ref[2 * held:] = jnp.zeros((high, width), out_ref.dtype)
+            for number, start in enumerate(range(0, rows, high)):
+                size = min(high, rows - start)
+                out_ref[2 * held:2 * held + size, number * lanes:(number + 1) * lanes] = lower_ref[start:start + size]
+
+
+def plane_kernel(lower_ref, *refs):
+    out_ref = refs[-1]
+    rows, lanes = lower_ref.shape
+    out_ref[0] = lower_ref[...]
+    for flip, found in enumerate(refs[:-1]):
+        high = packed_rows(lower_ref, found.shape[1])
+        base = found.shape[0] - high
+        for number, start in enumerate(range(0, rows, high)):
+            size = min(high, rows - start)
+            out_ref[flip + 1, start:start + size] = found[base:base + size, number * lanes:(number + 1) * lanes]
 
 
 def gather_kernel(*refs):
@@ -347,41 +370,63 @@
             scratch_shapes=[pltpu.VMEM((col_width, row_width), jnp.bfloat16)],
             compiler_params=small,
         )(weights[0])
-        joined = pl.pallas_call(
-            join_kernel,
-            out_shape=[jax.ShapeDtypeStruct((toks * columns, row_width), jnp.bfloat16)] * rows,
-            in_specs=[in_vmem] * 2,
-            out_specs=[in_vmem] * rows,
-            compiler_params=small,
-        )(own, swap(other, 1))
-        weight_pieces = [swap(value, 2 * flip) if flip else value for flip, value in enumerate(joined)]
-        places = list(range(rows))
-        cut = block // 2
+        cut = block * 3 // 4
         upper, lower = pl.pallas_call(
             piece_kernel,
             out_shape=[
-                jax.ShapeDtypeStruct((cut + 16, held), jnp.bfloat16), jax.ShapeDtypeStruct((cut, held), jnp.bfloat16)
+                jax.ShapeDtypeStruct((cut + 16, held), jnp.bfloat16),
+                jax.ShapeDtypeStruct((block - cut, held), jnp.bfloat16),
             ],
             in_specs=[scalars, in_vmem, in_vmem, in_vmem],
             out_specs=[in_vmem] * 2,
             scratch_shapes=[pltpu.VMEM((16, held), jnp.float32)],
             compiler_params=small,
         )(lengths, features, given, gains)
+        packed = packed_rows(lower, row_width)
+        joined = pl.pallas_call(
+            join_kernel,
+            out_shape=[
+                jax.ShapeDtypeStruct((toks * columns + (packed if flip else 0), row_width), jnp.bfloat16)
+                for flip in range(rows)
+            ],
+            in_specs=[in_vmem] * 3,
+            out_specs=[in_vmem] * rows,
+            compiler_params=small,
+        )(own, swap(other, 1), lower)
+        line = [upper] + [
+            lax.ppermute(upper, "col", [(i, (i + shift) % cols) for i in range(cols)]) for shift in range(1, cols)
+        ]
+        weight_pieces = [swap(value, 2 * flip) if flip else value for flip, value in enumerate(joined)]
+        places = list(range(rows))
+        line, weight_pieces = lax.optimization_barrier((line, weight_pieces))
+        plane = pl.pallas_call(
+            plane_kernel,
+            out_shape=jax.ShapeDtypeStruct((rows,) + lower.shape, jnp.bfloat16),
+            in_specs=[in_vmem] * rows,
+            out_specs=in_vmem,
+            compiler_params=small,
+        )(lower, *weight_pieces[1:])
         up = [(i, (i + 1) % cols) for i in range(cols)]
-        lines = [[upper], [lower]]
+        value = jnp.stack(line)
+        by_near, by_far = swap(value, 2), swap(value, 4)
+        middle = (cut + 16) // 2
+        crossed = [
+            (0, 0, value), (1, 0, by_near), (2, 0, by_far),
+            (3, 0, swap(by_far[:, :middle], 2)), (3, middle, swap(by_near[:, middle:], 4)),
+        ]
+        rounds = [plane]
         for _ in range(cols - 1):
-            for line in lines:
-                line.append(lax.ppermute(line[-1], "col", up))
-        lines, weight_pieces = lax.optimization_barrier((lines, weight_pieces))
+            rounds.append(lax.ppermute(rounds[-1], "col", up))
         pieces, copies = [], []
-        for first, line in ((0, lines[0]), (cut, lines[1])):
-            value = jnp.stack(line)
-            by_near, by_far = swap(value, 2), swap(value, 4)
-            across = swap(by_near, 4) if first else swap(by_far, 2)
-            for flip, found in enumerate((value, by_near, by_far, across)):
-                for part, arrived in enumerate((found, swap(found, 1))):
-                    pieces.append(arrived)
-                    copies.append([(i, (flip, i), part, held, first, cut) for i in range(cols)])
+        for flip, first, found in crossed:
+            high = min(first + found.shape[1], cut) - first
+            for part, arrived in enumerate((found, swap(found, 1))):
+                pieces.append(arrived)
+                copies.append([(i, (flip, i), part, held, first, high) for i in range(cols)])
+        for back, found in enumerate(rounds):
+            for part, arrived in enumerate((found, swap(found, 1))):
+                pieces.append(arrived)
+                copies.append([(flip, (flip, back), part, held, cut, block - cut) for flip in range(rows)])
         owners = (0, 0, -1, 1, 1, -1)
         small_inputs = []
     else:

time: 117 us -> 109 us (0.932)
  waiting for transfers between devices: 57.5 us -> 47 us
  starting transfers between devices: 24.2 us -> 25.8 us
    ppermute x26 -> x25, waiting for transfers between devices: 39.8 us -> 10.4 us  [swap(): return lax.ppermute(value, ('tok', 'row'), pairs)]
    ppermute x6, waiting for transfers between devices: 17.7 us -> 36.6 us  [the longest x3 21.8 us: body(): rounds.append(lax.ppermute(rounds[-1], 'col', up))]
    ppermute x6, starting transfers between devices: 4.98 us -> 6.4 us  [the longest x3 5.37 us: body(): lax.ppermute(upper, 'col', [(i, (i + shift) % cols) for i in range(cols)])]
    ppermute x26 -> x25, starting transfers between devices: 19.2 us -> 19.4 us  [swap(): return lax.ppermute(value, ('tok', 'row'), pairs)]
  transfers between devices with their start and end apart: 32 -> 31, of which waited for: 14 -> 15; matrix products, arithmetic and copies ran while one was open for 0% -> 0% of each run, Pallas kernels for 1% -> 1%
where the time goes in v4:
time: 109 us
  waiting for transfers between devices  47 us (43%)
  Pallas kernels  34.3 us (31%)
  starting transfers between devices  25.8 us (24%)
  local copies, waits for them, and re-layouts  1.43 us (1%)
    pallas_call x1, Pallas kernels, body(): pl.pallas_call(functools.partial(solve_kernel, owners, models, block, cop...  31.3 us
    ppermute x3, waiting for transfers between devices, body(): rounds.append(lax.ppermute(rounds[-1], 'col', up))  21.8 us
    ppermute x25, starting transfers between devices, swap(): return lax.ppermute(value, ('tok', 'row'), pairs)  19.4 us
    ppermute x3, waiting for transfers between devices, body(): lax.ppermute(upper, 'col', [(i, (i + shift) % cols) for i in range(cols)])  14.8 us
    ppermute x25, waiting for transfers between devices, swap(): return lax.ppermute(value, ('tok', 'row'), pairs)  10.4 us
    ppermute x3, starting transfers between devices, body(): lax.ppermute(upper, 'col', [(i, (i + shift) % cols) for i in range(cols)])  5.37 us
  transfers between devices with their start and end apart: 31, of which 15 were waited for; matrix products, arithmetic and copies ran while one was open for 0% of the time, Pallas kernels for 1%

profile of v4, /device:TPU:0, one launch (start us, length us, event | category | flops | bytes accessed | tf_op | source)
XLA Modules:
  0.0 108.7 jit_solution(9876363708124931206)
XLA Ops:
  0.0 1.3 %copy-done = bf16[1,1280,512]{2,1,0:T(8,128)(2,1)S(1)} copy-done((bf16[1,1280,512]{2,1,0:T(8,128)(2,1)S(1)}, bf16[1,1280,512]{2,1,0:T(8,128)(2,1)}, u32[]{:S(2)}) %copy-start) | copy-done | bytes 1310744
  2.8 1.4 %collective-permute-done.given_ref = bf16[320,128]{1,0:T(8,128)(2,1)S(1)} collective-permute-done((bf16[320,128]{1,0:T(8,128)(2,1)S(1)}, bf16[320,128]{1,0:T(8,128)(2,1)S(1)}, u32[]{:S(2)}, u32[]{:S(2)}) %collective-permute-start) | collective-permute-done | bytes 81952 | tf_op jit(solution)/shard_map/ppermute | solution.py:359
  5.1 2.9 %collective-permute-start.5 = (bf16[160,1280]{1,0:T(8,128)(2,1)S(1)}, bf16[160,1280]{1,0:T(8,128)(2,1)S(1)}, u32[]{:S(2)}, u32[]{:S(2)}) collective-permute-start(bf16[160,1280]{1,0:T(8,128)(2,1)S(1)} %get-tuple-element.34), channel_id=1, source_target_pairs={{0,4},{4,0},{8,12},{12,8},{16,20},{20,16},{24,28},{28,24},{1,5},{5... | collective-permute-start | bytes 1228808 | tf_op jit(solution)/shard_map/ppermute | solution.py:359
  8.0 1.5 %collective-permute-start.6 = (bf16[160,1280]{1,0:T(8,128)(2,1)S(1)}, bf16[160,1280]{1,0:T(8,128)(2,1)S(1)}, u32[]{:S(2)}, u32[]{:S(2)}) collective-permute-start(bf16[160,1280]{1,0:T(8,128)(2,1)S(1)} %get-tuple-element.35), channel_id=1, source_target_pairs={{0,8},{4,12},{8,0},{12,4},{16,24},{20,28},{24,16},{28,20},{1,9},{5... | collective-permute-start | bytes 1228808 | tf_op jit(solution)/shard_map/ppermute | solution.py:359
  9.6 4.1 %collective-permute-start.3 = (bf16[256,384]{1,0:T(8,128)(2,1)S(1)}, bf16[256,384]{1,0:T(8,128)(2,1)S(1)}, u32[]{:S(2)}, u32[]{:S(2)}) collective-permute-start(bf16[256,384]{1,0:T(8,128)(2,1)S(1)} %get-tuple-element.37), channel_id=1, source_target_pairs={{0,3},{1,0},{2,1},{3,2},{4,7},{5,4},{6,5},{7,6},{8,11},{9,8},{10,9... | collective-permute-start | bytes 589832 | tf_op jit(solution)/shard_map/ppermute | solution.py:397
  13.6 5.4 %collective-permute-done.3 = bf16[256,384]{1,0:T(8,128)(2,1)S(1)} collective-permute-done((bf16[256,384]{1,0:T(8,128)(2,1)S(1)}, bf16[256,384]{1,0:T(8,128)(2,1)S(1)}, u32[]{:S(2)}, u32[]{:S(2)}) %collective-permute-start.3) | collective-permute-done | bytes 196640 | tf_op jit(solution)/shard_map/ppermute | solution.py:397
  19.0 1.3 %collective-permute-start.1 = (bf16[256,384]{1,0:T(8,128)(2,1)S(1)}, bf16[256,384]{1,0:T(8,128)(2,1)S(1)}, u32[]{:S(2)}, u32[]{:S(2)}) collective-permute-start(bf16[256,384]{1,0:T(8,128)(2,1)S(1)} %get-tuple-element.37), channel_id=1, source_target_pairs={{0,1},{1,2},{2,3},{3,0},{4,5},{5,6},{6,7},{7,4},{8,9},{9,10},{10,1... | collective-permute-start | bytes 589832 | tf_op jit(solution)/shard_map/ppermute | solution.py:397
  20.3 9.5 %collective-permute-done.2 = bf16[256,384]{1,0:T(8,128)(2,1)S(1)} collective-permute-done((bf16[256,384]{1,0:T(8,128)(2,1)S(1)}, bf16[256,384]{1,0:T(8,128)(2,1)S(1)}, u32[]{:S(2)}, u32[]{:S(2)}) %collective-permute-start.2) | collective-permute-done | bytes 196640 | tf_op jit(solution)/shard_map/ppermute | solution.py:397
  29.9 1.6 %collective-permute-start.11 = (bf16[4,256,384]{2,1,0:T(8,128)(2,1)S(1)}, bf16[4,256,384]{2,1,0:T(8,128)(2,1)S(1)}, u32[]{:S(2)}, u32[]{:S(2)}) collective-permute-start(bf16[4,256,384]{2,1,0:T(8,128)(2,1)S(1)} %pad_maximum_fusion.refs_0_), channel_id=1, source_target_pairs={{0,8},{4,12},{8,0},{12,4},{16,24},{20,28},{24,16},{28,20},{1,9},{5... | collective-permute-start | bytes 2359304 | tf_op jit(solution)/shard_map/ppermute | solution.py:359
  31.5 1.5 %collective-permute-start.9 = (bf16[4,256,384]{2,1,0:T(8,128)(2,1)S(1)}, bf16[4,256,384]{2,1,0:T(8,128)(2,1)S(1)}, u32[]{:S(2)}, u32[]{:S(2)}) collective-permute-start(bf16[4,256,384]{2,1,0:T(8,128)(2,1)S(1)} %pad_maximum_fusion.refs_0_), channel_id=1, source_target_pairs={{0,4},{4,0},{8,12},{12,8},{16,20},{20,16},{24,28},{28,24},{1,5},{5... | collective-permute-start | bytes 2359304 | tf_op jit(solution)/shard_map/ppermute | solution.py:359
  33.9 7.4 %collective-permute-done.18.refs_12_ = bf16[4,80,384]{2,1,0:T(8,128)(2,1)S(1)} collective-permute-done((bf16[4,80,384]{2,1,0:T(8,128)(2,1)S(1)}, bf16[4,80,384]{2,1,0:T(8,128)(2,1)S(1)}, u32[]{:S(2)}, u32[]{:S(2)}) %collective-permute-start.18) | collective-permute-done | bytes 245792 | tf_op jit(solution)/shard_map/ppermute | solution.py:419
  41.9 7.5 %collective-permute-done.20.refs_14_ = bf16[4,80,384]{2,1,0:T(8,128)(2,1)S(1)} collective-permute-done((bf16[4,80,384]{2,1,0:T(8,128)(2,1)S(1)}, bf16[4,80,384]{2,1,0:T(8,128)(2,1)S(1)}, u32[]{:S(2)}, u32[]{:S(2)}) %collective-permute-start.20) | collective-permute-done | bytes 245792 | tf_op jit(solution)/shard_map/ppermute | solution.py:419
  50.0 1.5 %collective-permute-start.13 = (bf16[4,128,384]{2,1,0:T(8,128)(2,1)S(1)}, bf16[4,128,384]{2,1,0:T(8,128)(2,1)S(1)}, u32[]{:S(2)}, u32[]{:S(2)}) collective-permute-start(bf16[4,128,384]{2,1,0:T(8,128)(2,1)S(1)} %slice.13), channel_id=1, source_target_pairs={{0,4},{4,0},{8,12},{12,8},{16,20},{20,16},{24,28},{28,24},{1,5},{5... | collective-permute-start | bytes 1179656 | tf_op jit(solution)/shard_map/ppermute | solution.py:359
  51.5 1.2 %collective-permute-start.15 = (bf16[4,128,384]{2,1,0:T(8,128)(2,1)S(1)}, bf16[4,128,384]{2,1,0:T(8,128)(2,1)S(1)}, u32[]{:S(2)}, u32[]{:S(2)}) collective-permute-start(bf16[4,128,384]{2,1,0:T(8,128)(2,1)S(1)} %slice.14), channel_id=1, source_target_pairs={{0,8},{4,12},{8,0},{12,4},{16,24},{20,28},{24,16},{28,20},{1,9},{5... | collective-permute-start | bytes 1179656 | tf_op jit(solution)/shard_map/ppermute | solution.py:359
  52.7 6.8 %collective-permute-done.22.refs_16_ = bf16[4,80,384]{2,1,0:T(8,128)(2,1)S(1)} collective-permute-done((bf16[4,80,384]{2,1,0:T(8,128)(2,1)S(1)}, bf16[4,80,384]{2,1,0:T(8,128)(2,1)S(1)}, u32[]{:S(2)}, u32[]{:S(2)}) %collective-permute-start.22) | collective-permute-done | bytes 245792 | tf_op jit(solution)/shard_map/ppermute | solution.py:419
  60.0 1.5 %collective-permute-done.13.refs_6_ = bf16[4,128,384]{2,1,0:T(8,128)(2,1)S(1)} collective-permute-done((bf16[4,128,384]{2,1,0:T(8,128)(2,1)S(1)}, bf16[4,128,384]{2,1,0:T(8,128)(2,1)S(1)}, u32[]{:S(2)}, u32[]{:S(2)}) %collective-permute-start.13) | collective-permute-done | bytes 393248 | tf_op jit(solution)/shard_map/ppermute | solution.py:359
  61.6 1.2 %collective-permute-done.15.refs_8_ = bf16[4,128,384]{2,1,0:T(8,128)(2,1)S(1)} collective-permute-done((bf16[4,128,384]{2,1,0:T(8,128)(2,1)S(1)}, bf16[4,128,384]{2,1,0:T(8,128)(2,1)S(1)}, u32[]{:S(2)}, u32[]{:S(2)}) %collective-permute-start.15) | collective-permute-done | bytes 393248 | tf_op jit(solution)/shard_map/ppermute | solution.py:359
  63.3 1.6 %collective-permute-done.23.refs_17_ = bf16[4,80,384]{2,1,0:T(8,128)(2,1)S(1)} collective-permute-done((bf16[4,80,384]{2,1,0:T(8,128)(2,1)S(1)}, bf16[4,80,384]{2,1,0:T(8,128)(2,1)S(1)}, u32[]{:S(2)}, u32[]{:S(2)}) %collective-permute-start.23) | collective-permute-done | bytes 245792 | tf_op jit(solution)/shard_map/ppermute | solution.py:359
  64.9 31.3 %shard_map.50 = (bf16[64,640]{1,0:T(8,128)(2,1)S(1)}, bf16[64,640]{1,0:T(8,128)(2,1)S(1)}, bf16[64,640]{1,0:T(8,128)(2,1)S(1)}, bf16[64,640]{1,0:T(8,128)(2,1)S(...) custom-call(s32[2]{0:T(128)S(1)} %copy-done.2, ...), custom_call_target="tpu_custom_call" | custom-call | tf_op jit(solution)/shard_map/pallas_call | solution.py:461
  97.1 1.2 %collective-permute-start.25 = (bf16[64,640]{1,0:T(8,128)(2,1)S(1)}, bf16[64,640]{1,0:T(8,128)(2,1)S(1)}, u32[]{:S(2)}, u32[]{:S(2)}) collective-permute-start(bf16[64,640]{1,0:T(8,128)(2,1)S(1)} %get-tuple-element.47), channel_id=1, source_target_pairs={{0,8},{4,12},{8,0},{12,4},{16,24},{20,28},{24,16},{28,20},{1,9},{5... | collective-permute-start | bytes 245768 | tf_op jit(solution)/shard_map/ppermute | solution.py:359
  98.3 1.5 %collective-permute-start.26 = (bf16[64,640]{1,0:T(8,128)(2,1)S(1)}, bf16[64,640]{1,0:T(8,128)(2,1)S(1)}, u32[]{:S(2)}, u32[]{:S(2)}) collective-permute-start(bf16[64,640]{1,0:T(8,128)(2,1)S(1)} %get-tuple-element.48), channel_id=1, source_target_pairs={{0,12},{4,8},{8,4},{12,0},{16,28},{20,24},{24,20},{28,16},{1,13},{... | collective-permute-start | bytes 245768 | tf_op jit(solution)/shard_map/ppermute | solution.py:359
  99.8 1.7 %collective-permute-start.28 = (bf16[64,640]{1,0:T(8,128)(2,1)S(1)}, bf16[64,640]{1,0:T(8,128)(2,1)S(1)}, u32[]{:S(2)}, u32[]{:S(2)}) collective-permute-start(bf16[64,640]{1,0:T(8,128)(2,1)S(1)} %get-tuple-element.50), channel_id=1, source_target_pairs={{0,24},{4,28},{8,16},{12,20},{16,8},{20,12},{24,0},{28,4},{1,25},{... | collective-permute-start | bytes 245768 | tf_op jit(solution)/shard_map/ppermute | solution.py:359
  105.1 2.0 %collective-permute-done.29.refs_6_ = bf16[64,640]{1,0:T(8,128)(2,1)S(1)} collective-permute-done((bf16[64,640]{1,0:T(8,128)(2,1)S(1)}, bf16[64,640]{1,0:T(8,128)(2,1)S(1)}, u32[]{:S(2)}, u32[]{:S(2)}) %collective-permute-start.29) | collective-permute-done | bytes 81952 | tf_op jit(solution)/shard_map/ppermute | solution.py:359
  107.1 1.6 %shard_map.51 = f32[640,512]{1,0:T(8,128)} custom-call(bf16[64,640]{1,0:T(8,128)(2,1)S(1)} %get-tuple-element.45.refs_0_, bf16[64,640]{1,0:T(8,128)(2,1)S(1)} %collective-permute-done.24.refs_1_, bf16[64,640]{1,0:T(8,128)(2,1)S(1)} %collective-permute-done.25.refs_2_, bf16[64,640]{1,0:T(8,128)(2,1)S(1)} %collective-permute-done.26.refs_3_, ...), custom_call_target="tpu_custom_call" | custom-call | tf_op jit(solution)/shard_map/pallas_call | solution.py:491
  (56 shorter events, 10.2 us)
Async XLA Ops:
  5.1 24.7 %collective-permute-start.5 = (bf16[160,1280]{1,0:T(8,128)(2,1)S(1)}, bf16[160,1280]{1,0:T(8,128)(2,1)S(1)}, u32[]{:S(2)}, u32[]{:S(2)}) collective-permute-start(bf16[160,1280]{1,0:T(8,128)(2,1)S(1)} %get-tuple-element.34), channel_id=1, source_target_pairs={{0,4},{4,0},{8,12},{12,8},{16,20},{20,16},{24,28},{28,24},{1,5},{5... | collective-permute-start | bytes 1228808 | tf_op jit(solution)/shard_map/ppermute | solution.py:359
  8.0 21.8 %collective-permute-start.6 = (bf16[160,1280]{1,0:T(8,128)(2,1)S(1)}, bf16[160,1280]{1,0:T(8,128)(2,1)S(1)}, u32[]{:S(2)}, u32[]{:S(2)}) collective-permute-start(bf16[160,1280]{1,0:T(8,128)(2,1)S(1)} %get-tuple-element.35), channel_id=1, source_target_pairs={{0,8},{4,12},{8,0},{12,4},{16,24},{20,28},{24,16},{28,20},{1,9},{5... | collective-permute-start | bytes 1228808 | tf_op jit(solution)/shard_map/ppermute | solution.py:359
  9.5 20.2 %collective-permute-start.7 = (bf16[160,1280]{1,0:T(8,128)(2,1)S(1)}, bf16[160,1280]{1,0:T(8,128)(2,1)S(1)}, u32[]{:S(2)}, u32[]{:S(2)}) collective-permute-start(bf16[160,1280]{1,0:T(8,128)(2,1)S(1)} %get-tuple-element.36), channel_id=1, source_target_pairs={{0,12},{4,8},{8,4},{12,0},{16,28},{20,24},{24,20},{28,16},{1,13},{... | collective-permute-start | bytes 1228808 | tf_op jit(solution)/shard_map/ppermute | solution.py:359
  9.6 9.4 %collective-permute-start.3 = (bf16[256,384]{1,0:T(8,128)(2,1)S(1)}, bf16[256,384]{1,0:T(8,128)(2,1)S(1)}, u32[]{:S(2)}, u32[]{:S(2)}) collective-permute-start(bf16[256,384]{1,0:T(8,128)(2,1)S(1)} %get-tuple-element.37), channel_id=1, source_target_pairs={{0,3},{1,0},{2,1},{3,2},{4,7},{5,4},{6,5},{7,6},{8,11},{9,8},{10,9... | collective-permute-start | bytes 589832 | tf_op jit(solution)/shard_map/ppermute | solution.py:397
  13.6 16.2 %collective-permute-start.2 = (bf16[256,384]{1,0:T(8,128)(2,1)S(1)}, bf16[256,384]{1,0:T(8,128)(2,1)S(1)}, u32[]{:S(2)}, u32[]{:S(2)}) collective-permute-start(bf16[256,384]{1,0:T(8,128)(2,1)S(1)} %get-tuple-element.37), channel_id=1, source_target_pairs={{0,2},{1,3},{2,0},{3,1},{4,6},{5,7},{6,4},{7,5},{8,10},{9,11},{10,... | collective-permute-start | bytes 589832 | tf_op jit(solution)/shard_map/ppermute | solution.py:397
  19.0 10.8 %collective-permute-start.1 = (bf16[256,384]{1,0:T(8,128)(2,1)S(1)}, bf16[256,384]{1,0:T(8,128)(2,1)S(1)}, u32[]{:S(2)}, u32[]{:S(2)}) collective-permute-start(bf16[256,384]{1,0:T(8,128)(2,1)S(1)} %get-tuple-element.37), channel_id=1, source_target_pairs={{0,1},{1,2},{2,3},{3,0},{4,5},{5,6},{6,7},{7,4},{8,9},{9,10},{10,1... | collective-permute-start | bytes 589832 | tf_op jit(solution)/shard_map/ppermute | solution.py:397
  29.9 19.4 %collective-permute-start.11 = (bf16[4,256,384]{2,1,0:T(8,128)(2,1)S(1)}, bf16[4,256,384]{2,1,0:T(8,128)(2,1)S(1)}, u32[]{:S(2)}, u32[]{:S(2)}) collective-permute-start(bf16[4,256,384]{2,1,0:T(8,128)(2,1)S(1)} %pad_maximum_fusion.refs_0_), channel_id=1, source_target_pairs={{0,8},{4,12},{8,0},{12,4},{16,24},{20,28},{24,16},{28,20},{1,9},{5... | collective-permute-start | bytes 2359304 | tf_op jit(solution)/shard_map/ppermute | solution.py:359
  31.5 18.3 %collective-permute-start.9 = (bf16[4,256,384]{2,1,0:T(8,128)(2,1)S(1)}, bf16[4,256,384]{2,1,0:T(8,128)(2,1)S(1)}, u32[]{:S(2)}, u32[]{:S(2)}) collective-permute-start(bf16[4,256,384]{2,1,0:T(8,128)(2,1)S(1)} %pad_maximum_fusion.refs_0_), channel_id=1, source_target_pairs={{0,4},{4,0},{8,12},{12,8},{16,20},{20,16},{24,28},{28,24},{1,5},{5... | collective-permute-start | bytes 2359304 | tf_op jit(solution)/shard_map/ppermute | solution.py:359
  33.0 8.3 %collective-permute-start.18 = (bf16[4,80,384]{2,1,0:T(8,128)(2,1)S(1)}, bf16[4,80,384]{2,1,0:T(8,128)(2,1)S(1)}, u32[]{:S(2)}, u32[]{:S(2)}) collective-permute-start(bf16[4,80,384]{2,1,0:T(8,128)(2,1)S(1)} %shard_map.49.refs_10_), channel_id=1, source_target_pairs={{0,1},{1,2},{2,3},{3,0},{4,5},{5,6},{6,7},{7,4},{8,9},{9,10},{10,1... | collective-permute-start | bytes 737288 | tf_op jit(solution)/shard_map/ppermute | solution.py:419
  41.3 8.0 %collective-permute-start.20 = (bf16[4,80,384]{2,1,0:T(8,128)(2,1)S(1)}, bf16[4,80,384]{2,1,0:T(8,128)(2,1)S(1)}, u32[]{:S(2)}, u32[]{:S(2)}) collective-permute-start(bf16[4,80,384]{2,1,0:T(8,128)(2,1)S(1)} %collective-permute-done.18.refs_12_), channel_id=1, source_target_pairs={{0,1},{1,2},{2,3},{3,0},{4,5},{5,6},{6,7},{7,4},{8,9},{9,10},{10,1... | collective-permute-start | bytes 737288 | tf_op jit(solution)/shard_map/ppermute | solution.py:419
  41.3 8.7 %collective-permute-start.17 = (bf16[4,80,384]{2,1,0:T(8,128)(2,1)S(1)}, bf16[4,80,384]{2,1,0:T(8,128)(2,1)S(1)}, u32[]{:S(2)}, u32[]{:S(2)}) collective-permute-start(bf16[4,80,384]{2,1,0:T(8,128)(2,1)S(1)} %shard_map.49.refs_10_), channel_id=1, source_target_pairs={{0,16},{4,20},{8,24},{12,28},{16,0},{20,4},{24,8},{28,12},{1,17},{... | collective-permute-start | bytes 737288 | tf_op jit(solution)/shard_map/ppermute | solution.py:359
  41.4 21.4 %collective-permute-start.8 = (bf16[4,256,384]{2,1,0:T(8,128)(2,1)S(1)}, bf16[4,256,384]{2,1,0:T(8,128)(2,1)S(1)}, u32[]{:S(2)}, u32[]{:S(2)}) collective-permute-start(bf16[4,256,384]{2,1,0:T(8,128)(2,1)S(1)} %pad_maximum_fusion.refs_0_), channel_id=1, source_target_pairs={{0,16},{4,20},{8,24},{12,28},{16,0},{20,4},{24,8},{28,12},{1,17},{... | collective-permute-start | bytes 2359304 | tf_op jit(solution)/shard_map/ppermute | solution.py:359
  49.3 10.2 %collective-permute-start.22 = (bf16[4,80,384]{2,1,0:T(8,128)(2,1)S(1)}, bf16[4,80,384]{2,1,0:T(8,128)(2,1)S(1)}, u32[]{:S(2)}, u32[]{:S(2)}) collective-permute-start(bf16[4,80,384]{2,1,0:T(8,128)(2,1)S(1)} %collective-permute-done.20.refs_14_), channel_id=1, source_target_pairs={{0,1},{1,2},{2,3},{3,0},{4,5},{5,6},{6,7},{7,4},{8,9},{9,10},{10,1... | collective-permute-start | bytes 737288 | tf_op jit(solution)/shard_map/ppermute | solution.py:419
  49.8 9.7 %collective-permute-start.21 = (bf16[4,80,384]{2,1,0:T(8,128)(2,1)S(1)}, bf16[4,80,384]{2,1,0:T(8,128)(2,1)S(1)}, u32[]{:S(2)}, u32[]{:S(2)}) collective-permute-start(bf16[4,80,384]{2,1,0:T(8,128)(2,1)S(1)} %collective-permute-done.20.refs_14_), channel_id=1, source_target_pairs={{0,16},{4,20},{8,24},{12,28},{16,0},{20,4},{24,8},{28,12},{1,17},{... | collective-permute-start | bytes 737288 | tf_op jit(solution)/shard_map/ppermute | solution.py:359
  50.0 11.5 %collective-permute-start.13 = (bf16[4,128,384]{2,1,0:T(8,128)(2,1)S(1)}, bf16[4,128,384]{2,1,0:T(8,128)(2,1)S(1)}, u32[]{:S(2)}, u32[]{:S(2)}) collective-permute-start(bf16[4,128,384]{2,1,0:T(8,128)(2,1)S(1)} %slice.13), channel_id=1, source_target_pairs={{0,4},{4,0},{8,12},{12,8},{16,20},{20,16},{24,28},{28,24},{1,5},{5... | collective-permute-start | bytes 1179656 | tf_op jit(solution)/shard_map/ppermute | solution.py:359
  51.5 11.2 %collective-permute-start.15 = (bf16[4,128,384]{2,1,0:T(8,128)(2,1)S(1)}, bf16[4,128,384]{2,1,0:T(8,128)(2,1)S(1)}, u32[]{:S(2)}, u32[]{:S(2)}) collective-permute-start(bf16[4,128,384]{2,1,0:T(8,128)(2,1)S(1)} %slice.14), channel_id=1, source_target_pairs={{0,8},{4,12},{8,0},{12,4},{16,24},{20,28},{24,16},{28,20},{1,9},{5... | collective-permute-start | bytes 1179656 | tf_op jit(solution)/shard_map/ppermute | solution.py:359
  59.5 5.3 %collective-permute-start.12 = (bf16[4,256,384]{2,1,0:T(8,128)(2,1)S(1)}, bf16[4,256,384]{2,1,0:T(8,128)(2,1)S(1)}, u32[]{:S(2)}, u32[]{:S(2)}) collective-permute-start(bf16[4,256,384]{2,1,0:T(8,128)(2,1)S(1)} %collective-permute-done.11.refs_4_), channel_id=1, source_target_pairs={{0,16},{4,20},{8,24},{12,28},{16,0},{20,4},{24,8},{28,12},{1,17},{... | collective-permute-start | bytes 2359304 | tf_op jit(solution)/shard_map/ppermute | solution.py:359
  59.5 5.3 %collective-permute-start.10 = (bf16[4,256,384]{2,1,0:T(8,128)(2,1)S(1)}, bf16[4,256,384]{2,1,0:T(8,128)(2,1)S(1)}, u32[]{:S(2)}, u32[]{:S(2)}) collective-permute-start(bf16[4,256,384]{2,1,0:T(8,128)(2,1)S(1)} %collective-permute-done.9.refs_2_), channel_id=1, source_target_pairs={{0,16},{4,20},{8,24},{12,28},{16,0},{20,4},{24,8},{28,12},{1,17},{... | collective-permute-start | bytes 2359304 | tf_op jit(solution)/shard_map/ppermute | solution.py:359
  96.2 5.3 %collective-permute-start.24 = (bf16[64,640]{1,0:T(8,128)(2,1)S(1)}, bf16[64,640]{1,0:T(8,128)(2,1)S(1)}, u32[]{:S(2)}, u32[]{:S(2)}) collective-permute-start(bf16[64,640]{1,0:T(8,128)(2,1)S(1)} %get-tuple-element.46), channel_id=1, source_target_pairs={{0,4},{4,0},{8,12},{12,8},{16,20},{20,16},{24,28},{28,24},{1,5},{5... | collective-permute-start | bytes 245768 | tf_op jit(solution)/shard_map/ppermute | solution.py:359
  97.1 5.3 %collective-permute-start.25 = (bf16[64,640]{1,0:T(8,128)(2,1)S(1)}, bf16[64,640]{1,0:T(8,128)(2,1)S(1)}, u32[]{:S(2)}, u32[]{:S(2)}) collective-permute-start(bf16[64,640]{1,0:T(8,128)(2,1)S(1)} %get-tuple-element.47), channel_id=1, source_target_pairs={{0,8},{4,12},{8,0},{12,4},{16,24},{20,28},{24,16},{28,20},{1,9},{5... | collective-permute-start | bytes 245768 | tf_op jit(solution)/shard_map/ppermute | solution.py:359
  98.3 5.7 %collective-permute-start.26 = (bf16[64,640]{1,0:T(8,128)(2,1)S(1)}, bf16[64,640]{1,0:T(8,128)(2,1)S(1)}, u32[]{:S(2)}, u32[]{:S(2)}) collective-permute-start(bf16[64,640]{1,0:T(8,128)(2,1)S(1)} %get-tuple-element.48), channel_id=1, source_target_pairs={{0,12},{4,8},{8,4},{12,0},{16,28},{20,24},{24,20},{28,16},{1,13},{... | collective-permute-start | bytes 245768 | tf_op jit(solution)/shard_map/ppermute | solution.py:359
  99.8 5.3 %collective-permute-start.28 = (bf16[64,640]{1,0:T(8,128)(2,1)S(1)}, bf16[64,640]{1,0:T(8,128)(2,1)S(1)}, u32[]{:S(2)}, u32[]{:S(2)}) collective-permute-start(bf16[64,640]{1,0:T(8,128)(2,1)S(1)} %get-tuple-element.50), channel_id=1, source_target_pairs={{0,24},{4,28},{8,16},{12,20},{16,8},{20,12},{24,0},{28,4},{1,25},{... | collective-permute-start | bytes 245768 | tf_op jit(solution)/shard_map/ppermute | solution.py:359
  101.5 5.6 %collective-permute-start.29 = (bf16[64,640]{1,0:T(8,128)(2,1)S(1)}, bf16[64,640]{1,0:T(8,128)(2,1)S(1)}, u32[]{:S(2)}, u32[]{:S(2)}) collective-permute-start(bf16[64,640]{1,0:T(8,128)(2,1)S(1)} %get-tuple-element.51), channel_id=1, source_target_pairs={{0,28},{4,24},{8,20},{12,16},{16,12},{20,8},{24,4},{28,0},{1,29},{... | collective-permute-start | bytes 245768 | tf_op jit(solution)/shard_map/ppermute | solution.py:359
  102.4 4.7 %collective-permute-start.30 = (bf16[64,640]{1,0:T(8,128)(2,1)S(1)}, bf16[64,640]{1,0:T(8,128)(2,1)S(1)}, u32[]{:S(2)}, u32[]{:S(2)}) collective-permute-start(bf16[64,640]{1,0:T(8,128)(2,1)S(1)} %get-tuple-element.52), channel_id=1, source_target_pairs={{0,16},{4,20},{8,24},{12,28},{16,0},{20,4},{24,8},{28,12},{1,17},{... | collective-permute-start | bytes 245768 | tf_op jit(solution)/shard_map/ppermute | solution.py:359
  (11 other events, 28.7 us)

commit v5 on v4

--- a/solution.py
+++ b/solution.py
@@ -13,7 +13,7 @@
 EPSILON = 1e-06
 
 LANES = 128
-CHUNK = 512
+CHUNK = 1024
 MOST_TOKENS = 1024
 NEAR_FIRST = (0, 2, 4, 6, 3, 5, 7, 1)
 
@@ -77,52 +77,49 @@
     width, slots = tokens.shape
     columns = residual.shape[0]
     blocks = width // block
-    started = []
+    started = [[], [], []]
+
+    def begin(source, target, kind):
+        copy = pltpu.make_async_copy(source, target, sems.at[kind])
+        copy.start()
+        started[kind].append(copy)
+
+    def finish(kind):
+        for copy in started[kind]:
+            copy.wait()
+
     if riding:
         row, col, tok = lax.axis_index("row"), lax.axis_index("col"), lax.axis_index("tok")
         cols = lax.axis_size("col")
-        row_devices = lax.axis_size("row")
+    moves = []
     for piece, parts in zip(pieces, copies):
         for source, entry, part, lanes, first, held in parts:
             if riding:
                 flip, back = entry
                 entry = (row ^ flip) * cols + lax.rem(col - back + cols, cols)
                 part = tok ^ part
-            start = pl.multiple_of(entry * block + first, 16)
-            lane = pl.multiple_of(part * lanes, LANES)
-            copy = pltpu.make_async_copy(
-                piece.at[source, pl.ds(0, held)],
-                tokens.at[pl.ds(start, held), pl.ds(lane, lanes)],
-                sems.at[0],
-            )
-            copy.start()
-            started.append(copy)
-            if piece.shape[1] > held:
-                copy = pltpu.make_async_copy(
-                    piece.at[source, pl.ds(held, 16)],
-                    extras.at[part * blocks + entry],
-                    sems.at[0],
-                )
-                copy.start()
-                started.append(copy)
+            moves.append((piece, source, entry, part, lanes, first, held))
+    for piece, source, entry, part, lanes, first, held in moves:
+        if piece.shape[1] > held:
+            begin(piece.at[source, pl.ds(held, 16)], extras.at[part * blocks + entry], 0)
+    for piece, source, entry, part, lanes, first, held in moves:
+        start = pl.multiple_of(entry * block + first, 16)
+        lane = pl.multiple_of(part * lanes, LANES)
+        begin(piece.at[source, pl.ds(0, held)], tokens.at[pl.ds(start, held), pl.ds(lane, lanes)], 1)
     for piece, place in zip(weight_pieces, places):
-        moves = [(piece, weights)]
         if riding:
             row_width = piece.shape[1]
             lane = pl.multiple_of((row ^ place) * row_width, LANES)
-            moves = [
-                (
+            for part in range(2):
+                high = pl.multiple_of((tok ^ part) * columns, columns)
+                begin(
                     piece.at[pl.ds(part * columns, columns)],
-                    weights.at[pl.ds(pl.multiple_of((tok ^ part) * columns, columns), columns), pl.ds(lane, row_width)],
+                    weights.at[pl.ds(high, columns), pl.ds(lane, row_width)],
+                    2,
                 )
-                for part in range(2)
-            ]
-        for source, target in moves:
-            copy = pltpu.make_async_copy(source, target, sems.at[1])
-            copy.start()
-            started.append(copy)
-    for copy in started:
-        copy.wait()
+        else:
+            begin(piece, weights, 2)
+    finish(0)
 
     if riding:
         every = extras[...].astype(jnp.float32)
@@ -146,6 +143,7 @@
     else:
         squares, live = squares_ref[...], live_ref[...]
     inverse_rms = lax.rsqrt(squares / width + EPSILON) * live
+    finish(1)
 
     def norm_rows(step, carry):
         start = pl.multiple_of(step * LANES, LANES)
@@ -176,6 +174,7 @@
 
     lax.fori_loop(0, width // LANES, norm_rows, 0, unroll=4 if riding else 1)
 
+    finish(2)
     over_features(weights, tokens, values)
     picked = []
     for tile, owner in enumerate(owners):
@@ -370,7 +369,7 @@
             scratch_shapes=[pltpu.VMEM((col_width, row_width), jnp.bfloat16)],
             compiler_params=small,
         )(weights[0])
-        cut = block * 3 // 4
+        cut = block * 7 // 10
         upper, lower = pl.pallas_call(
             piece_kernel,
             out_shape=[
@@ -409,7 +408,7 @@
         up = [(i, (i + 1) % cols) for i in range(cols)]
         value = jnp.stack(line)
         by_near, by_far = swap(value, 2), swap(value, 4)
-        middle = (cut + 16) // 2
+        middle = cut // 2
         crossed = [
             (0, 0, value), (1, 0, by_near), (2, 0, by_far),
             (3, 0, swap(by_far[:, :middle], 2)), (3, middle, swap(by_near[:, middle:], 4)),
@@ -477,7 +476,7 @@
             pltpu.VMEM((2 * columns, slots_held), jnp.bfloat16),
             pltpu.VMEM((models * rows * cols, 16, slots_held // models) if paired else (8, 16, LANES), jnp.bfloat16),
             pltpu.VMEM((width if paired else 8, LANES), jnp.float32),
-            pltpu.SemaphoreType.DMA((2,)),
+            pltpu.SemaphoreType.DMA((3,)),
         ],
         compiler_params=pltpu.CompilerParams(vmem_limit_bytes=width * slots_held * 2 + (18 << 20)),
     )(

time: 109 us -> 107 us (0.982)
  starting transfers between devices: 25.8 us -> 24.1 us
    ppermute x3, waiting for transfers between devices: 21.8 us -> 24.8 us  [body(): rounds.append(lax.ppermute(rounds[-1], 'col', up))]
    ppermute x25, waiting for transfers between devices: 10.4 us -> 8.34 us  [swap(): return lax.ppermute(value, ('tok', 'row'), pairs)]
  transfers between devices with their start and end apart: 31 -> 31, of which waited for: 15 -> 14; matrix products, arithmetic and copies ran while one was open for 0% -> 0% of each run, Pallas kernels for 1% -> 1%
where the time goes in v5:
time: 107 us
  waiting for transfers between devices  47.5 us (44%)
  Pallas kernels  33.7 us (31%)
  starting transfers between devices  24.1 us (23%)
  local copies, waits for them, and re-layouts  1.43 us (1%)
    pallas_call x1, Pallas kernels, body(): pl.pallas_call(functools.partial(solve_kernel, owners, models, block, cop...  30.8 us
    ppermute x3, waiting for transfers between devices, body(): rounds.append(lax.ppermute(rounds[-1], 'col', up))  24.8 us
    ppermute x25, starting transfers between devices, swap(): return lax.ppermute(value, ('tok', 'row'), pairs)  18.4 us
    ppermute x3, waiting for transfers between devices, body(): lax.ppermute(upper, 'col', [(i, (i + shift) % cols) for i in range(cols)])  14.3 us
    ppermute x25, waiting for transfers between devices, swap(): return lax.ppermute(value, ('tok', 'row'), pairs)  8.34 us
    ppermute x3, starting transfers between devices, body(): lax.ppermute(upper, 'col', [(i, (i + shift) % cols) for i in range(cols)])  4.85 us
  transfers between devices with their start and end apart: 31, of which 14 were waited for; matrix products, arithmetic and copies ran while one was open for 0% of the time, Pallas kernels for 1%

profile of v5, /device:TPU:0, one launch (start us, length us, event | category | flops | bytes accessed | tf_op | source)
XLA Modules:
  0.0 107.0 jit_solution(18192764116983461123)
XLA Ops:
  0.0 1.3 %copy-done = bf16[1,1280,512]{2,1,0:T(8,128)(2,1)S(1)} copy-done((bf16[1,1280,512]{2,1,0:T(8,128)(2,1)S(1)}, bf16[1,1280,512]{2,1,0:T(8,128)(2,1)}, u32[]{:S(2)}) %copy-start) | copy-done | bytes 1310744
  2.8 1.4 %collective-permute-done.given_ref = bf16[320,128]{1,0:T(8,128)(2,1)S(1)} collective-permute-done((bf16[320,128]{1,0:T(8,128)(2,1)S(1)}, bf16[320,128]{1,0:T(8,128)(2,1)S(1)}, u32[]{:S(2)}, u32[]{:S(2)}) %collective-permute-start) | collective-permute-done | bytes 81952 | tf_op jit(solution)/shard_map/ppermute | solution.py:358
  5.1 2.9 %collective-permute-start.5 = (bf16[160,1280]{1,0:T(8,128)(2,1)S(1)}, bf16[160,1280]{1,0:T(8,128)(2,1)S(1)}, u32[]{:S(2)}, u32[]{:S(2)}) collective-permute-start(bf16[160,1280]{1,0:T(8,128)(2,1)S(1)} %get-tuple-element.34), channel_id=1, source_target_pairs={{0,4},{4,0},{8,12},{12,8},{16,20},{20,16},{24,28},{28,24},{1,5},{5... | collective-permute-start | bytes 1228808 | tf_op jit(solution)/shard_map/ppermute | solution.py:358
  8.0 1.5 %collective-permute-start.6 = (bf16[160,1280]{1,0:T(8,128)(2,1)S(1)}, bf16[160,1280]{1,0:T(8,128)(2,1)S(1)}, u32[]{:S(2)}, u32[]{:S(2)}) collective-permute-start(bf16[160,1280]{1,0:T(8,128)(2,1)S(1)} %get-tuple-element.35), channel_id=1, source_target_pairs={{0,8},{4,12},{8,0},{12,4},{16,24},{20,28},{24,16},{28,20},{1,9},{5... | collective-permute-start | bytes 1228808 | tf_op jit(solution)/shard_map/ppermute | solution.py:358
  9.6 4.1 %collective-permute-start.3 = (bf16[240,384]{1,0:T(8,128)(2,1)S(1)}, bf16[240,384]{1,0:T(8,128)(2,1)S(1)}, u32[]{:S(2)}, u32[]{:S(2)}) collective-permute-start(bf16[240,384]{1,0:T(8,128)(2,1)S(1)} %get-tuple-element.37), channel_id=1, source_target_pairs={{0,3},{1,0},{2,1},{3,2},{4,7},{5,4},{6,5},{7,6},{8,11},{9,8},{10,9... | collective-permute-start | bytes 552968 | tf_op jit(solution)/shard_map/ppermute | solution.py:396
  13.6 5.1 %collective-permute-done.3 = bf16[240,384]{1,0:T(8,128)(2,1)S(1)} collective-permute-done((bf16[240,384]{1,0:T(8,128)(2,1)S(1)}, bf16[240,384]{1,0:T(8,128)(2,1)S(1)}, u32[]{:S(2)}, u32[]{:S(2)}) %collective-permute-start.3) | collective-permute-done | bytes 184352 | tf_op jit(solution)/shard_map/ppermute | solution.py:396
  18.7 0.8 collective-permute-start.1
  19.5 9.2 %collective-permute-done.2 = bf16[240,384]{1,0:T(8,128)(2,1)S(1)} collective-permute-done((bf16[240,384]{1,0:T(8,128)(2,1)S(1)}, bf16[240,384]{1,0:T(8,128)(2,1)S(1)}, u32[]{:S(2)}, u32[]{:S(2)}) %collective-permute-start.2) | collective-permute-done | bytes 184352 | tf_op jit(solution)/shard_map/ppermute | solution.py:396
  28.9 1.6 %collective-permute-start.9 = (bf16[4,240,384]{2,1,0:T(8,128)(2,1)S(1)}, bf16[4,240,384]{2,1,0:T(8,128)(2,1)S(1)}, u32[]{:S(2)}, u32[]{:S(2)}) collective-permute-start(bf16[4,240,384]{2,1,0:T(8,128)(2,1)S(1)} %pad_maximum_fusion.refs_0_), channel_id=1, source_target_pairs={{0,4},{4,0},{8,12},{12,8},{16,20},{20,16},{24,28},{28,24},{1,5},{5... | collective-permute-start | bytes 2211848 | tf_op jit(solution)/shard_map/ppermute | solution.py:358
  30.4 0.9 collective-permute-start.18
  31.3 1.5 %collective-permute-start.11 = (bf16[4,240,384]{2,1,0:T(8,128)(2,1)S(1)}, bf16[4,240,384]{2,1,0:T(8,128)(2,1)S(1)}, u32[]{:S(2)}, u32[]{:S(2)}) collective-permute-start(bf16[4,240,384]{2,1,0:T(8,128)(2,1)S(1)} %pad_maximum_fusion.refs_0_), channel_id=1, source_target_pairs={{0,8},{4,12},{8,0},{12,4},{16,24},{20,28},{24,16},{28,20},{1,9},{5... | collective-permute-start | bytes 2211848 | tf_op jit(solution)/shard_map/ppermute | solution.py:358
  32.9 7.5 %collective-permute-done.18.refs_12_ = bf16[4,96,384]{2,1,0:T(8,128)(2,1)S(1)} collective-permute-done((bf16[4,96,384]{2,1,0:T(8,128)(2,1)S(1)}, bf16[4,96,384]{2,1,0:T(8,128)(2,1)S(1)}, u32[]{:S(2)}, u32[]{:S(2)}) %collective-permute-start.18) | collective-permute-done | bytes 294944 | tf_op jit(solution)/shard_map/ppermute | solution.py:418
  40.4 8.9 %collective-permute-done.20.refs_14_ = bf16[4,96,384]{2,1,0:T(8,128)(2,1)S(1)} collective-permute-done((bf16[4,96,384]{2,1,0:T(8,128)(2,1)S(1)}, bf16[4,96,384]{2,1,0:T(8,128)(2,1)S(1)}, u32[]{:S(2)}, u32[]{:S(2)}) %collective-permute-start.20) | collective-permute-done | bytes 294944 | tf_op jit(solution)/shard_map/ppermute | solution.py:418
  49.4 1.6 %collective-permute-start.15 = (bf16[4,128,384]{2,1,0:T(8,128)(2,1)S(1)}, bf16[4,128,384]{2,1,0:T(8,128)(2,1)S(1)}, u32[]{:S(2)}, u32[]{:S(2)}) collective-permute-start(bf16[4,128,384]{2,1,0:T(8,128)(2,1)S(1)} %slice.14), channel_id=1, source_target_pairs={{0,8},{4,12},{8,0},{12,4},{16,24},{20,28},{24,16},{28,20},{1,9},{5... | collective-permute-start | bytes 1179656 | tf_op jit(solution)/shard_map/ppermute | solution.py:358
  52.1 8.4 %collective-permute-done.22.refs_16_ = bf16[4,96,384]{2,1,0:T(8,128)(2,1)S(1)} collective-permute-done((bf16[4,96,384]{2,1,0:T(8,128)(2,1)S(1)}, bf16[4,96,384]{2,1,0:T(8,128)(2,1)S(1)}, u32[]{:S(2)}, u32[]{:S(2)}) %collective-permute-start.22) | collective-permute-done | bytes 294944 | tf_op jit(solution)/shard_map/ppermute | solution.py:418
  62.3 1.6 %collective-permute-done.23.refs_17_ = bf16[4,96,384]{2,1,0:T(8,128)(2,1)S(1)} collective-permute-done((bf16[4,96,384]{2,1,0:T(8,128)(2,1)S(1)}, bf16[4,96,384]{2,1,0:T(8,128)(2,1)S(1)}, u32[]{:S(2)}, u32[]{:S(2)}) %collective-permute-start.23) | collective-permute-done | bytes 294944 | tf_op jit(solution)/shard_map/ppermute | solution.py:358
  63.9 30.8 %shard_map.50 = (bf16[64,640]{1,0:T(8,128)(2,1)S(1)}, bf16[64,640]{1,0:T(8,128)(2,1)S(1)}, bf16[64,640]{1,0:T(8,128)(2,1)S(1)}, bf16[64,640]{1,0:T(8,128)(2,1)S(...) custom-call(s32[2]{0:T(128)S(1)} %copy-done.2, ...), custom_call_target="tpu_custom_call" | custom-call | tf_op jit(solution)/shard_map/pallas_call | solution.py:460
  95.3 1.4 %collective-permute-start.25 = (bf16[64,640]{1,0:T(8,128)(2,1)S(1)}, bf16[64,640]{1,0:T(8,128)(2,1)S(1)}, u32[]{:S(2)}, u32[]{:S(2)}) collective-permute-start(bf16[64,640]{1,0:T(8,128)(2,1)S(1)} %get-tuple-element.47), channel_id=1, source_target_pairs={{0,8},{4,12},{8,0},{12,4},{16,24},{20,28},{24,16},{28,20},{1,9},{5... | collective-permute-start | bytes 245768 | tf_op jit(solution)/shard_map/ppermute | solution.py:358
  96.6 1.6 %collective-permute-start.26 = (bf16[64,640]{1,0:T(8,128)(2,1)S(1)}, bf16[64,640]{1,0:T(8,128)(2,1)S(1)}, u32[]{:S(2)}, u32[]{:S(2)}) collective-permute-start(bf16[64,640]{1,0:T(8,128)(2,1)S(1)} %get-tuple-element.48), channel_id=1, source_target_pairs={{0,12},{4,8},{8,4},{12,0},{16,28},{20,24},{24,20},{28,16},{1,13},{... | collective-permute-start | bytes 245768 | tf_op jit(solution)/shard_map/ppermute | solution.py:358
  98.2 1.6 %collective-permute-start.28 = (bf16[64,640]{1,0:T(8,128)(2,1)S(1)}, bf16[64,640]{1,0:T(8,128)(2,1)S(1)}, u32[]{:S(2)}, u32[]{:S(2)}) collective-permute-start(bf16[64,640]{1,0:T(8,128)(2,1)S(1)} %get-tuple-element.50), channel_id=1, source_target_pairs={{0,24},{4,28},{8,16},{12,20},{16,8},{20,12},{24,0},{28,4},{1,25},{... | collective-permute-start | bytes 245768 | tf_op jit(solution)/shard_map/ppermute | solution.py:358
  99.9 0.9 collective-permute-start.29
  102.1 0.9 collective-permute-done.27.refs_4_
  103.7 1.8 %collective-permute-done.29.refs_6_ = bf16[64,640]{1,0:T(8,128)(2,1)S(1)} collective-permute-done((bf16[64,640]{1,0:T(8,128)(2,1)S(1)}, bf16[64,640]{1,0:T(8,128)(2,1)S(1)}, u32[]{:S(2)}, u32[]{:S(2)}) %collective-permute-start.29) | collective-permute-done | bytes 81952 | tf_op jit(solution)/shard_map/ppermute | solution.py:358
  105.5 1.6 %shard_map.51 = f32[640,512]{1,0:T(8,128)} custom-call(bf16[64,640]{1,0:T(8,128)(2,1)S(1)} %get-tuple-element.45.refs_0_, bf16[64,640]{1,0:T(8,128)(2,1)S(1)} %collective-permute-done.24.refs_1_, bf16[64,640]{1,0:T(8,128)(2,1)S(1)} %collective-permute-done.25.refs_2_, bf16[64,640]{1,0:T(8,128)(2,1)S(1)} %collective-permute-done.26.refs_3_, ...), custom_call_target="tpu_custom_call" | custom-call | tf_op jit(solution)/shard_map/pallas_call | solution.py:490
  (56 shorter events, 8.1 us)
Async XLA Ops:
  5.1 23.6 %collective-permute-start.5 = (bf16[160,1280]{1,0:T(8,128)(2,1)S(1)}, bf16[160,1280]{1,0:T(8,128)(2,1)S(1)}, u32[]{:S(2)}, u32[]{:S(2)}) collective-permute-start(bf16[160,1280]{1,0:T(8,128)(2,1)S(1)} %get-tuple-element.34), channel_id=1, source_target_pairs={{0,4},{4,0},{8,12},{12,8},{16,20},{20,16},{24,28},{28,24},{1,5},{5... | collective-permute-start | bytes 1228808 | tf_op jit(solution)/shard_map/ppermute | solution.py:358
  8.0 20.7 %collective-permute-start.6 = (bf16[160,1280]{1,0:T(8,128)(2,1)S(1)}, bf16[160,1280]{1,0:T(8,128)(2,1)S(1)}, u32[]{:S(2)}, u32[]{:S(2)}) collective-permute-start(bf16[160,1280]{1,0:T(8,128)(2,1)S(1)} %get-tuple-element.35), channel_id=1, source_target_pairs={{0,8},{4,12},{8,0},{12,4},{16,24},{20,28},{24,16},{28,20},{1,9},{5... | collective-permute-start | bytes 1228808 | tf_op jit(solution)/shard_map/ppermute | solution.py:358
  9.5 19.2 %collective-permute-start.7 = (bf16[160,1280]{1,0:T(8,128)(2,1)S(1)}, bf16[160,1280]{1,0:T(8,128)(2,1)S(1)}, u32[]{:S(2)}, u32[]{:S(2)}) collective-permute-start(bf16[160,1280]{1,0:T(8,128)(2,1)S(1)} %get-tuple-element.36), channel_id=1, source_target_pairs={{0,12},{4,8},{8,4},{12,0},{16,28},{20,24},{24,20},{28,16},{1,13},{... | collective-permute-start | bytes 1228808 | tf_op jit(solution)/shard_map/ppermute | solution.py:358
  9.6 9.2 %collective-permute-start.3 = (bf16[240,384]{1,0:T(8,128)(2,1)S(1)}, bf16[240,384]{1,0:T(8,128)(2,1)S(1)}, u32[]{:S(2)}, u32[]{:S(2)}) collective-permute-start(bf16[240,384]{1,0:T(8,128)(2,1)S(1)} %get-tuple-element.37), channel_id=1, source_target_pairs={{0,3},{1,0},{2,1},{3,2},{4,7},{5,4},{6,5},{7,6},{8,11},{9,8},{10,9... | collective-permute-start | bytes 552968 | tf_op jit(solution)/shard_map/ppermute | solution.py:396
  13.6 15.1 %collective-permute-start.2 = (bf16[240,384]{1,0:T(8,128)(2,1)S(1)}, bf16[240,384]{1,0:T(8,128)(2,1)S(1)}, u32[]{:S(2)}, u32[]{:S(2)}) collective-permute-start(bf16[240,384]{1,0:T(8,128)(2,1)S(1)} %get-tuple-element.37), channel_id=1, source_target_pairs={{0,2},{1,3},{2,0},{3,1},{4,6},{5,7},{6,4},{7,5},{8,10},{9,11},{10,... | collective-permute-start | bytes 552968 | tf_op jit(solution)/shard_map/ppermute | solution.py:396
  18.7 10.0 %collective-permute-start.1 = (bf16[240,384]{1,0:T(8,128)(2,1)S(1)}, bf16[240,384]{1,0:T(8,128)(2,1)S(1)}, u32[]{:S(2)}, u32[]{:S(2)}) collective-permute-start(bf16[240,384]{1,0:T(8,128)(2,1)S(1)} %get-tuple-element.37), channel_id=1, source_target_pairs={{0,1},{1,2},{2,3},{3,0},{4,5},{5,6},{6,7},{7,4},{8,9},{9,10},{10,1... | collective-permute-start | bytes 552968 | tf_op jit(solution)/shard_map/ppermute | solution.py:396
  28.9 20.5 %collective-permute-start.9 = (bf16[4,240,384]{2,1,0:T(8,128)(2,1)S(1)}, bf16[4,240,384]{2,1,0:T(8,128)(2,1)S(1)}, u32[]{:S(2)}, u32[]{:S(2)}) collective-permute-start(bf16[4,240,384]{2,1,0:T(8,128)(2,1)S(1)} %pad_maximum_fusion.refs_0_), channel_id=1, source_target_pairs={{0,4},{4,0},{8,12},{12,8},{16,20},{20,16},{24,28},{28,24},{1,5},{5... | collective-permute-start | bytes 2211848 | tf_op jit(solution)/shard_map/ppermute | solution.py:358
  30.4 9.9 %collective-permute-start.18 = (bf16[4,96,384]{2,1,0:T(8,128)(2,1)S(1)}, bf16[4,96,384]{2,1,0:T(8,128)(2,1)S(1)}, u32[]{:S(2)}, u32[]{:S(2)}) collective-permute-start(bf16[4,96,384]{2,1,0:T(8,128)(2,1)S(1)} %shard_map.49.refs_10_), channel_id=1, source_target_pairs={{0,1},{1,2},{2,3},{3,0},{4,5},{5,6},{6,7},{7,4},{8,9},{9,10},{10,1... | collective-permute-start | bytes 884744 | tf_op jit(solution)/shard_map/ppermute | solution.py:418
  31.3 19.6 %collective-permute-start.11 = (bf16[4,240,384]{2,1,0:T(8,128)(2,1)S(1)}, bf16[4,240,384]{2,1,0:T(8,128)(2,1)S(1)}, u32[]{:S(2)}, u32[]{:S(2)}) collective-permute-start(bf16[4,240,384]{2,1,0:T(8,128)(2,1)S(1)} %pad_maximum_fusion.refs_0_), channel_id=1, source_target_pairs={{0,8},{4,12},{8,0},{12,4},{16,24},{20,28},{24,16},{28,20},{1,9},{5... | collective-permute-start | bytes 2211848 | tf_op jit(solution)/shard_map/ppermute | solution.py:358
  32.9 18.7 %collective-permute-start.8 = (bf16[4,240,384]{2,1,0:T(8,128)(2,1)S(1)}, bf16[4,240,384]{2,1,0:T(8,128)(2,1)S(1)}, u32[]{:S(2)}, u32[]{:S(2)}) collective-permute-start(bf16[4,240,384]{2,1,0:T(8,128)(2,1)S(1)} %pad_maximum_fusion.refs_0_), channel_id=1, source_target_pairs={{0,16},{4,20},{8,24},{12,28},{16,0},{20,4},{24,8},{28,12},{1,17},{... | collective-permute-start | bytes 2211848 | tf_op jit(solution)/shard_map/ppermute | solution.py:358
  40.4 8.9 %collective-permute-start.20 = (bf16[4,96,384]{2,1,0:T(8,128)(2,1)S(1)}, bf16[4,96,384]{2,1,0:T(8,128)(2,1)S(1)}, u32[]{:S(2)}, u32[]{:S(2)}) collective-permute-start(bf16[4,96,384]{2,1,0:T(8,128)(2,1)S(1)} %collective-permute-done.18.refs_12_), channel_id=1, source_target_pairs={{0,1},{1,2},{2,3},{3,0},{4,5},{5,6},{6,7},{7,4},{8,9},{9,10},{10,1... | collective-permute-start | bytes 884744 | tf_op jit(solution)/shard_map/ppermute | solution.py:418
  40.4 9.0 %collective-permute-start.17 = (bf16[4,96,384]{2,1,0:T(8,128)(2,1)S(1)}, bf16[4,96,384]{2,1,0:T(8,128)(2,1)S(1)}, u32[]{:S(2)}, u32[]{:S(2)}) collective-permute-start(bf16[4,96,384]{2,1,0:T(8,128)(2,1)S(1)} %shard_map.49.refs_10_), channel_id=1, source_target_pairs={{0,16},{4,20},{8,24},{12,28},{16,0},{20,4},{24,8},{28,12},{1,17},{... | collective-permute-start | bytes 884744 | tf_op jit(solution)/shard_map/ppermute | solution.py:358
  49.3 11.2 %collective-permute-start.22 = (bf16[4,96,384]{2,1,0:T(8,128)(2,1)S(1)}, bf16[4,96,384]{2,1,0:T(8,128)(2,1)S(1)}, u32[]{:S(2)}, u32[]{:S(2)}) collective-permute-start(bf16[4,96,384]{2,1,0:T(8,128)(2,1)S(1)} %collective-permute-done.20.refs_14_), channel_id=1, source_target_pairs={{0,1},{1,2},{2,3},{3,0},{4,5},{5,6},{6,7},{7,4},{8,9},{9,10},{10,1... | collective-permute-start | bytes 884744 | tf_op jit(solution)/shard_map/ppermute | solution.py:418
  49.4 11.6 %collective-permute-start.15 = (bf16[4,128,384]{2,1,0:T(8,128)(2,1)S(1)}, bf16[4,128,384]{2,1,0:T(8,128)(2,1)S(1)}, u32[]{:S(2)}, u32[]{:S(2)}) collective-permute-start(bf16[4,128,384]{2,1,0:T(8,128)(2,1)S(1)} %slice.14), channel_id=1, source_target_pairs={{0,8},{4,12},{8,0},{12,4},{16,24},{20,28},{24,16},{28,20},{1,9},{5... | collective-permute-start | bytes 1179656 | tf_op jit(solution)/shard_map/ppermute | solution.py:358
  51.0 12.9 %collective-permute-start.12 = (bf16[4,240,384]{2,1,0:T(8,128)(2,1)S(1)}, bf16[4,240,384]{2,1,0:T(8,128)(2,1)S(1)}, u32[]{:S(2)}, u32[]{:S(2)}) collective-permute-start(bf16[4,240,384]{2,1,0:T(8,128)(2,1)S(1)} %collective-permute-done.11.refs_4_), channel_id=1, source_target_pairs={{0,16},{4,20},{8,24},{12,28},{16,0},{20,4},{24,8},{28,12},{1,17},{... | collective-permute-start | bytes 2211848 | tf_op jit(solution)/shard_map/ppermute | solution.py:358
  51.2 12.7 %collective-permute-start.10 = (bf16[4,240,384]{2,1,0:T(8,128)(2,1)S(1)}, bf16[4,240,384]{2,1,0:T(8,128)(2,1)S(1)}, u32[]{:S(2)}, u32[]{:S(2)}) collective-permute-start(bf16[4,240,384]{2,1,0:T(8,128)(2,1)S(1)} %collective-permute-done.9.refs_2_), channel_id=1, source_target_pairs={{0,16},{4,20},{8,24},{12,28},{16,0},{20,4},{24,8},{28,12},{1,17},{... | collective-permute-start | bytes 2211848 | tf_op jit(solution)/shard_map/ppermute | solution.py:358
  51.5 10.2 %collective-permute-start.13 = (bf16[4,112,384]{2,1,0:T(8,128)(2,1)S(1)}, bf16[4,112,384]{2,1,0:T(8,128)(2,1)S(1)}, u32[]{:S(2)}, u32[]{:S(2)}) collective-permute-start(bf16[4,112,384]{2,1,0:T(8,128)(2,1)S(1)} %slice.13), channel_id=1, source_target_pairs={{0,4},{4,0},{8,12},{12,8},{16,20},{20,16},{24,28},{28,24},{1,5},{5... | collective-permute-start | bytes 1032200 | tf_op jit(solution)/shard_map/ppermute | solution.py:358
  94.7 5.2 %collective-permute-start.24 = (bf16[64,640]{1,0:T(8,128)(2,1)S(1)}, bf16[64,640]{1,0:T(8,128)(2,1)S(1)}, u32[]{:S(2)}, u32[]{:S(2)}) collective-permute-start(bf16[64,640]{1,0:T(8,128)(2,1)S(1)} %get-tuple-element.46), channel_id=1, source_target_pairs={{0,4},{4,0},{8,12},{12,8},{16,20},{20,16},{24,28},{28,24},{1,5},{5... | collective-permute-start | bytes 245768 | tf_op jit(solution)/shard_map/ppermute | solution.py:358
  95.3 5.5 %collective-permute-start.25 = (bf16[64,640]{1,0:T(8,128)(2,1)S(1)}, bf16[64,640]{1,0:T(8,128)(2,1)S(1)}, u32[]{:S(2)}, u32[]{:S(2)}) collective-permute-start(bf16[64,640]{1,0:T(8,128)(2,1)S(1)} %get-tuple-element.47), channel_id=1, source_target_pairs={{0,8},{4,12},{8,0},{12,4},{16,24},{20,28},{24,16},{28,20},{1,9},{5... | collective-permute-start | bytes 245768 | tf_op jit(solution)/shard_map/ppermute | solution.py:358
  96.6 5.4 %collective-permute-start.26 = (bf16[64,640]{1,0:T(8,128)(2,1)S(1)}, bf16[64,640]{1,0:T(8,128)(2,1)S(1)}, u32[]{:S(2)}, u32[]{:S(2)}) collective-permute-start(bf16[64,640]{1,0:T(8,128)(2,1)S(1)} %get-tuple-element.48), channel_id=1, source_target_pairs={{0,12},{4,8},{8,4},{12,0},{16,28},{20,24},{24,20},{28,16},{1,13},{... | collective-permute-start | bytes 245768 | tf_op jit(solution)/shard_map/ppermute | solution.py:358
  98.2 4.7 %collective-permute-start.27 = (bf16[64,640]{1,0:T(8,128)(2,1)S(1)}, bf16[64,640]{1,0:T(8,128)(2,1)S(1)}, u32[]{:S(2)}, u32[]{:S(2)}) collective-permute-start(bf16[64,640]{1,0:T(8,128)(2,1)S(1)} %get-tuple-element.49), channel_id=1, source_target_pairs={{0,20},{4,16},{8,28},{12,24},{16,4},{20,0},{24,12},{28,8},{1,21},{... | collective-permute-start | bytes 245768 | tf_op jit(solution)/shard_map/ppermute | solution.py:358
  98.2 5.4 %collective-permute-start.28 = (bf16[64,640]{1,0:T(8,128)(2,1)S(1)}, bf16[64,640]{1,0:T(8,128)(2,1)S(1)}, u32[]{:S(2)}, u32[]{:S(2)}) collective-permute-start(bf16[64,640]{1,0:T(8,128)(2,1)S(1)} %get-tuple-element.50), channel_id=1, source_target_pairs={{0,24},{4,28},{8,16},{12,20},{16,8},{20,12},{24,0},{28,4},{1,25},{... | collective-permute-start | bytes 245768 | tf_op jit(solution)/shard_map/ppermute | solution.py:358
  99.9 5.6 %collective-permute-start.29 = (bf16[64,640]{1,0:T(8,128)(2,1)S(1)}, bf16[64,640]{1,0:T(8,128)(2,1)S(1)}, u32[]{:S(2)}, u32[]{:S(2)}) collective-permute-start(bf16[64,640]{1,0:T(8,128)(2,1)S(1)} %get-tuple-element.51), channel_id=1, source_target_pairs={{0,28},{4,24},{8,20},{12,16},{16,12},{20,8},{24,4},{28,0},{1,29},{... | collective-permute-start | bytes 245768 | tf_op jit(solution)/shard_map/ppermute | solution.py:358
  100.8 4.7 %collective-permute-start.30 = (bf16[64,640]{1,0:T(8,128)(2,1)S(1)}, bf16[64,640]{1,0:T(8,128)(2,1)S(1)}, u32[]{:S(2)}, u32[]{:S(2)}) collective-permute-start(bf16[64,640]{1,0:T(8,128)(2,1)S(1)} %get-tuple-element.52), channel_id=1, source_target_pairs={{0,16},{4,20},{8,24},{12,28},{16,0},{20,4},{24,8},{28,12},{1,17},{... | collective-permute-start | bytes 245768 | tf_op jit(solution)/shard_map/ppermute | solution.py:358
  (11 other events, 24.6 us)

commit v6 on v5

--- a/solution.py
+++ b/solution.py
@@ -32,6 +32,20 @@
     def some(step, carry):
         lanes = pl.ds(pl.multiple_of(step * CHUNK, CHUNK), CHUNK)
         found[:, lanes] = jnp.dot(left[...], tokens[:, lanes], preferred_element_type=jnp.float32)
+        return carry
+
+    lax.fori_loop(0, slots // CHUNK, some, 0)
+
+
+def add_over_features(left, tokens, part, found):
+    slots = tokens.shape[1]
+    if slots <= MOST_TOKENS:
+        found[...] += jnp.dot(left, tokens[part, :], preferred_element_type=jnp.float32)
+        return
+
+    def some(step, carry):
+        lanes = pl.ds(pl.multiple_of(step * CHUNK, CHUNK), CHUNK)
+        found[:, lanes] += jnp.dot(left, tokens[part, lanes], preferred_element_type=jnp.float32)
         return carry
 
     lax.fori_loop(0, slots // CHUNK, some, 0)
@@ -72,7 +86,7 @@
     pieces = refs[:len(copies)]
     weight_pieces = refs[len(copies):len(copies) + len(places)]
     out_refs = refs[len(copies) + len(places):-14]
-    (tokens, weights, squared, diagonal, residual, direction, merged, terms, values, outputs, seen, extras, gains_held,
+    (tokens, weights, squared, diagonal, residual, direction, merged, kept, values, outputs, seen, extras, gains_held,
      sems) = refs[-14:]
     width, slots = tokens.shape
     columns = residual.shape[0]
@@ -185,52 +199,64 @@
             picked.append(values[owner * columns:(owner + 1) * columns, lanes])
     outputs[...] = jnp.concatenate(picked, axis=1).astype(jnp.bfloat16)
 
-    norm_now = jnp.zeros((columns, 1), jnp.float32)
+    nothing = jnp.zeros((columns, 1), jnp.float32)
+    both = values.at[:2 * columns]
+
+    def total(value):
+        return jnp.sum(value, axis=1, keepdims=True)
+
+    norm_now, weighted = nothing, nothing
+    both[...] = jnp.zeros(both.shape, jnp.float32)
     for start in range(0, width, CHUNK):
         part = slice(start, start + CHUNK)
-        weighted = jnp.zeros((columns, CHUNK), jnp.float32)
+        diagonal_part = jnp.zeros((columns, CHUNK), jnp.float32)
         for model in range(models):
             rows = weights[model * columns:(model + 1) * columns, part].astype(jnp.float32)
-            weighted = weighted + squared[model:model + 1, part] * rows
-        right = MIXING * over_tokens(outputs, tokens, part) + (1.0 - MIXING) * weighted
+            diagonal_part = diagonal_part + squared[model:model + 1, part] * rows
+        right = MIXING * over_tokens(outputs, tokens, part) + (1.0 - MIXING) * diagonal_part
         residual[:, part] = right
         direction[:, part] = jnp.zeros_like(right)
         merged[:, part] = jnp.zeros_like(right)
-        norm_now = norm_now + jnp.sum(right * right, axis=1, keepdims=True)
-
-    def step_of(scale, norm_now):
-        weighted = jnp.zeros((columns, 1), jnp.float32)
+        norm_now = norm_now + total(right * right)
+        weighted = weighted + total(diagonal[:, part] * right * right)
+        add_over_features(two_terms(right), tokens, part, both)
+    kept[...] = both[:columns] + both[columns:]
+
+    def step_of(norm_now, weighted):
+        curvature = MIXING * total(kept[...] * kept[...]) + (1.0 - MIXING) * weighted
+        return norm_now / curvature
+
+    def iterate(_, carry):
+        scale, norm_now, weighted = carry
+        step_size = step_of(norm_now, weighted)
+        seen[...] = two_terms(kept[...])
+        both[...] = jnp.zeros(both.shape, jnp.float32)
+        norm_next, by_residual, by_both = nothing, nothing, nothing
         for start in range(0, width, CHUNK):
             part = slice(start, start + CHUNK)
-            value = residual[:, part] + scale * direction[:, part]
-            direction[:, part] = value
-            terms[:, part] = two_terms(value)
-            weighted = weighted + jnp.sum(diagonal[:, part] * value * value, axis=1, keepdims=True)
-        both = values.at[:2 * columns]
-        over_features(terms, tokens, both)
-        both = both[:columns] + both[columns:]
-        seen[...] = two_terms(both)
-        curvature = MIXING * jnp.sum(both * both, axis=1, keepdims=True) + (1.0 - MIXING) * weighted
-        return norm_now / curvature
-
-    def iterate(_, carry):
-        scale, norm_now = carry
-        step_size = step_of(scale, norm_now)
-        norm_next = jnp.zeros((columns, 1), jnp.float32)
-        for start in range(0, width, CHUNK):
-            part = slice(start, start + CHUNK)
-            both = over_tokens(seen, tokens, part)
-            along = direction[:, part]
-            image = MIXING * (both[:columns] + both[columns:]) + (1.0 - MIXING) * diagonal[:, part] * along
+            product = over_tokens(seen, tokens, part)
+            along = residual[:, part] + scale * direction[:, part]
+            direction[:, part] = along
+            image = MIXING * (product[:columns] + product[columns:]) + (1.0 - MIXING) * diagonal[:, part] * along
             merged[:, part] = merged[:, part] + step_size * along
             value = residual[:, part] - step_size * image
             residual[:, part] = value
-            norm_next = norm_next + jnp.sum(value * value, axis=1, keepdims=True)
-        return norm_next / norm_now, norm_next
-
-    scale, norm_now = lax.fori_loop(0, ITERS - 1, iterate, (jnp.zeros((columns, 1), jnp.float32), norm_now))
-    step_size = step_of(scale, norm_now)
-    merged[...] = merged[...] + step_size * direction[...]
+            norm_next = norm_next + total(value * value)
+            scaled = diagonal[:, part] * value
+            by_residual = by_residual + total(scaled * value)
+            by_both = by_both + total(scaled * along)
+            add_over_features(two_terms(value), tokens, part, both)
+        scale = norm_next / norm_now
+        kept[...] = both[:columns] + both[columns:] + scale * kept[...]
+        weighted = by_residual + 2.0 * scale * by_both + scale * scale * weighted
+        return scale, norm_next, weighted
+
+    scale, norm_now, weighted = lax.fori_loop(0, ITERS - 1, iterate, (nothing, norm_now, weighted))
+    step_size = step_of(norm_now, weighted)
+    for start in range(0, width, CHUNK):
+        part = slice(start, start + CHUNK)
+        along = residual[:, part] + scale * direction[:, part]
+        merged[:, part] = merged[:, part] + step_size * along
     for number, out_ref in enumerate(out_refs):
         sub_rows = out_ref.shape[1]
         if len(out_refs) > 1:
@@ -413,9 +439,12 @@
             (0, 0, value), (1, 0, by_near), (2, 0, by_far),
             (3, 0, swap(by_far[:, :middle], 2)), (3, middle, swap(by_near[:, middle:], 4)),
         ]
+        middle = plane.shape[1] // 2
         rounds = [plane]
+        halves = [plane[:, :middle], plane[:, middle:]]
         for _ in range(cols - 1):
-            rounds.append(lax.ppermute(rounds[-1], "col", up))
+            halves = [lax.ppermute(value, "col", up) for value in halves]
+            rounds.append(jnp.concatenate(halves, axis=1))
         pieces, copies = [], []
         for flip, first, found in crossed:
             high = min(first + found.shape[1], cut) - first
@@ -470,7 +499,7 @@
             pltpu.VMEM((columns, width), jnp.float32),
             pltpu.VMEM((columns, width), jnp.float32),
             pltpu.VMEM((columns, width), jnp.float32),
-            pltpu.VMEM((2 * columns, width), jnp.bfloat16),
+            pltpu.VMEM((columns, slots_held), jnp.float32),
             pltpu.VMEM((max(models, 2) * columns, slots_held), jnp.float32),
             pltpu.VMEM((columns, slots_held), jnp.bfloat16),
             pltpu.VMEM((2 * columns, slots_held), jnp.bfloat16),

time: 107 us -> 114 us (1.065)
  starting transfers between devices: 24.1 us -> 28 us
  waiting for transfers between devices: 47.5 us -> 49.9 us
    ppermute x25, waiting for transfers between devices: 8.34 us -> 16.9 us  [swap(): return lax.ppermute(value, ('tok', 'row'), pairs)]
    ppermute x3 -> x6, waiting for transfers between devices: 24.8 us -> 18.8 us  [body(): halves = [lax.ppermute(value, 'col', up) for value in halves]]
    ppermute x3 -> x6, starting transfers between devices: 0.89 us -> 3.89 us  [body(): halves = [lax.ppermute(value, 'col', up) for value in halves]]
  transfers between devices with their start and end apart: 31 -> 34, of which waited for: 14 -> 17; matrix products, arithmetic and copies ran while one was open for 0% -> 0% of each run, Pallas kernels for 1% -> 1%
where the time goes in v6:
time: 114 us
  waiting for transfers between devices  49.9 us (44%)
  Pallas kernels  34.2 us (30%)
  starting transfers between devices  28 us (25%)
  local copies, waits for them, and re-layouts  1.58 us (1%)
    pallas_call x1, Pallas kernels, body(): pl.pallas_call(functools.partial(solve_kernel, owners, models, block, cop...  31.3 us
    ppermute x25, starting transfers between devices, swap(): return lax.ppermute(value, ('tok', 'row'), pairs)  19.2 us
    ppermute x6, waiting for transfers between devices, body(): halves = [lax.ppermute(value, 'col', up) for value in halves]  18.8 us
    ppermute x25, waiting for transfers between devices, swap(): return lax.ppermute(value, ('tok', 'row'), pairs)  16.9 us
    ppermute x3, waiting for transfers between devices, body(): lax.ppermute(upper, 'col', [(i, (i + shift) % cols) for i in range(cols)])  14.3 us
    ppermute x3, starting transfers between devices, body(): lax.ppermute(upper, 'col', [(i, (i + shift) % cols) for i in range(cols)])  4.85 us
    ppermute x6, starting transfers between devices, body(): halves = [lax.ppermute(value, 'col', up) for value in halves]  3.89 us
  transfers between devices with their start and end apart: 34, of which 17 were waited for; matrix products, arithmetic and copies ran while one was open for 0% of the time, Pallas kernels for 1%

profile of v6, /device:TPU:0, one launch (start us, length us, event | category | flops | bytes accessed | tf_op | source)
XLA Modules:
  0.0 114.0 jit_solution(4941403292107197604)
XLA Ops:
  5.1 2.9 %collective-permute-start.5 = (bf16[160,1280]{1,0:T(8,128)(2,1)S(1)}, bf16[160,1280]{1,0:T(8,128)(2,1)S(1)}, u32[]{:S(2)}, u32[]{:S(2)}) collective-permute-start(bf16[160,1280]{1,0:T(8,128)(2,1)S(1)} %get-tuple-element.34), channel_id=1, source_target_pairs={{0,4},{4,0},{8,12},{12,8},{16,20},{20,16},{24,28},{28,24},{1,5},{5... | collective-permute-start | bytes 1228808 | tf_op jit(solution)/shard_map/ppermute | solution.py:384
  8.0 1.5 %collective-permute-start.6 = (bf16[160,1280]{1,0:T(8,128)(2,1)S(1)}, bf16[160,1280]{1,0:T(8,128)(2,1)S(1)}, u32[]{:S(2)}, u32[]{:S(2)}) collective-permute-start(bf16[160,1280]{1,0:T(8,128)(2,1)S(1)} %get-tuple-element.35), channel_id=1, source_target_pairs={{0,8},{4,12},{8,0},{12,4},{16,24},{20,28},{24,16},{28,20},{1,9},{5... | collective-permute-start | bytes 1228808 | tf_op jit(solution)/shard_map/ppermute | solution.py:384
  9.6 4.1 %collective-permute-start.3 = (bf16[240,384]{1,0:T(8,128)(2,1)S(1)}, bf16[240,384]{1,0:T(8,128)(2,1)S(1)}, u32[]{:S(2)}, u32[]{:S(2)}) collective-permute-start(bf16[240,384]{1,0:T(8,128)(2,1)S(1)} %get-tuple-element.37), channel_id=1, source_target_pairs={{0,3},{1,0},{2,1},{3,2},{4,7},{5,4},{6,5},{7,6},{8,11},{9,8},{10,9... | collective-permute-start | bytes 552968 | tf_op jit(solution)/shard_map/ppermute | solution.py:422
  13.6 5.1 %collective-permute-done.3 = bf16[240,384]{1,0:T(8,128)(2,1)S(1)} collective-permute-done((bf16[240,384]{1,0:T(8,128)(2,1)S(1)}, bf16[240,384]{1,0:T(8,128)(2,1)S(1)}, u32[]{:S(2)}, u32[]{:S(2)}) %collective-permute-start.3) | collective-permute-done | bytes 184352 | tf_op jit(solution)/shard_map/ppermute | solution.py:422
  19.5 9.2 %collective-permute-done.2 = bf16[240,384]{1,0:T(8,128)(2,1)S(1)} collective-permute-done((bf16[240,384]{1,0:T(8,128)(2,1)S(1)}, bf16[240,384]{1,0:T(8,128)(2,1)S(1)}, u32[]{:S(2)}, u32[]{:S(2)}) %collective-permute-start.2) | collective-permute-done | bytes 184352 | tf_op jit(solution)/shard_map/ppermute | solution.py:422
  29.8 1.5 %collective-permute-start.9 = (bf16[4,240,384]{2,1,0:T(8,128)(2,1)S(1)}, bf16[4,240,384]{2,1,0:T(8,128)(2,1)S(1)}, u32[]{:S(2)}, u32[]{:S(2)}) collective-permute-start(bf16[4,240,384]{2,1,0:T(8,128)(2,1)S(1)} %pad_maximum_fusion.refs_0_), channel_id=1, source_target_pairs={{0,4},{4,0},{8,12},{12,8},{16,20},{20,16},{24,28},{28,24},{1,5},{5... | collective-permute-start | bytes 2211848 | tf_op jit(solution)/shard_map/ppermute | solution.py:384
  31.4 2.5 %collective-permute-start.19 = (bf16[4,48,384]{2,1,0:T(8,128)(2,1)S(1)}, bf16[4,48,384]{2,1,0:T(8,128)(2,1)S(1)}, u32[]{:S(2)}, u32[]{:S(2)}) collective-permute-start(bf16[4,48,384]{2,1,0:T(8,128)(2,1)S(1)} %get-tuple-element.53), channel_id=1, source_target_pairs={{0,1},{1,2},{2,3},{3,0},{4,5},{5,6},{6,7},{7,4},{8,9},{9,10},{10,1... | collective-permute-start | bytes 442376 | tf_op jit(solution)/shard_map/ppermute | solution.py:446
  33.9 1.5 %collective-permute-start.11 = (bf16[4,240,384]{2,1,0:T(8,128)(2,1)S(1)}, bf16[4,240,384]{2,1,0:T(8,128)(2,1)S(1)}, u32[]{:S(2)}, u32[]{:S(2)}) collective-permute-start(bf16[4,240,384]{2,1,0:T(8,128)(2,1)S(1)} %pad_maximum_fusion.refs_0_), channel_id=1, source_target_pairs={{0,8},{4,12},{8,0},{12,4},{16,24},{20,28},{24,16},{28,20},{1,9},{5... | collective-permute-start | bytes 2211848 | tf_op jit(solution)/shard_map/ppermute | solution.py:384
  35.4 1.9 %collective-permute-done.18 = bf16[4,48,384]{2,1,0:T(8,128)(2,1)S(1)} collective-permute-done((bf16[4,48,384]{2,1,0:T(8,128)(2,1)S(1)}, bf16[4,48,384]{2,1,0:T(8,128)(2,1)S(1)}, u32[]{:S(2)}, u32[]{:S(2)}) %collective-permute-start.18) | collective-permute-done | bytes 147488 | tf_op jit(solution)/shard_map/ppermute | solution.py:446
  37.3 1.7 %collective-permute-done.19 = bf16[4,48,384]{2,1,0:T(8,128)(2,1)S(1)} collective-permute-done((bf16[4,48,384]{2,1,0:T(8,128)(2,1)S(1)}, bf16[4,48,384]{2,1,0:T(8,128)(2,1)S(1)}, u32[]{:S(2)}, u32[]{:S(2)}) %collective-permute-start.19) | collective-permute-done | bytes 147488 | tf_op jit(solution)/shard_map/ppermute | solution.py:446
  39.5 5.7 %collective-permute-done.21 = bf16[4,48,384]{2,1,0:T(8,128)(2,1)S(1)} collective-permute-done((bf16[4,48,384]{2,1,0:T(8,128)(2,1)S(1)}, bf16[4,48,384]{2,1,0:T(8,128)(2,1)S(1)}, u32[]{:S(2)}, u32[]{:S(2)}) %collective-permute-start.21) | collective-permute-done | bytes 147488 | tf_op jit(solution)/shard_map/ppermute | solution.py:446
  45.3 2.5 %collective-permute-done.22 = bf16[4,48,384]{2,1,0:T(8,128)(2,1)S(1)} collective-permute-done((bf16[4,48,384]{2,1,0:T(8,128)(2,1)S(1)}, bf16[4,48,384]{2,1,0:T(8,128)(2,1)S(1)}, u32[]{:S(2)}, u32[]{:S(2)}) %collective-permute-start.22) | collective-permute-done | bytes 147488 | tf_op jit(solution)/shard_map/ppermute | solution.py:446
  47.9 4.6 %collective-permute-done.24 = bf16[4,48,384]{2,1,0:T(8,128)(2,1)S(1)} collective-permute-done((bf16[4,48,384]{2,1,0:T(8,128)(2,1)S(1)}, bf16[4,48,384]{2,1,0:T(8,128)(2,1)S(1)}, u32[]{:S(2)}, u32[]{:S(2)}) %collective-permute-start.24) | collective-permute-done | bytes 147488 | tf_op jit(solution)/shard_map/ppermute | solution.py:446
  52.5 2.3 %collective-permute-done.25 = bf16[4,48,384]{2,1,0:T(8,128)(2,1)S(1)} collective-permute-done((bf16[4,48,384]{2,1,0:T(8,128)(2,1)S(1)}, bf16[4,48,384]{2,1,0:T(8,128)(2,1)S(1)}, u32[]{:S(2)}, u32[]{:S(2)}) %collective-permute-start.25) | collective-permute-done | bytes 147488 | tf_op jit(solution)/shard_map/ppermute | solution.py:446
  55.4 2.2 %collective-permute-start.15 = (bf16[4,128,384]{2,1,0:T(8,128)(2,1)S(1)}, bf16[4,128,384]{2,1,0:T(8,128)(2,1)S(1)}, u32[]{:S(2)}, u32[]{:S(2)}) collective-permute-start(bf16[4,128,384]{2,1,0:T(8,128)(2,1)S(1)} %slice.22), channel_id=1, source_target_pairs={{0,8},{4,12},{8,0},{12,4},{16,24},{20,28},{24,16},{28,20},{1,9},{5... | collective-permute-start | bytes 1179656 | tf_op jit(solution)/shard_map/ppermute | solution.py:384
  58.3 1.4 %collective-permute-start.13 = (bf16[4,112,384]{2,1,0:T(8,128)(2,1)S(1)}, bf16[4,112,384]{2,1,0:T(8,128)(2,1)S(1)}, u32[]{:S(2)}, u32[]{:S(2)}) collective-permute-start(bf16[4,112,384]{2,1,0:T(8,128)(2,1)S(1)} %slice.21), channel_id=1, source_target_pairs={{0,4},{4,0},{8,12},{12,8},{16,20},{20,16},{24,28},{28,24},{1,5},{5... | collective-permute-start | bytes 1032200 | tf_op jit(solution)/shard_map/ppermute | solution.py:384
  59.6 7.3 %collective-permute-done.15.refs_8_ = bf16[4,128,384]{2,1,0:T(8,128)(2,1)S(1)} collective-permute-done((bf16[4,128,384]{2,1,0:T(8,128)(2,1)S(1)}, bf16[4,128,384]{2,1,0:T(8,128)(2,1)S(1)}, u32[]{:S(2)}, u32[]{:S(2)}) %collective-permute-start.15) | collective-permute-done | bytes 393248 | tf_op jit(solution)/shard_map/ppermute | solution.py:384
  66.9 1.8 %collective-permute-done.13.refs_6_ = bf16[4,112,384]{2,1,0:T(8,128)(2,1)S(1)} collective-permute-done((bf16[4,112,384]{2,1,0:T(8,128)(2,1)S(1)}, bf16[4,112,384]{2,1,0:T(8,128)(2,1)S(1)}, u32[]{:S(2)}, u32[]{:S(2)}) %collective-permute-start.13) | collective-permute-done | bytes 344096 | tf_op jit(solution)/shard_map/ppermute | solution.py:384
  68.7 1.6 %collective-permute-done.14.refs_7_ = bf16[4,112,384]{2,1,0:T(8,128)(2,1)S(1)} collective-permute-done((bf16[4,112,384]{2,1,0:T(8,128)(2,1)S(1)}, bf16[4,112,384]{2,1,0:T(8,128)(2,1)S(1)}, u32[]{:S(2)}, u32[]{:S(2)}) %collective-permute-start.14) | collective-permute-done | bytes 344096 | tf_op jit(solution)/shard_map/ppermute | solution.py:384
  70.4 31.3 %shard_map.50 = (bf16[64,640]{1,0:T(8,128)(2,1)S(1)}, bf16[64,640]{1,0:T(8,128)(2,1)S(1)}, bf16[64,640]{1,0:T(8,128)(2,1)S(1)}, bf16[64,640]{1,0:T(8,128)(2,1)S(...) custom-call(s32[2]{0:T(128)S(1)} %copy-done.2, ...), custom_call_target="tpu_custom_call" | custom-call | tf_op jit(solution)/shard_map/pallas_call | solution.py:489
  103.6 1.7 %collective-permute-start.29 = (bf16[64,640]{1,0:T(8,128)(2,1)S(1)}, bf16[64,640]{1,0:T(8,128)(2,1)S(1)}, u32[]{:S(2)}, u32[]{:S(2)}) collective-permute-start(bf16[64,640]{1,0:T(8,128)(2,1)S(1)} %get-tuple-element.48), channel_id=1, source_target_pairs={{0,12},{4,8},{8,4},{12,0},{16,28},{20,24},{24,20},{28,16},{1,13},{... | collective-permute-start | bytes 245768 | tf_op jit(solution)/shard_map/ppermute | solution.py:384
  107.8 1.4 %collective-permute-done.28.refs_2_ = bf16[64,640]{1,0:T(8,128)(2,1)S(1)} collective-permute-done((bf16[64,640]{1,0:T(8,128)(2,1)S(1)}, bf16[64,640]{1,0:T(8,128)(2,1)S(1)}, u32[]{:S(2)}, u32[]{:S(2)}) %collective-permute-start.28) | collective-permute-done | bytes 81952 | tf_op jit(solution)/shard_map/ppermute | solution.py:384
  110.4 2.1 %collective-permute-done.32.refs_6_ = bf16[64,640]{1,0:T(8,128)(2,1)S(1)} collective-permute-done((bf16[64,640]{1,0:T(8,128)(2,1)S(1)}, bf16[64,640]{1,0:T(8,128)(2,1)S(1)}, u32[]{:S(2)}, u32[]{:S(2)}) %collective-permute-start.32) | collective-permute-done | bytes 81952 | tf_op jit(solution)/shard_map/ppermute | solution.py:384
  112.5 1.6 %shard_map.51 = f32[640,512]{1,0:T(8,128)} custom-call(bf16[64,640]{1,0:T(8,128)(2,1)S(1)} %get-tuple-element.45.refs_0_, bf16[64,640]{1,0:T(8,128)(2,1)S(1)} %collective-permute-done.27.refs_1_, bf16[64,640]{1,0:T(8,128)(2,1)S(1)} %collective-permute-done.28.refs_2_, bf16[64,640]{1,0:T(8,128)(2,1)S(1)} %collective-permute-done.29.refs_3_, ...), custom_call_target="tpu_custom_call" | custom-call | tf_op jit(solution)/shard_map/pallas_call | solution.py:519
  (69 shorter events, 14.5 us)
Async XLA Ops:
  5.1 23.6 %collective-permute-start.5 = (bf16[160,1280]{1,0:T(8,128)(2,1)S(1)}, bf16[160,1280]{1,0:T(8,128)(2,1)S(1)}, u32[]{:S(2)}, u32[]{:S(2)}) collective-permute-start(bf16[160,1280]{1,0:T(8,128)(2,1)S(1)} %get-tuple-element.34), channel_id=1, source_target_pairs={{0,4},{4,0},{8,12},{12,8},{16,20},{20,16},{24,28},{28,24},{1,5},{5... | collective-permute-start | bytes 1228808 | tf_op jit(solution)/shard_map/ppermute | solution.py:384
  8.0 20.7 %collective-permute-start.6 = (bf16[160,1280]{1,0:T(8,128)(2,1)S(1)}, bf16[160,1280]{1,0:T(8,128)(2,1)S(1)}, u32[]{:S(2)}, u32[]{:S(2)}) collective-permute-start(bf16[160,1280]{1,0:T(8,128)(2,1)S(1)} %get-tuple-element.35), channel_id=1, source_target_pairs={{0,8},{4,12},{8,0},{12,4},{16,24},{20,28},{24,16},{28,20},{1,9},{5... | collective-permute-start | bytes 1228808 | tf_op jit(solution)/shard_map/ppermute | solution.py:384
  9.5 19.2 %collective-permute-start.7 = (bf16[160,1280]{1,0:T(8,128)(2,1)S(1)}, bf16[160,1280]{1,0:T(8,128)(2,1)S(1)}, u32[]{:S(2)}, u32[]{:S(2)}) collective-permute-start(bf16[160,1280]{1,0:T(8,128)(2,1)S(1)} %get-tuple-element.36), channel_id=1, source_target_pairs={{0,12},{4,8},{8,4},{12,0},{16,28},{20,24},{24,20},{28,16},{1,13},{... | collective-permute-start | bytes 1228808 | tf_op jit(solution)/shard_map/ppermute | solution.py:384
  9.6 9.2 %collective-permute-start.3 = (bf16[240,384]{1,0:T(8,128)(2,1)S(1)}, bf16[240,384]{1,0:T(8,128)(2,1)S(1)}, u32[]{:S(2)}, u32[]{:S(2)}) collective-permute-start(bf16[240,384]{1,0:T(8,128)(2,1)S(1)} %get-tuple-element.37), channel_id=1, source_target_pairs={{0,3},{1,0},{2,1},{3,2},{4,7},{5,4},{6,5},{7,6},{8,11},{9,8},{10,9... | collective-permute-start | bytes 552968 | tf_op jit(solution)/shard_map/ppermute | solution.py:422
  13.6 15.1 %collective-permute-start.2 = (bf16[240,384]{1,0:T(8,128)(2,1)S(1)}, bf16[240,384]{1,0:T(8,128)(2,1)S(1)}, u32[]{:S(2)}, u32[]{:S(2)}) collective-permute-start(bf16[240,384]{1,0:T(8,128)(2,1)S(1)} %get-tuple-element.37), channel_id=1, source_target_pairs={{0,2},{1,3},{2,0},{3,1},{4,6},{5,7},{6,4},{7,5},{8,10},{9,11},{10,... | collective-permute-start | bytes 552968 | tf_op jit(solution)/shard_map/ppermute | solution.py:422
  18.7 10.0 %collective-permute-start.1 = (bf16[240,384]{1,0:T(8,128)(2,1)S(1)}, bf16[240,384]{1,0:T(8,128)(2,1)S(1)}, u32[]{:S(2)}, u32[]{:S(2)}) collective-permute-start(bf16[240,384]{1,0:T(8,128)(2,1)S(1)} %get-tuple-element.37), channel_id=1, source_target_pairs={{0,1},{1,2},{2,3},{3,0},{4,5},{5,6},{6,7},{7,4},{8,9},{9,10},{10,1... | collective-permute-start | bytes 552968 | tf_op jit(solution)/shard_map/ppermute | solution.py:422
  28.8 8.5 %collective-permute-start.18 = (bf16[4,48,384]{2,1,0:T(8,128)(2,1)S(1)}, bf16[4,48,384]{2,1,0:T(8,128)(2,1)S(1)}, u32[]{:S(2)}, u32[]{:S(2)}) collective-permute-start(bf16[4,48,384]{2,1,0:T(8,128)(2,1)S(1)} %get-tuple-element.54), channel_id=1, source_target_pairs={{0,1},{1,2},{2,3},{3,0},{4,5},{5,6},{6,7},{7,4},{8,9},{9,10},{10,1... | collective-permute-start | bytes 442376 | tf_op jit(solution)/shard_map/ppermute | solution.py:446
  29.8 25.0 %collective-permute-start.9 = (bf16[4,240,384]{2,1,0:T(8,128)(2,1)S(1)}, bf16[4,240,384]{2,1,0:T(8,128)(2,1)S(1)}, u32[]{:S(2)}, u32[]{:S(2)}) collective-permute-start(bf16[4,240,384]{2,1,0:T(8,128)(2,1)S(1)} %pad_maximum_fusion.refs_0_), channel_id=1, source_target_pairs={{0,4},{4,0},{8,12},{12,8},{16,20},{20,16},{24,28},{28,24},{1,5},{5... | collective-permute-start | bytes 2211848 | tf_op jit(solution)/shard_map/ppermute | solution.py:384
  31.4 7.6 %collective-permute-start.19 = (bf16[4,48,384]{2,1,0:T(8,128)(2,1)S(1)}, bf16[4,48,384]{2,1,0:T(8,128)(2,1)S(1)}, u32[]{:S(2)}, u32[]{:S(2)}) collective-permute-start(bf16[4,48,384]{2,1,0:T(8,128)(2,1)S(1)} %get-tuple-element.53), channel_id=1, source_target_pairs={{0,1},{1,2},{2,3},{3,0},{4,5},{5,6},{6,7},{7,4},{8,9},{9,10},{10,1... | collective-permute-start | bytes 442376 | tf_op jit(solution)/shard_map/ppermute | solution.py:446
  33.9 21.6 %collective-permute-start.17 = (bf16[4,96,384]{2,1,0:T(8,128)(2,1)S(1)}, bf16[4,96,384]{2,1,0:T(8,128)(2,1)S(1)}, u32[]{:S(2)}, u32[]{:S(2)}) collective-permute-start(bf16[4,96,384]{2,1,0:T(8,128)(2,1)S(1)} %shard_map.49.refs_10_), channel_id=1, source_target_pairs={{0,16},{4,20},{8,24},{12,28},{16,0},{20,4},{24,8},{28,12},{1,17},{... | collective-permute-start | bytes 884744 | tf_op jit(solution)/shard_map/ppermute | solution.py:384
  33.9 23.8 %collective-permute-start.11 = (bf16[4,240,384]{2,1,0:T(8,128)(2,1)S(1)}, bf16[4,240,384]{2,1,0:T(8,128)(2,1)S(1)}, u32[]{:S(2)}, u32[]{:S(2)}) collective-permute-start(bf16[4,240,384]{2,1,0:T(8,128)(2,1)S(1)} %pad_maximum_fusion.refs_0_), channel_id=1, source_target_pairs={{0,8},{4,12},{8,0},{12,4},{16,24},{20,28},{24,16},{28,20},{1,9},{5... | collective-permute-start | bytes 2211848 | tf_op jit(solution)/shard_map/ppermute | solution.py:384
  37.3 8.0 %collective-permute-start.21 = (bf16[4,48,384]{2,1,0:T(8,128)(2,1)S(1)}, bf16[4,48,384]{2,1,0:T(8,128)(2,1)S(1)}, u32[]{:S(2)}, u32[]{:S(2)}) collective-permute-start(bf16[4,48,384]{2,1,0:T(8,128)(2,1)S(1)} %collective-permute-done.18), channel_id=1, source_target_pairs={{0,1},{1,2},{2,3},{3,0},{4,5},{5,6},{6,7},{7,4},{8,9},{9,10},{10,1... | collective-permute-start | bytes 442376 | tf_op jit(solution)/shard_map/ppermute | solution.py:446
  39.0 8.8 %collective-permute-start.22 = (bf16[4,48,384]{2,1,0:T(8,128)(2,1)S(1)}, bf16[4,48,384]{2,1,0:T(8,128)(2,1)S(1)}, u32[]{:S(2)}, u32[]{:S(2)}) collective-permute-start(bf16[4,48,384]{2,1,0:T(8,128)(2,1)S(1)} %collective-permute-done.19), channel_id=1, source_target_pairs={{0,1},{1,2},{2,3},{3,0},{4,5},{5,6},{6,7},{7,4},{8,9},{9,10},{10,1... | collective-permute-start | bytes 442376 | tf_op jit(solution)/shard_map/ppermute | solution.py:446
  45.3 7.2 %collective-permute-start.24 = (bf16[4,48,384]{2,1,0:T(8,128)(2,1)S(1)}, bf16[4,48,384]{2,1,0:T(8,128)(2,1)S(1)}, u32[]{:S(2)}, u32[]{:S(2)}) collective-permute-start(bf16[4,48,384]{2,1,0:T(8,128)(2,1)S(1)} %collective-permute-done.21), channel_id=1, source_target_pairs={{0,1},{1,2},{2,3},{3,0},{4,5},{5,6},{6,7},{7,4},{8,9},{9,10},{10,1... | collective-permute-start | bytes 442376 | tf_op jit(solution)/shard_map/ppermute | solution.py:446
  47.8 6.9 %collective-permute-start.25 = (bf16[4,48,384]{2,1,0:T(8,128)(2,1)S(1)}, bf16[4,48,384]{2,1,0:T(8,128)(2,1)S(1)}, u32[]{:S(2)}, u32[]{:S(2)}) collective-permute-start(bf16[4,48,384]{2,1,0:T(8,128)(2,1)S(1)} %collective-permute-done.22), channel_id=1, source_target_pairs={{0,1},{1,2},{2,3},{3,0},{4,5},{5,6},{6,7},{7,4},{8,9},{9,10},{10,1... | collective-permute-start | bytes 442376 | tf_op jit(solution)/shard_map/ppermute | solution.py:446
  52.5 5.2 %collective-permute-start.20 = (bf16[4,96,384]{2,1,0:T(8,128)(2,1)S(1)}, bf16[4,96,384]{2,1,0:T(8,128)(2,1)S(1)}, u32[]{:S(2)}, u32[]{:S(2)}) collective-permute-start(bf16[4,96,384]{2,1,0:T(8,128)(2,1)S(1)} %constant_dynamic-update-slice_fusion.refs_12_), channel_id=1, source_target_pairs={{0,16},{4,20},{8,24},{12,28},{16,0},{20,4},{24,8},{28,12},{1,17},{... | collective-permute-start | bytes 884744 | tf_op jit(solution)/shard_map/ppermute | solution.py:384
  55.4 11.5 %collective-permute-start.15 = (bf16[4,128,384]{2,1,0:T(8,128)(2,1)S(1)}, bf16[4,128,384]{2,1,0:T(8,128)(2,1)S(1)}, u32[]{:S(2)}, u32[]{:S(2)}) collective-permute-start(bf16[4,128,384]{2,1,0:T(8,128)(2,1)S(1)} %slice.22), channel_id=1, source_target_pairs={{0,8},{4,12},{8,0},{12,4},{16,24},{20,28},{24,16},{28,20},{1,9},{5... | collective-permute-start | bytes 1179656 | tf_op jit(solution)/shard_map/ppermute | solution.py:384
  57.6 11.1 %collective-permute-start.8 = (bf16[4,240,384]{2,1,0:T(8,128)(2,1)S(1)}, bf16[4,240,384]{2,1,0:T(8,128)(2,1)S(1)}, u32[]{:S(2)}, u32[]{:S(2)}) collective-permute-start(bf16[4,240,384]{2,1,0:T(8,128)(2,1)S(1)} %pad_maximum_fusion.refs_0_), channel_id=1, source_target_pairs={{0,16},{4,20},{8,24},{12,28},{16,0},{20,4},{24,8},{28,12},{1,17},{... | collective-permute-start | bytes 2211848 | tf_op jit(solution)/shard_map/ppermute | solution.py:384
  57.6 12.8 %collective-permute-start.12 = (bf16[4,240,384]{2,1,0:T(8,128)(2,1)S(1)}, bf16[4,240,384]{2,1,0:T(8,128)(2,1)S(1)}, u32[]{:S(2)}, u32[]{:S(2)}) collective-permute-start(bf16[4,240,384]{2,1,0:T(8,128)(2,1)S(1)} %collective-permute-done.11.refs_4_), channel_id=1, source_target_pairs={{0,16},{4,20},{8,24},{12,28},{16,0},{20,4},{24,8},{28,12},{1,17},{... | collective-permute-start | bytes 2211848 | tf_op jit(solution)/shard_map/ppermute | solution.py:384
  58.1 12.3 %collective-permute-start.10 = (bf16[4,240,384]{2,1,0:T(8,128)(2,1)S(1)}, bf16[4,240,384]{2,1,0:T(8,128)(2,1)S(1)}, u32[]{:S(2)}, u32[]{:S(2)}) collective-permute-start(bf16[4,240,384]{2,1,0:T(8,128)(2,1)S(1)} %collective-permute-done.9.refs_2_), channel_id=1, source_target_pairs={{0,16},{4,20},{8,24},{12,28},{16,0},{20,4},{24,8},{28,12},{1,17},{... | collective-permute-start | bytes 2211848 | tf_op jit(solution)/shard_map/ppermute | solution.py:384
  58.3 10.5 %collective-permute-start.13 = (bf16[4,112,384]{2,1,0:T(8,128)(2,1)S(1)}, bf16[4,112,384]{2,1,0:T(8,128)(2,1)S(1)}, u32[]{:S(2)}, u32[]{:S(2)}) collective-permute-start(bf16[4,112,384]{2,1,0:T(8,128)(2,1)S(1)} %slice.21), channel_id=1, source_target_pairs={{0,4},{4,0},{8,12},{12,8},{16,20},{20,16},{24,28},{28,24},{1,5},{5... | collective-permute-start | bytes 1032200 | tf_op jit(solution)/shard_map/ppermute | solution.py:384
  103.1 6.1 %collective-permute-start.28 = (bf16[64,640]{1,0:T(8,128)(2,1)S(1)}, bf16[64,640]{1,0:T(8,128)(2,1)S(1)}, u32[]{:S(2)}, u32[]{:S(2)}) collective-permute-start(bf16[64,640]{1,0:T(8,128)(2,1)S(1)} %get-tuple-element.47), channel_id=1, source_target_pairs={{0,8},{4,12},{8,0},{12,4},{16,24},{20,28},{24,16},{28,20},{1,9},{5... | collective-permute-start | bytes 245768 | tf_op jit(solution)/shard_map/ppermute | solution.py:384
  103.6 6.1 %collective-permute-start.29 = (bf16[64,640]{1,0:T(8,128)(2,1)S(1)}, bf16[64,640]{1,0:T(8,128)(2,1)S(1)}, u32[]{:S(2)}, u32[]{:S(2)}) collective-permute-start(bf16[64,640]{1,0:T(8,128)(2,1)S(1)} %get-tuple-element.48), channel_id=1, source_target_pairs={{0,12},{4,8},{8,4},{12,0},{16,28},{20,24},{24,20},{28,16},{1,13},{... | collective-permute-start | bytes 245768 | tf_op jit(solution)/shard_map/ppermute | solution.py:384
  106.8 5.7 %collective-permute-start.32 = (bf16[64,640]{1,0:T(8,128)(2,1)S(1)}, bf16[64,640]{1,0:T(8,128)(2,1)S(1)}, u32[]{:S(2)}, u32[]{:S(2)}) collective-permute-start(bf16[64,640]{1,0:T(8,128)(2,1)S(1)} %get-tuple-element.51), channel_id=1, source_target_pairs={{0,28},{4,24},{8,20},{12,16},{16,12},{20,8},{24,4},{28,0},{1,29},{... | collective-permute-start | bytes 245768 | tf_op jit(solution)/shard_map/ppermute | solution.py:384
  (14 other events, 44.4 us)

commit v7 on v5

--- a/solution.py
+++ b/solution.py
@@ -89,14 +89,14 @@
             copy.wait()
 
     if riding:
-        row, col, tok = lax.axis_index("row"), lax.axis_index("col"), lax.axis_index("tok")
+        row, tok = lax.axis_index("row"), lax.axis_index("tok")
         cols = lax.axis_size("col")
     moves = []
     for piece, parts in zip(pieces, copies):
         for source, entry, part, lanes, first, held in parts:
             if riding:
                 flip, back = entry
-                entry = (row ^ flip) * cols + lax.rem(col - back + cols, cols)
+                entry = (row ^ flip) * cols + back
                 part = tok ^ part
             moves.append((piece, source, entry, part, lanes, first, held))
     for piece, source, entry, part, lanes, first, held in moves:
@@ -392,12 +392,10 @@
             out_specs=[in_vmem] * rows,
             compiler_params=small,
         )(own, swap(other, 1), lower)
-        line = [upper] + [
-            lax.ppermute(upper, "col", [(i, (i + shift) % cols) for i in range(cols)]) for shift in range(1, cols)
-        ]
+        value = lax.all_gather(upper, "col", axis=0, tiled=False)
         weight_pieces = [swap(value, 2 * flip) if flip else value for flip, value in enumerate(joined)]
         places = list(range(rows))
-        line, weight_pieces = lax.optimization_barrier((line, weight_pieces))
+        value, weight_pieces = lax.optimization_barrier((value, weight_pieces))
         plane = pl.pallas_call(
             plane_kernel,
             out_shape=jax.ShapeDtypeStruct((rows,) + lower.shape, jnp.bfloat16),
@@ -405,27 +403,24 @@
             out_specs=in_vmem,
             compiler_params=small,
         )(lower, *weight_pieces[1:])
-        up = [(i, (i + 1) % cols) for i in range(cols)]
-        value = jnp.stack(line)
         by_near, by_far = swap(value, 2), swap(value, 4)
         middle = cut // 2
         crossed = [
             (0, 0, value), (1, 0, by_near), (2, 0, by_far),
             (3, 0, swap(by_far[:, :middle], 2)), (3, middle, swap(by_near[:, middle:], 4)),
         ]
-        rounds = [plane]
-        for _ in range(cols - 1):
-            rounds.append(lax.ppermute(rounds[-1], "col", up))
+        rounds = lax.all_gather(plane, "col", axis=0, tiled=False).reshape((cols * rows,) + lower.shape)
         pieces, copies = [], []
         for flip, first, found in crossed:
             high = min(first + found.shape[1], cut) - first
             for part, arrived in enumerate((found, swap(found, 1))):
                 pieces.append(arrived)
                 copies.append([(i, (flip, i), part, held, first, high) for i in range(cols)])
-        for back, found in enumerate(rounds):
-            for part, arrived in enumerate((found, swap(found, 1))):
-                pieces.append(arrived)
-                copies.append([(flip, (flip, back), part, held, cut, block - cut) for flip in range(rows)])
+        for part, arrived in enumerate((rounds, swap(rounds, 1))):
+            pieces.append(arrived)
+            copies.append([
+                (i, (i % rows, i // rows), part, held, cut, block - cut) for i in range(cols * rows)
+            ])
         owners = (0, 0, -1, 1, 1, -1)
         small_inputs = []
     else:

time: 107 us -> 133 us (1.24)
  blocking collectives: 0 us -> 19.8 us
  between operations: 0.13 us -> 13.5 us
  starting transfers between devices: 24.1 us -> 19.3 us
  waiting for transfers between devices: 47.5 us -> 43.4 us
    ppermute x6 -> x0, waiting for transfers between devices: 39.2 us -> none  [the longest x3 24.8 us: body(): rounds.append(lax.ppermute(rounds[-1], 'col', up))]
    all_gather x0 -> x1, waiting for transfers between devices: none -> 27.2 us  [body(): lax.all_gather(plane, 'col', axis=0, tiled=False)]
    all_gather x0 -> x1, blocking collectives: none -> 19.8 us  [body(): value = lax.all_gather(upper, 'col', axis=0, tiled=False)]
    ppermute x25 -> x22, waiting for transfers between devices: 8.34 us -> 16.2 us  [swap(): return lax.ppermute(value, ('tok', 'row'), pairs)]
    ppermute x6 -> x0, starting transfers between devices: 5.74 us -> none  [the longest x3 4.85 us: body(): lax.ppermute(upper, 'col', [(i, (i + shift) % cols) for i in range(cols)])]
    ppermute x25 -> x22, starting transfers between devices: 18.4 us -> 19.3 us  [swap(): return lax.ppermute(value, ('tok', 'row'), pairs)]
  transfers between devices with their start and end apart: 31 -> 23, of which waited for: 14 -> 8; matrix products, arithmetic and copies ran while one was open for 0% -> 0% of each run, Pallas kernels for 1% -> 1%
where the time goes in v7:
time: 133 us
  waiting for transfers between devices  43.4 us (33%)
  Pallas kernels  34.3 us (26%)
  blocking collectives  19.8 us (15%)
  starting transfers between devices  19.3 us (15%)
  between operations  13.5 us (10%)
  local copies, waits for them, and re-layouts  2.4 us (2%)
    pallas_call x1, Pallas kernels, body(): pl.pallas_call(functools.partial(solve_kernel, owners, models, block, cop...  30.6 us
    all_gather x1, waiting for transfers between devices, body(): lax.all_gather(plane, 'col', axis=0, tiled=False)  27.2 us
    all_gather x1, blocking collectives, body(): value = lax.all_gather(upper, 'col', axis=0, tiled=False)  19.8 us
    ppermute x22, starting transfers between devices, swap(): return lax.ppermute(value, ('tok', 'row'), pairs)  19.3 us
    ppermute x22, waiting for transfers between devices, swap(): return lax.ppermute(value, ('tok', 'row'), pairs)  16.2 us
  transfers between devices with their start and end apart: 23, of which 8 were waited for; matrix products, arithmetic and copies ran while one was open for 0% of the time, Pallas kernels for 1%

profile of v7, /device:TPU:0, one launch (start us, length us, event | category | flops | bytes accessed | tf_op | source)
XLA Modules:
  0.0 132.7 jit_solution(14341340597976599772)
XLA Ops:
  6.5 1.3 copy-done
  9.4 1.4 %collective-permute-done.given_ref = bf16[320,128]{1,0:T(8,128)(2,1)S(1)} collective-permute-done((bf16[320,128]{1,0:T(8,128)(2,1)S(1)}, bf16[320,128]{1,0:T(8,128)(2,1)S(1)}, u32[]{:S(2)}, u32[]{:S(2)}) %collective-permute-start) | collective-permute-done | bytes 81952 | tf_op jit(solution)/shard_map/ppermute | solution.py:358
  10.7 0.8 shard_map.46
  11.6 2.9 %collective-permute-start.2 = (bf16[160,1280]{1,0:T(8,128)(2,1)S(1)}, bf16[160,1280]{1,0:T(8,128)(2,1)S(1)}, u32[]{:S(2)}, u32[]{:S(2)}) collective-permute-start(bf16[160,1280]{1,0:T(8,128)(2,1)S(1)} %get-tuple-element.31), channel_id=1, source_target_pairs={{0,4},{4,0},{8,12},{12,8},{16,20},{20,16},{24,28},{28,24},{1,5},{5... | collective-permute-start | bytes 1228808 | tf_op jit(solution)/shard_map/ppermute | solution.py:358
  14.6 1.5 %collective-permute-start.3 = (bf16[160,1280]{1,0:T(8,128)(2,1)S(1)}, bf16[160,1280]{1,0:T(8,128)(2,1)S(1)}, u32[]{:S(2)}, u32[]{:S(2)}) collective-permute-start(bf16[160,1280]{1,0:T(8,128)(2,1)S(1)} %get-tuple-element.32), channel_id=1, source_target_pairs={{0,8},{4,12},{8,0},{12,4},{16,24},{20,28},{24,16},{28,20},{1,9},{5... | collective-permute-start | bytes 1228808 | tf_op jit(solution)/shard_map/ppermute | solution.py:358
  16.1 19.8 %all-gather = bf16[960,384]{1,0:T(8,128)(2,1)S(1)} all-gather(bf16[240,384]{1,0:T(8,128)(2,1)S(1)} %get-tuple-element.26), channel_id=2, replica_groups=mesh['tok'=2,'row'=4,'col'=4] {'col'}, dimensions={0}, use_global_device_ids=true | all-gather | bytes 921600 | tf_op jit(solution)/shard_map/all_gather | solution.py:395
  36.7 1.6 %collective-permute-start.6 = (bf16[4,240,384]{2,1,0:T(8,128)(2,1)S(1)}, bf16[4,240,384]{2,1,0:T(8,128)(2,1)S(1)}, u32[]{:S(2)}, u32[]{:S(2)}) collective-permute-start(bf16[4,240,384]{2,1,0:T(8,128)(2,1)S(1)} %bitcast.3), channel_id=1, source_target_pairs={{0,4},{4,0},{8,12},{12,8},{16,20},{20,16},{24,28},{28,24},{1,5},{5... | collective-permute-start | bytes 2211848 | tf_op jit(solution)/shard_map/ppermute | solution.py:358
  38.2 1.5 %collective-permute-start.8 = (bf16[4,240,384]{2,1,0:T(8,128)(2,1)S(1)}, bf16[4,240,384]{2,1,0:T(8,128)(2,1)S(1)}, u32[]{:S(2)}, u32[]{:S(2)}) collective-permute-start(bf16[4,240,384]{2,1,0:T(8,128)(2,1)S(1)} %bitcast.4), channel_id=1, source_target_pairs={{0,8},{4,12},{8,0},{12,4},{16,24},{20,28},{24,16},{28,20},{1,9},{5... | collective-permute-start | bytes 2211848 | tf_op jit(solution)/shard_map/ppermute | solution.py:358
  39.8 27.2 %all-gather.4.cloned.1.call-done.refs_10_ = bf16[16,96,384]{2,1,0:T(8,128)(2,1)} async-done(((bf16[4,96,384]{2,1,0:T(8,128)(2,1)}), bf16[16,96,384]{2,1,0:T(8,128)(2,1)}) %all-gather.4.cloned.1.call-update) | async-done | bytes 1179664 | tf_op jit(solution)/shard_map/all_gather | solution.py:412
  67.0 1.5 %collective-permute-start.12 = (bf16[4,128,384]{2,1,0:T(8,128)(2,1)S(1)}, bf16[4,128,384]{2,1,0:T(8,128)(2,1)S(1)}, u32[]{:S(2)}, u32[]{:S(2)}) collective-permute-start(bf16[4,128,384]{2,1,0:T(8,128)(2,1)S(1)} %slice.14), channel_id=1, source_target_pairs={{0,8},{4,12},{8,0},{12,4},{16,24},{20,28},{24,16},{28,20},{1,9},{5... | collective-permute-start | bytes 1179656 | tf_op jit(solution)/shard_map/ppermute | solution.py:358
  69.1 1.5 %collective-permute-start.10 = (bf16[4,112,384]{2,1,0:T(8,128)(2,1)S(1)}, bf16[4,112,384]{2,1,0:T(8,128)(2,1)S(1)}, u32[]{:S(2)}, u32[]{:S(2)}) collective-permute-start(bf16[4,112,384]{2,1,0:T(8,128)(2,1)S(1)} %slice.13), channel_id=1, source_target_pairs={{0,4},{4,0},{8,12},{12,8},{16,20},{20,16},{24,28},{28,24},{1,5},{5... | collective-permute-start | bytes 1032200 | tf_op jit(solution)/shard_map/ppermute | solution.py:358
  70.6 8.0 %collective-permute-done.12.refs_8_ = bf16[4,128,384]{2,1,0:T(8,128)(2,1)S(1)} collective-permute-done((bf16[4,128,384]{2,1,0:T(8,128)(2,1)S(1)}, bf16[4,128,384]{2,1,0:T(8,128)(2,1)S(1)}, u32[]{:S(2)}, u32[]{:S(2)}) %collective-permute-start.12) | collective-permute-done | bytes 393248 | tf_op jit(solution)/shard_map/ppermute | solution.py:358
  78.6 0.8 collective-permute-done.10.refs_6_
  79.4 1.6 %collective-permute-done.11.refs_7_ = bf16[4,112,384]{2,1,0:T(8,128)(2,1)S(1)} collective-permute-done((bf16[4,112,384]{2,1,0:T(8,128)(2,1)S(1)}, bf16[4,112,384]{2,1,0:T(8,128)(2,1)S(1)}, u32[]{:S(2)}, u32[]{:S(2)}) %collective-permute-start.11) | collective-permute-done | bytes 344096 | tf_op jit(solution)/shard_map/ppermute | solution.py:358
  81.1 1.0 copy-done.4
  82.0 30.6 %shard_map.50 = (bf16[64,640]{1,0:T(8,128)(2,1)S(1)}, bf16[64,640]{1,0:T(8,128)(2,1)S(1)}, bf16[64,640]{1,0:T(8,128)(2,1)S(1)}, bf16[64,640]{1,0:T(8,128)(2,1)S(...) custom-call(s32[2]{0:T(128)S(1)} %copy-done.5, ...), custom_call_target="tpu_custom_call" | custom-call | tf_op jit(solution)/shard_map/pallas_call | solution.py:455
  112.6 1.5 %collective-permute-start.15 = (bf16[64,640]{1,0:T(8,128)(2,1)S(1)}, bf16[64,640]{1,0:T(8,128)(2,1)S(1)}, u32[]{:S(2)}, u32[]{:S(2)}) collective-permute-start(bf16[64,640]{1,0:T(8,128)(2,1)S(1)} %get-tuple-element.40), channel_id=1, source_target_pairs={{0,4},{4,0},{8,12},{12,8},{16,20},{20,16},{24,28},{28,24},{1,5},{5... | collective-permute-start | bytes 245768 | tf_op jit(solution)/shard_map/ppermute | solution.py:358
  114.2 1.3 collective-permute-start.16
  115.4 0.8 collective-permute-start.17
  116.5 2.1 %collective-permute-start.19 = (bf16[64,640]{1,0:T(8,128)(2,1)S(1)}, bf16[64,640]{1,0:T(8,128)(2,1)S(1)}, u32[]{:S(2)}, u32[]{:S(2)}) collective-permute-start(bf16[64,640]{1,0:T(8,128)(2,1)S(1)} %get-tuple-element.44), channel_id=1, source_target_pairs={{0,24},{4,28},{8,16},{12,20},{16,8},{20,12},{24,0},{28,4},{1,25},{... | collective-permute-start | bytes 245768 | tf_op jit(solution)/shard_map/ppermute | solution.py:358
  118.8 1.0 collective-permute-start.21
  119.8 1.8 %collective-permute-done.17.refs_3_ = bf16[64,640]{1,0:T(8,128)(2,1)S(1)} collective-permute-done((bf16[64,640]{1,0:T(8,128)(2,1)S(1)}, bf16[64,640]{1,0:T(8,128)(2,1)S(1)}, u32[]{:S(2)}, u32[]{:S(2)}) %collective-permute-start.17) | collective-permute-done | bytes 81952 | tf_op jit(solution)/shard_map/ppermute | solution.py:358
  122.0 2.3 %collective-permute-done.20.refs_6_ = bf16[64,640]{1,0:T(8,128)(2,1)S(1)} collective-permute-done((bf16[64,640]{1,0:T(8,128)(2,1)S(1)}, bf16[64,640]{1,0:T(8,128)(2,1)S(1)}, u32[]{:S(2)}, u32[]{:S(2)}) %collective-permute-start.20) | collective-permute-done | bytes 81952 | tf_op jit(solution)/shard_map/ppermute | solution.py:358
  124.3 1.6 %shard_map.51 = f32[640,512]{1,0:T(8,128)} custom-call(bf16[64,640]{1,0:T(8,128)(2,1)S(1)} %get-tuple-element.39.refs_0_, bf16[64,640]{1,0:T(8,128)(2,1)S(1)} %collective-permute-done.15.refs_1_, bf16[64,640]{1,0:T(8,128)(2,1)S(1)} %collective-permute-done.16.refs_2_, bf16[64,640]{1,0:T(8,128)(2,1)S(1)} %collective-permute-done.17.refs_3_, ...), custom_call_target="tpu_custom_call" | custom-call | tf_op jit(solution)/shard_map/pallas_call | solution.py:485
  (47 shorter events, 4.0 us)
Async XLA Ops:
  6.5 60.4 %all-gather.4.cloned.1.call-start = ((), (), s32[]{:S(2)}) async-start(), calls=%async_computation | async-start | bytes 1474560 | tf_op jit(solution)/shard_map/all_gather | solution.py:412
  8.4 3.1 %collective-permute-start.1 = (bf16[4,64,1280]{2,1,0:T(8,128)(2,1)S(1)}, bf16[4,64,1280]{2,1,0:T(8,128)(2,1)S(1)}, u32[]{:S(2)}, u32[]{:S(2)}) collective-permute-start(bf16[4,64,1280]{2,1,0:T(8,128)(2,1)S(1)} %get-tuple-element.28), channel_id=1, source_target_pairs={{0,16},{4,20},{8,24},{12,28},{16,0},{20,4},{24,8},{28,12},{1,17},{... | collective-permute-start | bytes 1966088 | tf_op jit(solution)/shard_map/ppermute | solution.py:358
  8.9 1.8 %collective-permute-start = (bf16[320,128]{1,0:T(8,128)(2,1)S(1)}, bf16[320,128]{1,0:T(8,128)(2,1)S(1)}, u32[]{:S(2)}, u32[]{:S(2)}) collective-permute-start(bf16[320,128]{1,0:T(8,128)(2,1)S(1)} %slice.12), channel_id=1, source_target_pairs={{0,16},{4,20},{8,24},{12,28},{16,0},{20,4},{24,8},{28,12},{1,17},{... | collective-permute-start | bytes 245768 | tf_op jit(solution)/shard_map/ppermute | solution.py:358
  11.6 24.3 %copy-start.3 = (bf16[128,1280]{1,0:T(8,128)(2,1)}, bf16[128,1280]{1,0:T(8,128)(2,1)S(1)}, u32[]{:S(2)}) copy-start(bf16[128,1280]{1,0:T(8,128)(2,1)S(1)} %get-tuple-element.38.refs_12_) | copy-start | bytes 983044
  11.6 24.3 %collective-permute-start.2 = (bf16[160,1280]{1,0:T(8,128)(2,1)S(1)}, bf16[160,1280]{1,0:T(8,128)(2,1)S(1)}, u32[]{:S(2)}, u32[]{:S(2)}) collective-permute-start(bf16[160,1280]{1,0:T(8,128)(2,1)S(1)} %get-tuple-element.31), channel_id=1, source_target_pairs={{0,4},{4,0},{8,12},{12,8},{16,20},{20,16},{24,28},{28,24},{1,5},{5... | collective-permute-start | bytes 1228808 | tf_op jit(solution)/shard_map/ppermute | solution.py:358
  14.6 21.3 %collective-permute-start.3 = (bf16[160,1280]{1,0:T(8,128)(2,1)S(1)}, bf16[160,1280]{1,0:T(8,128)(2,1)S(1)}, u32[]{:S(2)}, u32[]{:S(2)}) collective-permute-start(bf16[160,1280]{1,0:T(8,128)(2,1)S(1)} %get-tuple-element.32), channel_id=1, source_target_pairs={{0,8},{4,12},{8,0},{12,4},{16,24},{20,28},{24,16},{28,20},{1,9},{5... | collective-permute-start | bytes 1228808 | tf_op jit(solution)/shard_map/ppermute | solution.py:358
  16.1 19.8 %collective-permute-start.4 = (bf16[160,1280]{1,0:T(8,128)(2,1)S(1)}, bf16[160,1280]{1,0:T(8,128)(2,1)S(1)}, u32[]{:S(2)}, u32[]{:S(2)}) collective-permute-start(bf16[160,1280]{1,0:T(8,128)(2,1)S(1)} %get-tuple-element.33), channel_id=1, source_target_pairs={{0,12},{4,8},{8,4},{12,0},{16,28},{20,24},{24,20},{28,16},{1,13},{... | collective-permute-start | bytes 1228808 | tf_op jit(solution)/shard_map/ppermute | solution.py:358
  36.7 30.3 %collective-permute-start.6 = (bf16[4,240,384]{2,1,0:T(8,128)(2,1)S(1)}, bf16[4,240,384]{2,1,0:T(8,128)(2,1)S(1)}, u32[]{:S(2)}, u32[]{:S(2)}) collective-permute-start(bf16[4,240,384]{2,1,0:T(8,128)(2,1)S(1)} %bitcast.3), channel_id=1, source_target_pairs={{0,4},{4,0},{8,12},{12,8},{16,20},{20,16},{24,28},{28,24},{1,5},{5... | collective-permute-start | bytes 2211848 | tf_op jit(solution)/shard_map/ppermute | solution.py:358
  38.2 30.3 %collective-permute-start.8 = (bf16[4,240,384]{2,1,0:T(8,128)(2,1)S(1)}, bf16[4,240,384]{2,1,0:T(8,128)(2,1)S(1)}, u32[]{:S(2)}, u32[]{:S(2)}) collective-permute-start(bf16[4,240,384]{2,1,0:T(8,128)(2,1)S(1)} %bitcast.4), channel_id=1, source_target_pairs={{0,8},{4,12},{8,0},{12,4},{16,24},{20,28},{24,16},{28,20},{1,9},{5... | collective-permute-start | bytes 2211848 | tf_op jit(solution)/shard_map/ppermute | solution.py:358
  39.8 29.3 %collective-permute-start.5 = (bf16[4,240,384]{2,1,0:T(8,128)(2,1)S(1)}, bf16[4,240,384]{2,1,0:T(8,128)(2,1)}, u32[]{:S(2)}, u32[]{:S(2)}) collective-permute-start(bf16[4,240,384]{2,1,0:T(8,128)(2,1)S(1)} %bitcast.5), channel_id=1, source_target_pairs={{0,16},{4,20},{8,24},{12,28},{16,0},{20,4},{24,8},{28,12},{1,17},{... | collective-permute-start | bytes 2211848 | tf_op jit(solution)/shard_map/ppermute | solution.py:358
  66.9 14.1 %collective-permute-start.14 = (bf16[16,96,384]{2,1,0:T(8,128)(2,1)}, bf16[16,96,384]{2,1,0:T(8,128)(2,1)S(1)}, u32[]{:S(2)}, u32[]{:S(2)}) collective-permute-start(bf16[16,96,384]{2,1,0:T(8,128)(2,1)} %all-gather.4.cloned.1.call-done.refs_10_), channel_id=1, source_target_pairs={{0,16},{4,20},{8,24},{12,28},{16,0},{20,4},{24,8},{28,12},{1,17},{... | collective-permute-start | bytes 3538952 | tf_op jit(solution)/shard_map/ppermute | solution.py:358
  67.0 11.6 %collective-permute-start.12 = (bf16[4,128,384]{2,1,0:T(8,128)(2,1)S(1)}, bf16[4,128,384]{2,1,0:T(8,128)(2,1)S(1)}, u32[]{:S(2)}, u32[]{:S(2)}) collective-permute-start(bf16[4,128,384]{2,1,0:T(8,128)(2,1)S(1)} %slice.14), channel_id=1, source_target_pairs={{0,8},{4,12},{8,0},{12,4},{16,24},{20,28},{24,16},{28,20},{1,9},{5... | collective-permute-start | bytes 1179656 | tf_op jit(solution)/shard_map/ppermute | solution.py:358
  68.5 12.5 %collective-permute-start.9 = (bf16[4,240,384]{2,1,0:T(8,128)(2,1)S(1)}, bf16[4,240,384]{2,1,0:T(8,128)(2,1)S(1)}, u32[]{:S(2)}, u32[]{:S(2)}) collective-permute-start(bf16[4,240,384]{2,1,0:T(8,128)(2,1)S(1)} %collective-permute-done.8.refs_4_), channel_id=1, source_target_pairs={{0,16},{4,20},{8,24},{12,28},{16,0},{20,4},{24,8},{28,12},{1,17},{... | collective-permute-start | bytes 2211848 | tf_op jit(solution)/shard_map/ppermute | solution.py:358
  68.8 12.3 %collective-permute-start.7 = (bf16[4,240,384]{2,1,0:T(8,128)(2,1)S(1)}, bf16[4,240,384]{2,1,0:T(8,128)(2,1)S(1)}, u32[]{:S(2)}, u32[]{:S(2)}) collective-permute-start(bf16[4,240,384]{2,1,0:T(8,128)(2,1)S(1)} %collective-permute-done.6.refs_2_), channel_id=1, source_target_pairs={{0,16},{4,20},{8,24},{12,28},{16,0},{20,4},{24,8},{28,12},{1,17},{... | collective-permute-start | bytes 2211848 | tf_op jit(solution)/shard_map/ppermute | solution.py:358
  69.1 10.3 %collective-permute-start.10 = (bf16[4,112,384]{2,1,0:T(8,128)(2,1)S(1)}, bf16[4,112,384]{2,1,0:T(8,128)(2,1)S(1)}, u32[]{:S(2)}, u32[]{:S(2)}) collective-permute-start(bf16[4,112,384]{2,1,0:T(8,128)(2,1)S(1)} %slice.13), channel_id=1, source_target_pairs={{0,4},{4,0},{8,12},{12,8},{16,20},{20,16},{24,28},{28,24},{1,5},{5... | collective-permute-start | bytes 1032200 | tf_op jit(solution)/shard_map/ppermute | solution.py:358
  78.6 2.4 %collective-permute-start.13 = (bf16[4,128,384]{2,1,0:T(8,128)(2,1)S(1)}, bf16[4,128,384]{2,1,0:T(8,128)(2,1)S(1)}, u32[]{:S(2)}, u32[]{:S(2)}) collective-permute-start(bf16[4,128,384]{2,1,0:T(8,128)(2,1)S(1)} %collective-permute-done.12.refs_8_), channel_id=1, source_target_pairs={{0,16},{4,20},{8,24},{12,28},{16,0},{20,4},{24,8},{28,12},{1,17},{... | collective-permute-start | bytes 1179656 | tf_op jit(solution)/shard_map/ppermute | solution.py:358
  79.4 1.7 %collective-permute-start.11 = (bf16[4,112,384]{2,1,0:T(8,128)(2,1)S(1)}, bf16[4,112,384]{2,1,0:T(8,128)(2,1)S(1)}, u32[]{:S(2)}, u32[]{:S(2)}) collective-permute-start(bf16[4,112,384]{2,1,0:T(8,128)(2,1)S(1)} %collective-permute-done.10.refs_6_), channel_id=1, source_target_pairs={{0,16},{4,20},{8,24},{12,28},{16,0},{20,4},{24,8},{28,12},{1,17},{... | collective-permute-start | bytes 1032200 | tf_op jit(solution)/shard_map/ppermute | solution.py:358
  112.6 6.0 %collective-permute-start.15 = (bf16[64,640]{1,0:T(8,128)(2,1)S(1)}, bf16[64,640]{1,0:T(8,128)(2,1)S(1)}, u32[]{:S(2)}, u32[]{:S(2)}) collective-permute-start(bf16[64,640]{1,0:T(8,128)(2,1)S(1)} %get-tuple-element.40), channel_id=1, source_target_pairs={{0,4},{4,0},{8,12},{12,8},{16,20},{20,16},{24,28},{28,24},{1,5},{5... | collective-permute-start | bytes 245768 | tf_op jit(solution)/shard_map/ppermute | solution.py:358
  114.2 4.7 %collective-permute-start.16 = (bf16[64,640]{1,0:T(8,128)(2,1)S(1)}, bf16[64,640]{1,0:T(8,128)(2,1)S(1)}, u32[]{:S(2)}, u32[]{:S(2)}) collective-permute-start(bf16[64,640]{1,0:T(8,128)(2,1)S(1)} %get-tuple-element.41), channel_id=1, source_target_pairs={{0,8},{4,12},{8,0},{12,4},{16,24},{20,28},{24,16},{28,20},{1,9},{5... | collective-permute-start | bytes 245768 | tf_op jit(solution)/shard_map/ppermute | solution.py:358
  115.4 6.2 %collective-permute-start.17 = (bf16[64,640]{1,0:T(8,128)(2,1)S(1)}, bf16[64,640]{1,0:T(8,128)(2,1)S(1)}, u32[]{:S(2)}, u32[]{:S(2)}) collective-permute-start(bf16[64,640]{1,0:T(8,128)(2,1)S(1)} %get-tuple-element.42), channel_id=1, source_target_pairs={{0,12},{4,8},{8,4},{12,0},{16,28},{20,24},{24,20},{28,16},{1,13},{... | collective-permute-start | bytes 245768 | tf_op jit(solution)/shard_map/ppermute | solution.py:358
  116.2 5.5 %collective-permute-start.18 = (bf16[64,640]{1,0:T(8,128)(2,1)S(1)}, bf16[64,640]{1,0:T(8,128)(2,1)S(1)}, u32[]{:S(2)}, u32[]{:S(2)}) collective-permute-start(bf16[64,640]{1,0:T(8,128)(2,1)S(1)} %get-tuple-element.43), channel_id=1, source_target_pairs={{0,20},{4,16},{8,28},{12,24},{16,4},{20,0},{24,12},{28,8},{1,21},{... | collective-permute-start | bytes 245768 | tf_op jit(solution)/shard_map/ppermute | solution.py:358
  116.5 5.4 %collective-permute-start.19 = (bf16[64,640]{1,0:T(8,128)(2,1)S(1)}, bf16[64,640]{1,0:T(8,128)(2,1)S(1)}, u32[]{:S(2)}, u32[]{:S(2)}) collective-permute-start(bf16[64,640]{1,0:T(8,128)(2,1)S(1)} %get-tuple-element.44), channel_id=1, source_target_pairs={{0,24},{4,28},{8,16},{12,20},{16,8},{20,12},{24,0},{28,4},{1,25},{... | collective-permute-start | bytes 245768 | tf_op jit(solution)/shard_map/ppermute | solution.py:358
  118.6 5.6 %collective-permute-start.20 = (bf16[64,640]{1,0:T(8,128)(2,1)S(1)}, bf16[64,640]{1,0:T(8,128)(2,1)S(1)}, u32[]{:S(2)}, u32[]{:S(2)}) collective-permute-start(bf16[64,640]{1,0:T(8,128)(2,1)S(1)} %get-tuple-element.45), channel_id=1, source_target_pairs={{0,28},{4,24},{8,20},{12,16},{16,12},{20,8},{24,4},{28,0},{1,29},{... | collective-permute-start | bytes 245768 | tf_op jit(solution)/shard_map/ppermute | solution.py:358
  118.8 5.4 %collective-permute-start.21 = (bf16[64,640]{1,0:T(8,128)(2,1)S(1)}, bf16[64,640]{1,0:T(8,128)(2,1)S(1)}, u32[]{:S(2)}, u32[]{:S(2)}) collective-permute-start(bf16[64,640]{1,0:T(8,128)(2,1)S(1)} %get-tuple-element.46), channel_id=1, source_target_pairs={{0,16},{4,20},{8,24},{12,28},{16,0},{20,4},{24,8},{28,12},{1,17},{... | collective-permute-start | bytes 245768 | tf_op jit(solution)/shard_map/ppermute | solution.py:358
  (6 other events, 24.5 us)
Sparse Core Ops, SparseCore 0:
  36.8 30.0 all-gather.3

commit v8 on v5

--- a/solution.py
+++ b/solution.py
@@ -21,6 +21,20 @@
 def two_terms(value):
     high = value.astype(jnp.bfloat16).astype(jnp.float32)
     return jnp.concatenate([high, value - high], axis=0).astype(jnp.bfloat16)
+
+
+def add_over_features(left, tokens, part, found):
+    slots = tokens.shape[1]
+    if slots <= MOST_TOKENS:
+        found[...] += jnp.dot(left, tokens[part, :], preferred_element_type=jnp.float32)
+        return
+
+    def some(step, carry):
+        lanes = pl.ds(pl.multiple_of(step * CHUNK, CHUNK), CHUNK)
+        found[:, lanes] += jnp.dot(left, tokens[part, lanes], preferred_element_type=jnp.float32)
+        return carry
+
+    lax.fori_loop(0, slots // CHUNK, some, 0)
 
 
 def over_features(left, tokens, found):
@@ -145,8 +159,7 @@
     inverse_rms = lax.rsqrt(squares / width + EPSILON) * live
     finish(1)
 
-    def norm_rows(step, carry):
-        start = pl.multiple_of(step * LANES, LANES)
+    def norm_rows(start):
         gains = gains_ref[pl.ds(start, LANES), :]
         sums = [jnp.zeros((LANES, LANES), jnp.float32) for _ in range(models)]
         for tile, owner in enumerate(owners):
@@ -170,12 +183,20 @@
         for model in range(models):
             squared[model:model + 1, pl.ds(start, LANES)] = sums[model]
         diagonal[:, pl.ds(start, LANES)] = functools.reduce(jnp.add, sums)
+
+    def norm_and_multiply(step, carry):
+        start = pl.multiple_of(step * 2 * LANES, 2 * LANES)
+        for half in range(2):
+            norm_rows(pl.multiple_of(start + half * LANES, LANES))
+        rows = pl.ds(start, 2 * LANES)
+        add_over_features(weights[:, rows], tokens, rows, values.at[:models * columns])
         return carry
 
-    lax.fori_loop(0, width // LANES, norm_rows, 0, unroll=4 if riding else 1)
-
     finish(2)
-    over_features(weights, tokens, values)
+    values[...] = jnp.zeros_like(values)
+
+    lax.fori_loop(0, width // (2 * LANES), norm_and_multiply, 0, unroll=2 if riding else 1)
+
     picked = []
     for tile, owner in enumerate(owners):
         lanes = slice(tile * LANES, (tile + 1) * LANES)

time: 107 us -> 106 us (level)
  Pallas kernels: 33.7 us -> 32.6 us
    pallas_call x1, Pallas kernels: 30.8 us -> 29.7 us  [body(): pl.pallas_call(functools.partial(solve_kernel, owners, models, block, cop...]
where the time goes in v8:
time: 106 us
  waiting for transfers between devices  47.5 us (45%)
  Pallas kernels  32.6 us (31%)
  starting transfers between devices  24.1 us (23%)
  local copies, waits for them, and re-layouts  1.43 us (1%)
    pallas_call x1, Pallas kernels, body(): pl.pallas_call(functools.partial(solve_kernel, owners, models, block, cop...  29.7 us
    ppermute x3, waiting for transfers between devices, body(): rounds.append(lax.ppermute(rounds[-1], 'col', up))  24.8 us
    ppermute x25, starting transfers between devices, swap(): return lax.ppermute(value, ('tok', 'row'), pairs)  18.4 us
    ppermute x3, waiting for transfers between devices, body(): lax.ppermute(upper, 'col', [(i, (i + shift) % cols) for i in range(cols)])  14.3 us
    ppermute x25, waiting for transfers between devices, swap(): return lax.ppermute(value, ('tok', 'row'), pairs)  8.32 us
    ppermute x3, starting transfers between devices, body(): lax.ppermute(upper, 'col', [(i, (i + shift) % cols) for i in range(cols)])  4.85 us
  transfers between devices with their start and end apart: 31, of which 14 were waited for; matrix products, arithmetic and copies ran while one was open for 0% of the time, Pallas kernels for 1%

profile of v8, /device:TPU:0, one launch (start us, length us, event | category | flops | bytes accessed | tf_op | source)
XLA Modules:
  0.0 105.9 jit_solution(17122299121255273358)
XLA Ops:
  0.0 1.3 %copy-done = bf16[1,1280,512]{2,1,0:T(8,128)(2,1)S(1)} copy-done((bf16[1,1280,512]{2,1,0:T(8,128)(2,1)S(1)}, bf16[1,1280,512]{2,1,0:T(8,128)(2,1)}, u32[]{:S(2)}) %copy-start) | copy-done | bytes 1310744
  2.8 1.4 %collective-permute-done.given_ref = bf16[320,128]{1,0:T(8,128)(2,1)S(1)} collective-permute-done((bf16[320,128]{1,0:T(8,128)(2,1)S(1)}, bf16[320,128]{1,0:T(8,128)(2,1)S(1)}, u32[]{:S(2)}, u32[]{:S(2)}) %collective-permute-start) | collective-permute-done | bytes 81952 | tf_op jit(solution)/shard_map/ppermute | solution.py:379
  5.1 2.9 %collective-permute-start.5 = (bf16[160,1280]{1,0:T(8,128)(2,1)S(1)}, bf16[160,1280]{1,0:T(8,128)(2,1)S(1)}, u32[]{:S(2)}, u32[]{:S(2)}) collective-permute-start(bf16[160,1280]{1,0:T(8,128)(2,1)S(1)} %get-tuple-element.34), channel_id=1, source_target_pairs={{0,4},{4,0},{8,12},{12,8},{16,20},{20,16},{24,28},{28,24},{1,5},{5... | collective-permute-start | bytes 1228808 | tf_op jit(solution)/shard_map/ppermute | solution.py:379
  8.0 1.5 %collective-permute-start.6 = (bf16[160,1280]{1,0:T(8,128)(2,1)S(1)}, bf16[160,1280]{1,0:T(8,128)(2,1)S(1)}, u32[]{:S(2)}, u32[]{:S(2)}) collective-permute-start(bf16[160,1280]{1,0:T(8,128)(2,1)S(1)} %get-tuple-element.35), channel_id=1, source_target_pairs={{0,8},{4,12},{8,0},{12,4},{16,24},{20,28},{24,16},{28,20},{1,9},{5... | collective-permute-start | bytes 1228808 | tf_op jit(solution)/shard_map/ppermute | solution.py:379
  9.6 4.1 %collective-permute-start.3 = (bf16[240,384]{1,0:T(8,128)(2,1)S(1)}, bf16[240,384]{1,0:T(8,128)(2,1)S(1)}, u32[]{:S(2)}, u32[]{:S(2)}) collective-permute-start(bf16[240,384]{1,0:T(8,128)(2,1)S(1)} %get-tuple-element.37), channel_id=1, source_target_pairs={{0,3},{1,0},{2,1},{3,2},{4,7},{5,4},{6,5},{7,6},{8,11},{9,8},{10,9... | collective-permute-start | bytes 552968 | tf_op jit(solution)/shard_map/ppermute | solution.py:417
  13.6 5.1 %collective-permute-done.3 = bf16[240,384]{1,0:T(8,128)(2,1)S(1)} collective-permute-done((bf16[240,384]{1,0:T(8,128)(2,1)S(1)}, bf16[240,384]{1,0:T(8,128)(2,1)S(1)}, u32[]{:S(2)}, u32[]{:S(2)}) %collective-permute-start.3) | collective-permute-done | bytes 184352 | tf_op jit(solution)/shard_map/ppermute | solution.py:417
  18.7 0.8 collective-permute-start.1
  19.5 9.2 %collective-permute-done.2 = bf16[240,384]{1,0:T(8,128)(2,1)S(1)} collective-permute-done((bf16[240,384]{1,0:T(8,128)(2,1)S(1)}, bf16[240,384]{1,0:T(8,128)(2,1)S(1)}, u32[]{:S(2)}, u32[]{:S(2)}) %collective-permute-start.2) | collective-permute-done | bytes 184352 | tf_op jit(solution)/shard_map/ppermute | solution.py:417
  28.9 1.6 %collective-permute-start.9 = (bf16[4,240,384]{2,1,0:T(8,128)(2,1)S(1)}, bf16[4,240,384]{2,1,0:T(8,128)(2,1)S(1)}, u32[]{:S(2)}, u32[]{:S(2)}) collective-permute-start(bf16[4,240,384]{2,1,0:T(8,128)(2,1)S(1)} %pad_maximum_fusion.refs_0_), channel_id=1, source_target_pairs={{0,4},{4,0},{8,12},{12,8},{16,20},{20,16},{24,28},{28,24},{1,5},{5... | collective-permute-start | bytes 2211848 | tf_op jit(solution)/shard_map/ppermute | solution.py:379
  30.4 0.9 collective-permute-start.18
  31.3 1.5 %collective-permute-start.11 = (bf16[4,240,384]{2,1,0:T(8,128)(2,1)S(1)}, bf16[4,240,384]{2,1,0:T(8,128)(2,1)S(1)}, u32[]{:S(2)}, u32[]{:S(2)}) collective-permute-start(bf16[4,240,384]{2,1,0:T(8,128)(2,1)S(1)} %pad_maximum_fusion.refs_0_), channel_id=1, source_target_pairs={{0,8},{4,12},{8,0},{12,4},{16,24},{20,28},{24,16},{28,20},{1,9},{5... | collective-permute-start | bytes 2211848 | tf_op jit(solution)/shard_map/ppermute | solution.py:379
  32.9 7.5 %collective-permute-done.18.refs_12_ = bf16[4,96,384]{2,1,0:T(8,128)(2,1)S(1)} collective-permute-done((bf16[4,96,384]{2,1,0:T(8,128)(2,1)S(1)}, bf16[4,96,384]{2,1,0:T(8,128)(2,1)S(1)}, u32[]{:S(2)}, u32[]{:S(2)}) %collective-permute-start.18) | collective-permute-done | bytes 294944 | tf_op jit(solution)/shard_map/ppermute | solution.py:439
  40.4 8.9 %collective-permute-done.20.refs_14_ = bf16[4,96,384]{2,1,0:T(8,128)(2,1)S(1)} collective-permute-done((bf16[4,96,384]{2,1,0:T(8,128)(2,1)S(1)}, bf16[4,96,384]{2,1,0:T(8,128)(2,1)S(1)}, u32[]{:S(2)}, u32[]{:S(2)}) %collective-permute-start.20) | collective-permute-done | bytes 294944 | tf_op jit(solution)/shard_map/ppermute | solution.py:439
  49.4 1.6 %collective-permute-start.15 = (bf16[4,128,384]{2,1,0:T(8,128)(2,1)S(1)}, bf16[4,128,384]{2,1,0:T(8,128)(2,1)S(1)}, u32[]{:S(2)}, u32[]{:S(2)}) collective-permute-start(bf16[4,128,384]{2,1,0:T(8,128)(2,1)S(1)} %slice.14), channel_id=1, source_target_pairs={{0,8},{4,12},{8,0},{12,4},{16,24},{20,28},{24,16},{28,20},{1,9},{5... | collective-permute-start | bytes 1179656 | tf_op jit(solution)/shard_map/ppermute | solution.py:379
  52.1 8.4 %collective-permute-done.22.refs_16_ = bf16[4,96,384]{2,1,0:T(8,128)(2,1)S(1)} collective-permute-done((bf16[4,96,384]{2,1,0:T(8,128)(2,1)S(1)}, bf16[4,96,384]{2,1,0:T(8,128)(2,1)S(1)}, u32[]{:S(2)}, u32[]{:S(2)}) %collective-permute-start.22) | collective-permute-done | bytes 294944 | tf_op jit(solution)/shard_map/ppermute | solution.py:439
  62.3 1.6 %collective-permute-done.23.refs_17_ = bf16[4,96,384]{2,1,0:T(8,128)(2,1)S(1)} collective-permute-done((bf16[4,96,384]{2,1,0:T(8,128)(2,1)S(1)}, bf16[4,96,384]{2,1,0:T(8,128)(2,1)S(1)}, u32[]{:S(2)}, u32[]{:S(2)}) %collective-permute-start.23) | collective-permute-done | bytes 294944 | tf_op jit(solution)/shard_map/ppermute | solution.py:379
  63.9 29.7 %shard_map.50 = (bf16[64,640]{1,0:T(8,128)(2,1)S(1)}, bf16[64,640]{1,0:T(8,128)(2,1)S(1)}, bf16[64,640]{1,0:T(8,128)(2,1)S(1)}, bf16[64,640]{1,0:T(8,128)(2,1)S(...) custom-call(s32[2]{0:T(128)S(1)} %copy-done.2, ...), custom_call_target="tpu_custom_call" | custom-call | tf_op jit(solution)/shard_map/pallas_call | solution.py:481
  94.2 1.4 %collective-permute-start.25 = (bf16[64,640]{1,0:T(8,128)(2,1)S(1)}, bf16[64,640]{1,0:T(8,128)(2,1)S(1)}, u32[]{:S(2)}, u32[]{:S(2)}) collective-permute-start(bf16[64,640]{1,0:T(8,128)(2,1)S(1)} %get-tuple-element.47), channel_id=1, source_target_pairs={{0,8},{4,12},{8,0},{12,4},{16,24},{20,28},{24,16},{28,20},{1,9},{5... | collective-permute-start | bytes 245768 | tf_op jit(solution)/shard_map/ppermute | solution.py:379
  95.5 1.6 %collective-permute-start.26 = (bf16[64,640]{1,0:T(8,128)(2,1)S(1)}, bf16[64,640]{1,0:T(8,128)(2,1)S(1)}, u32[]{:S(2)}, u32[]{:S(2)}) collective-permute-start(bf16[64,640]{1,0:T(8,128)(2,1)S(1)} %get-tuple-element.48), channel_id=1, source_target_pairs={{0,12},{4,8},{8,4},{12,0},{16,28},{20,24},{24,20},{28,16},{1,13},{... | collective-permute-start | bytes 245768 | tf_op jit(solution)/shard_map/ppermute | solution.py:379
  97.2 1.6 %collective-permute-start.28 = (bf16[64,640]{1,0:T(8,128)(2,1)S(1)}, bf16[64,640]{1,0:T(8,128)(2,1)S(1)}, u32[]{:S(2)}, u32[]{:S(2)}) collective-permute-start(bf16[64,640]{1,0:T(8,128)(2,1)S(1)} %get-tuple-element.50), channel_id=1, source_target_pairs={{0,24},{4,28},{8,16},{12,20},{16,8},{20,12},{24,0},{28,4},{1,25},{... | collective-permute-start | bytes 245768 | tf_op jit(solution)/shard_map/ppermute | solution.py:379
  98.8 0.9 collective-permute-start.29
  101.0 0.9 collective-permute-done.27.refs_4_
  102.6 1.8 %collective-permute-done.29.refs_6_ = bf16[64,640]{1,0:T(8,128)(2,1)S(1)} collective-permute-done((bf16[64,640]{1,0:T(8,128)(2,1)S(1)}, bf16[64,640]{1,0:T(8,128)(2,1)S(1)}, u32[]{:S(2)}, u32[]{:S(2)}) %collective-permute-start.29) | collective-permute-done | bytes 81952 | tf_op jit(solution)/shard_map/ppermute | solution.py:379
  104.4 1.6 %shard_map.51 = f32[640,512]{1,0:T(8,128)} custom-call(bf16[64,640]{1,0:T(8,128)(2,1)S(1)} %get-tuple-element.45.refs_0_, bf16[64,640]{1,0:T(8,128)(2,1)S(1)} %collective-permute-done.24.refs_1_, bf16[64,640]{1,0:T(8,128)(2,1)S(1)} %collective-permute-done.25.refs_2_, bf16[64,640]{1,0:T(8,128)(2,1)S(1)} %collective-permute-done.26.refs_3_, ...), custom_call_target="tpu_custom_call" | custom-call | tf_op jit(solution)/shard_map/pallas_call | solution.py:511
  (56 shorter events, 8.1 us)
Async XLA Ops:
  5.1 23.6 %collective-permute-start.5 = (bf16[160,1280]{1,0:T(8,128)(2,1)S(1)}, bf16[160,1280]{1,0:T(8,128)(2,1)S(1)}, u32[]{:S(2)}, u32[]{:S(2)}) collective-permute-start(bf16[160,1280]{1,0:T(8,128)(2,1)S(1)} %get-tuple-element.34), channel_id=1, source_target_pairs={{0,4},{4,0},{8,12},{12,8},{16,20},{20,16},{24,28},{28,24},{1,5},{5... | collective-permute-start | bytes 1228808 | tf_op jit(solution)/shard_map/ppermute | solution.py:379
  8.0 20.7 %collective-permute-start.6 = (bf16[160,1280]{1,0:T(8,128)(2,1)S(1)}, bf16[160,1280]{1,0:T(8,128)(2,1)S(1)}, u32[]{:S(2)}, u32[]{:S(2)}) collective-permute-start(bf16[160,1280]{1,0:T(8,128)(2,1)S(1)} %get-tuple-element.35), channel_id=1, source_target_pairs={{0,8},{4,12},{8,0},{12,4},{16,24},{20,28},{24,16},{28,20},{1,9},{5... | collective-permute-start | bytes 1228808 | tf_op jit(solution)/shard_map/ppermute | solution.py:379
  9.5 19.2 %collective-permute-start.7 = (bf16[160,1280]{1,0:T(8,128)(2,1)S(1)}, bf16[160,1280]{1,0:T(8,128)(2,1)S(1)}, u32[]{:S(2)}, u32[]{:S(2)}) collective-permute-start(bf16[160,1280]{1,0:T(8,128)(2,1)S(1)} %get-tuple-element.36), channel_id=1, source_target_pairs={{0,12},{4,8},{8,4},{12,0},{16,28},{20,24},{24,20},{28,16},{1,13},{... | collective-permute-start | bytes 1228808 | tf_op jit(solution)/shard_map/ppermute | solution.py:379
  9.6 9.2 %collective-permute-start.3 = (bf16[240,384]{1,0:T(8,128)(2,1)S(1)}, bf16[240,384]{1,0:T(8,128)(2,1)S(1)}, u32[]{:S(2)}, u32[]{:S(2)}) collective-permute-start(bf16[240,384]{1,0:T(8,128)(2,1)S(1)} %get-tuple-element.37), channel_id=1, source_target_pairs={{0,3},{1,0},{2,1},{3,2},{4,7},{5,4},{6,5},{7,6},{8,11},{9,8},{10,9... | collective-permute-start | bytes 552968 | tf_op jit(solution)/shard_map/ppermute | solution.py:417
  13.6 15.1 %collective-permute-start.2 = (bf16[240,384]{1,0:T(8,128)(2,1)S(1)}, bf16[240,384]{1,0:T(8,128)(2,1)S(1)}, u32[]{:S(2)}, u32[]{:S(2)}) collective-permute-start(bf16[240,384]{1,0:T(8,128)(2,1)S(1)} %get-tuple-element.37), channel_id=1, source_target_pairs={{0,2},{1,3},{2,0},{3,1},{4,6},{5,7},{6,4},{7,5},{8,10},{9,11},{10,... | collective-permute-start | bytes 552968 | tf_op jit(solution)/shard_map/ppermute | solution.py:417
  18.7 10.0 %collective-permute-start.1 = (bf16[240,384]{1,0:T(8,128)(2,1)S(1)}, bf16[240,384]{1,0:T(8,128)(2,1)S(1)}, u32[]{:S(2)}, u32[]{:S(2)}) collective-permute-start(bf16[240,384]{1,0:T(8,128)(2,1)S(1)} %get-tuple-element.37), channel_id=1, source_target_pairs={{0,1},{1,2},{2,3},{3,0},{4,5},{5,6},{6,7},{7,4},{8,9},{9,10},{10,1... | collective-permute-start | bytes 552968 | tf_op jit(solution)/shard_map/ppermute | solution.py:417
  28.9 20.5 %collective-permute-start.9 = (bf16[4,240,384]{2,1,0:T(8,128)(2,1)S(1)}, bf16[4,240,384]{2,1,0:T(8,128)(2,1)S(1)}, u32[]{:S(2)}, u32[]{:S(2)}) collective-permute-start(bf16[4,240,384]{2,1,0:T(8,128)(2,1)S(1)} %pad_maximum_fusion.refs_0_), channel_id=1, source_target_pairs={{0,4},{4,0},{8,12},{12,8},{16,20},{20,16},{24,28},{28,24},{1,5},{5... | collective-permute-start | bytes 2211848 | tf_op jit(solution)/shard_map/ppermute | solution.py:379
  30.4 9.9 %collective-permute-start.18 = (bf16[4,96,384]{2,1,0:T(8,128)(2,1)S(1)}, bf16[4,96,384]{2,1,0:T(8,128)(2,1)S(1)}, u32[]{:S(2)}, u32[]{:S(2)}) collective-permute-start(bf16[4,96,384]{2,1,0:T(8,128)(2,1)S(1)} %shard_map.49.refs_10_), channel_id=1, source_target_pairs={{0,1},{1,2},{2,3},{3,0},{4,5},{5,6},{6,7},{7,4},{8,9},{9,10},{10,1... | collective-permute-start | bytes 884744 | tf_op jit(solution)/shard_map/ppermute | solution.py:439
  31.3 19.6 %collective-permute-start.11 = (bf16[4,240,384]{2,1,0:T(8,128)(2,1)S(1)}, bf16[4,240,384]{2,1,0:T(8,128)(2,1)S(1)}, u32[]{:S(2)}, u32[]{:S(2)}) collective-permute-start(bf16[4,240,384]{2,1,0:T(8,128)(2,1)S(1)} %pad_maximum_fusion.refs_0_), channel_id=1, source_target_pairs={{0,8},{4,12},{8,0},{12,4},{16,24},{20,28},{24,16},{28,20},{1,9},{5... | collective-permute-start | bytes 2211848 | tf_op jit(solution)/shard_map/ppermute | solution.py:379
  32.9 18.7 %collective-permute-start.8 = (bf16[4,240,384]{2,1,0:T(8,128)(2,1)S(1)}, bf16[4,240,384]{2,1,0:T(8,128)(2,1)S(1)}, u32[]{:S(2)}, u32[]{:S(2)}) collective-permute-start(bf16[4,240,384]{2,1,0:T(8,128)(2,1)S(1)} %pad_maximum_fusion.refs_0_), channel_id=1, source_target_pairs={{0,16},{4,20},{8,24},{12,28},{16,0},{20,4},{24,8},{28,12},{1,17},{... | collective-permute-start | bytes 2211848 | tf_op jit(solution)/shard_map/ppermute | solution.py:379
  40.4 8.9 %collective-permute-start.20 = (bf16[4,96,384]{2,1,0:T(8,128)(2,1)S(1)}, bf16[4,96,384]{2,1,0:T(8,128)(2,1)S(1)}, u32[]{:S(2)}, u32[]{:S(2)}) collective-permute-start(bf16[4,96,384]{2,1,0:T(8,128)(2,1)S(1)} %collective-permute-done.18.refs_12_), channel_id=1, source_target_pairs={{0,1},{1,2},{2,3},{3,0},{4,5},{5,6},{6,7},{7,4},{8,9},{9,10},{10,1... | collective-permute-start | bytes 884744 | tf_op jit(solution)/shard_map/ppermute | solution.py:439
  40.4 9.0 %collective-permute-start.17 = (bf16[4,96,384]{2,1,0:T(8,128)(2,1)S(1)}, bf16[4,96,384]{2,1,0:T(8,128)(2,1)S(1)}, u32[]{:S(2)}, u32[]{:S(2)}) collective-permute-start(bf16[4,96,384]{2,1,0:T(8,128)(2,1)S(1)} %shard_map.49.refs_10_), channel_id=1, source_target_pairs={{0,16},{4,20},{8,24},{12,28},{16,0},{20,4},{24,8},{28,12},{1,17},{... | collective-permute-start | bytes 884744 | tf_op jit(solution)/shard_map/ppermute | solution.py:379
  49.3 11.2 %collective-permute-start.22 = (bf16[4,96,384]{2,1,0:T(8,128)(2,1)S(1)}, bf16[4,96,384]{2,1,0:T(8,128)(2,1)S(1)}, u32[]{:S(2)}, u32[]{:S(2)}) collective-permute-start(bf16[4,96,384]{2,1,0:T(8,128)(2,1)S(1)} %collective-permute-done.20.refs_14_), channel_id=1, source_target_pairs={{0,1},{1,2},{2,3},{3,0},{4,5},{5,6},{6,7},{7,4},{8,9},{9,10},{10,1... | collective-permute-start | bytes 884744 | tf_op jit(solution)/shard_map/ppermute | solution.py:439
  49.4 11.6 %collective-permute-start.15 = (bf16[4,128,384]{2,1,0:T(8,128)(2,1)S(1)}, bf16[4,128,384]{2,1,0:T(8,128)(2,1)S(1)}, u32[]{:S(2)}, u32[]{:S(2)}) collective-permute-start(bf16[4,128,384]{2,1,0:T(8,128)(2,1)S(1)} %slice.14), channel_id=1, source_target_pairs={{0,8},{4,12},{8,0},{12,4},{16,24},{20,28},{24,16},{28,20},{1,9},{5... | collective-permute-start | bytes 1179656 | tf_op jit(solution)/shard_map/ppermute | solution.py:379
  51.0 12.9 %collective-permute-start.12 = (bf16[4,240,384]{2,1,0:T(8,128)(2,1)S(1)}, bf16[4,240,384]{2,1,0:T(8,128)(2,1)S(1)}, u32[]{:S(2)}, u32[]{:S(2)}) collective-permute-start(bf16[4,240,384]{2,1,0:T(8,128)(2,1)S(1)} %collective-permute-done.11.refs_4_), channel_id=1, source_target_pairs={{0,16},{4,20},{8,24},{12,28},{16,0},{20,4},{24,8},{28,12},{1,17},{... | collective-permute-start | bytes 2211848 | tf_op jit(solution)/shard_map/ppermute | solution.py:379
  51.2 12.7 %collective-permute-start.10 = (bf16[4,240,384]{2,1,0:T(8,128)(2,1)S(1)}, bf16[4,240,384]{2,1,0:T(8,128)(2,1)S(1)}, u32[]{:S(2)}, u32[]{:S(2)}) collective-permute-start(bf16[4,240,384]{2,1,0:T(8,128)(2,1)S(1)} %collective-permute-done.9.refs_2_), channel_id=1, source_target_pairs={{0,16},{4,20},{8,24},{12,28},{16,0},{20,4},{24,8},{28,12},{1,17},{... | collective-permute-start | bytes 2211848 | tf_op jit(solution)/shard_map/ppermute | solution.py:379
  51.5 10.2 %collective-permute-start.13 = (bf16[4,112,384]{2,1,0:T(8,128)(2,1)S(1)}, bf16[4,112,384]{2,1,0:T(8,128)(2,1)S(1)}, u32[]{:S(2)}, u32[]{:S(2)}) collective-permute-start(bf16[4,112,384]{2,1,0:T(8,128)(2,1)S(1)} %slice.13), channel_id=1, source_target_pairs={{0,4},{4,0},{8,12},{12,8},{16,20},{20,16},{24,28},{28,24},{1,5},{5... | collective-permute-start | bytes 1032200 | tf_op jit(solution)/shard_map/ppermute | solution.py:379
  93.6 5.2 %collective-permute-start.24 = (bf16[64,640]{1,0:T(8,128)(2,1)S(1)}, bf16[64,640]{1,0:T(8,128)(2,1)S(1)}, u32[]{:S(2)}, u32[]{:S(2)}) collective-permute-start(bf16[64,640]{1,0:T(8,128)(2,1)S(1)} %get-tuple-element.46), channel_id=1, source_target_pairs={{0,4},{4,0},{8,12},{12,8},{16,20},{20,16},{24,28},{28,24},{1,5},{5... | collective-permute-start | bytes 245768 | tf_op jit(solution)/shard_map/ppermute | solution.py:379
  94.2 5.5 %collective-permute-start.25 = (bf16[64,640]{1,0:T(8,128)(2,1)S(1)}, bf16[64,640]{1,0:T(8,128)(2,1)S(1)}, u32[]{:S(2)}, u32[]{:S(2)}) collective-permute-start(bf16[64,640]{1,0:T(8,128)(2,1)S(1)} %get-tuple-element.47), channel_id=1, source_target_pairs={{0,8},{4,12},{8,0},{12,4},{16,24},{20,28},{24,16},{28,20},{1,9},{5... | collective-permute-start | bytes 245768 | tf_op jit(solution)/shard_map/ppermute | solution.py:379
  95.5 5.4 %collective-permute-start.26 = (bf16[64,640]{1,0:T(8,128)(2,1)S(1)}, bf16[64,640]{1,0:T(8,128)(2,1)S(1)}, u32[]{:S(2)}, u32[]{:S(2)}) collective-permute-start(bf16[64,640]{1,0:T(8,128)(2,1)S(1)} %get-tuple-element.48), channel_id=1, source_target_pairs={{0,12},{4,8},{8,4},{12,0},{16,28},{20,24},{24,20},{28,16},{1,13},{... | collective-permute-start | bytes 245768 | tf_op jit(solution)/shard_map/ppermute | solution.py:379
  97.1 4.7 %collective-permute-start.27 = (bf16[64,640]{1,0:T(8,128)(2,1)S(1)}, bf16[64,640]{1,0:T(8,128)(2,1)S(1)}, u32[]{:S(2)}, u32[]{:S(2)}) collective-permute-start(bf16[64,640]{1,0:T(8,128)(2,1)S(1)} %get-tuple-element.49), channel_id=1, source_target_pairs={{0,20},{4,16},{8,28},{12,24},{16,4},{20,0},{24,12},{28,8},{1,21},{... | collective-permute-start | bytes 245768 | tf_op jit(solution)/shard_map/ppermute | solution.py:379
  97.2 5.4 %collective-permute-start.28 = (bf16[64,640]{1,0:T(8,128)(2,1)S(1)}, bf16[64,640]{1,0:T(8,128)(2,1)S(1)}, u32[]{:S(2)}, u32[]{:S(2)}) collective-permute-start(bf16[64,640]{1,0:T(8,128)(2,1)S(1)} %get-tuple-element.50), channel_id=1, source_target_pairs={{0,24},{4,28},{8,16},{12,20},{16,8},{20,12},{24,0},{28,4},{1,25},{... | collective-permute-start | bytes 245768 | tf_op jit(solution)/shard_map/ppermute | solution.py:379
  98.8 5.6 %collective-permute-start.29 = (bf16[64,640]{1,0:T(8,128)(2,1)S(1)}, bf16[64,640]{1,0:T(8,128)(2,1)S(1)}, u32[]{:S(2)}, u32[]{:S(2)}) collective-permute-start(bf16[64,640]{1,0:T(8,128)(2,1)S(1)} %get-tuple-element.51), channel_id=1, source_target_pairs={{0,28},{4,24},{8,20},{12,16},{16,12},{20,8},{24,4},{28,0},{1,29},{... | collective-permute-start | bytes 245768 | tf_op jit(solution)/shard_map/ppermute | solution.py:379
  99.7 4.7 %collective-permute-start.30 = (bf16[64,640]{1,0:T(8,128)(2,1)S(1)}, bf16[64,640]{1,0:T(8,128)(2,1)S(1)}, u32[]{:S(2)}, u32[]{:S(2)}) collective-permute-start(bf16[64,640]{1,0:T(8,128)(2,1)S(1)} %get-tuple-element.52), channel_id=1, source_target_pairs={{0,16},{4,20},{8,24},{12,28},{16,0},{20,4},{24,8},{28,12},{1,17},{... | collective-permute-start | bytes 245768 | tf_op jit(solution)/shard_map/ppermute | solution.py:379
  (11 other events, 24.6 us)

commit v9 on v8

--- a/solution.py
+++ b/solution.py
@@ -15,7 +15,7 @@
 LANES = 128
 CHUNK = 1024
 MOST_TOKENS = 1024
-NEAR_FIRST = (0, 2, 4, 6, 3, 5, 7, 1)
+FLIPS = (0, 6, 2, 4, 7, 3, 5, 1)
 
 
 def two_terms(value):
@@ -195,7 +195,7 @@
     finish(2)
     values[...] = jnp.zeros_like(values)
 
-    lax.fori_loop(0, width // (2 * LANES), norm_and_multiply, 0, unroll=2 if riding else 1)
+    lax.fori_loop(0, width // (2 * LANES), norm_and_multiply, 0, unroll=4 if riding else 1)
 
     picked = []
     for tile, owner in enumerate(owners):
@@ -255,7 +255,7 @@
     for number, out_ref in enumerate(out_refs):
         sub_rows = out_ref.shape[1]
         if len(out_refs) > 1:
-            flip = NEAR_FIRST[number]
+            flip = FLIPS[number]
             sub_block = (row ^ flip // 2) * 2 + (tok ^ flip % 2)
             start = pl.multiple_of(sub_block * sub_rows, LANES)
             out_ref[...] = merged[:, pl.ds(start, sub_rows)].astype(out_ref.dtype)
@@ -347,7 +347,7 @@
 def gather_kernel(*refs):
     out_ref, ordered = refs[-2:]
     row, tok = lax.axis_index("row"), lax.axis_index("tok")
-    for flip, piece in zip(NEAR_FIRST, refs[:-2]):
+    for flip, piece in zip(FLIPS, refs[:-2]):
         held = piece.shape[0]
         start = pl.multiple_of(((row ^ flip // 2) * 2 + (tok ^ flip % 2)) * held, held)
         ordered[pl.ds(start, held), :] = piece[...].astype(jnp.float32)
@@ -507,7 +507,7 @@
         *weight_pieces,
     )
     if paired:
-        arrived = [found[0]] + [swap(x, flip) for x, flip in zip(found[1:], NEAR_FIRST[1:])]
+        arrived = [found[0]] + [swap(x, flip) for x, flip in zip(found[1:], FLIPS[1:])]
         return pl.pallas_call(
             gather_kernel,
             out_shape=jax.ShapeDtypeStruct((sub_rows, col_width), jnp.float32),

time: 106 us -> 106 us (level)
  transfers between devices with their start and end apart: 31 -> 31, of which waited for: 14 -> 16; matrix products, arithmetic and copies ran while one was open for 0% -> 0% of each run, Pallas kernels for 1% -> 1%
where the time goes in v9:
time: 106 us
  waiting for transfers between devices  47.9 us (45%)
  Pallas kernels  32.6 us (31%)
  starting transfers between devices  24 us (23%)
  local copies, waits for them, and re-layouts  1.43 us (1%)
    pallas_call x1, Pallas kernels, body(): pl.pallas_call(functools.partial(solve_kernel, owners, models, block, cop...  29.7 us
    ppermute x3, waiting for transfers between devices, body(): rounds.append(lax.ppermute(rounds[-1], 'col', up))  24.8 us
    ppermute x25, starting transfers between devices, swap(): return lax.ppermute(value, ('tok', 'row'), pairs)  18.2 us
    ppermute x3, waiting for transfers between devices, body(): lax.ppermute(upper, 'col', [(i, (i + shift) % cols) for i in range(cols)])  14.3 us
    ppermute x25, waiting for transfers between devices, swap(): return lax.ppermute(value, ('tok', 'row'), pairs)  8.69 us
    ppermute x3, starting transfers between devices, body(): lax.ppermute(upper, 'col', [(i, (i + shift) % cols) for i in range(cols)])  4.85 us
  transfers between devices with their start and end apart: 31, of which 16 were waited for; matrix products, arithmetic and copies ran while one was open for 0% of the time, Pallas kernels for 1%

profile of v9, /device:TPU:0, one launch (start us, length us, event | category | flops | bytes accessed | tf_op | source)
XLA Modules:
  0.0 106.1 jit_solution(16489027773455043899)
XLA Ops:
  0.0 1.3 %copy-done = bf16[1,1280,512]{2,1,0:T(8,128)(2,1)S(1)} copy-done((bf16[1,1280,512]{2,1,0:T(8,128)(2,1)S(1)}, bf16[1,1280,512]{2,1,0:T(8,128)(2,1)}, u32[]{:S(2)}) %copy-start) | copy-done | bytes 1310744
  2.8 1.4 %collective-permute-done.given_ref = bf16[320,128]{1,0:T(8,128)(2,1)S(1)} collective-permute-done((bf16[320,128]{1,0:T(8,128)(2,1)S(1)}, bf16[320,128]{1,0:T(8,128)(2,1)S(1)}, u32[]{:S(2)}, u32[]{:S(2)}) %collective-permute-start) | collective-permute-done | bytes 81952 | tf_op jit(solution)/shard_map/ppermute | solution.py:379
  5.1 2.9 %collective-permute-start.5 = (bf16[160,1280]{1,0:T(8,128)(2,1)S(1)}, bf16[160,1280]{1,0:T(8,128)(2,1)S(1)}, u32[]{:S(2)}, u32[]{:S(2)}) collective-permute-start(bf16[160,1280]{1,0:T(8,128)(2,1)S(1)} %get-tuple-element.34), channel_id=1, source_target_pairs={{0,4},{4,0},{8,12},{12,8},{16,20},{20,16},{24,28},{28,24},{1,5},{5... | collective-permute-start | bytes 1228808 | tf_op jit(solution)/shard_map/ppermute | solution.py:379
  8.0 1.5 %collective-permute-start.6 = (bf16[160,1280]{1,0:T(8,128)(2,1)S(1)}, bf16[160,1280]{1,0:T(8,128)(2,1)S(1)}, u32[]{:S(2)}, u32[]{:S(2)}) collective-permute-start(bf16[160,1280]{1,0:T(8,128)(2,1)S(1)} %get-tuple-element.35), channel_id=1, source_target_pairs={{0,8},{4,12},{8,0},{12,4},{16,24},{20,28},{24,16},{28,20},{1,9},{5... | collective-permute-start | bytes 1228808 | tf_op jit(solution)/shard_map/ppermute | solution.py:379
  9.6 4.1 %collective-permute-start.3 = (bf16[240,384]{1,0:T(8,128)(2,1)S(1)}, bf16[240,384]{1,0:T(8,128)(2,1)S(1)}, u32[]{:S(2)}, u32[]{:S(2)}) collective-permute-start(bf16[240,384]{1,0:T(8,128)(2,1)S(1)} %get-tuple-element.37), channel_id=1, source_target_pairs={{0,3},{1,0},{2,1},{3,2},{4,7},{5,4},{6,5},{7,6},{8,11},{9,8},{10,9... | collective-permute-start | bytes 552968 | tf_op jit(solution)/shard_map/ppermute | solution.py:417
  13.6 5.1 %collective-permute-done.3 = bf16[240,384]{1,0:T(8,128)(2,1)S(1)} collective-permute-done((bf16[240,384]{1,0:T(8,128)(2,1)S(1)}, bf16[240,384]{1,0:T(8,128)(2,1)S(1)}, u32[]{:S(2)}, u32[]{:S(2)}) %collective-permute-start.3) | collective-permute-done | bytes 184352 | tf_op jit(solution)/shard_map/ppermute | solution.py:417
  18.7 0.8 collective-permute-start.1
  19.5 9.2 %collective-permute-done.2 = bf16[240,384]{1,0:T(8,128)(2,1)S(1)} collective-permute-done((bf16[240,384]{1,0:T(8,128)(2,1)S(1)}, bf16[240,384]{1,0:T(8,128)(2,1)S(1)}, u32[]{:S(2)}, u32[]{:S(2)}) %collective-permute-start.2) | collective-permute-done | bytes 184352 | tf_op jit(solution)/shard_map/ppermute | solution.py:417
  28.9 1.6 %collective-permute-start.9 = (bf16[4,240,384]{2,1,0:T(8,128)(2,1)S(1)}, bf16[4,240,384]{2,1,0:T(8,128)(2,1)S(1)}, u32[]{:S(2)}, u32[]{:S(2)}) collective-permute-start(bf16[4,240,384]{2,1,0:T(8,128)(2,1)S(1)} %pad_maximum_fusion.refs_0_), channel_id=1, source_target_pairs={{0,4},{4,0},{8,12},{12,8},{16,20},{20,16},{24,28},{28,24},{1,5},{5... | collective-permute-start | bytes 2211848 | tf_op jit(solution)/shard_map/ppermute | solution.py:379
  30.4 0.9 collective-permute-start.18
  31.3 1.5 %collective-permute-start.11 = (bf16[4,240,384]{2,1,0:T(8,128)(2,1)S(1)}, bf16[4,240,384]{2,1,0:T(8,128)(2,1)S(1)}, u32[]{:S(2)}, u32[]{:S(2)}) collective-permute-start(bf16[4,240,384]{2,1,0:T(8,128)(2,1)S(1)} %pad_maximum_fusion.refs_0_), channel_id=1, source_target_pairs={{0,8},{4,12},{8,0},{12,4},{16,24},{20,28},{24,16},{28,20},{1,9},{5... | collective-permute-start | bytes 2211848 | tf_op jit(solution)/shard_map/ppermute | solution.py:379
  32.9 7.5 %collective-permute-done.18.refs_12_ = bf16[4,96,384]{2,1,0:T(8,128)(2,1)S(1)} collective-permute-done((bf16[4,96,384]{2,1,0:T(8,128)(2,1)S(1)}, bf16[4,96,384]{2,1,0:T(8,128)(2,1)S(1)}, u32[]{:S(2)}, u32[]{:S(2)}) %collective-permute-start.18) | collective-permute-done | bytes 294944 | tf_op jit(solution)/shard_map/ppermute | solution.py:439
  40.4 8.9 %collective-permute-done.20.refs_14_ = bf16[4,96,384]{2,1,0:T(8,128)(2,1)S(1)} collective-permute-done((bf16[4,96,384]{2,1,0:T(8,128)(2,1)S(1)}, bf16[4,96,384]{2,1,0:T(8,128)(2,1)S(1)}, u32[]{:S(2)}, u32[]{:S(2)}) %collective-permute-start.20) | collective-permute-done | bytes 294944 | tf_op jit(solution)/shard_map/ppermute | solution.py:439
  49.4 1.6 %collective-permute-start.15 = (bf16[4,128,384]{2,1,0:T(8,128)(2,1)S(1)}, bf16[4,128,384]{2,1,0:T(8,128)(2,1)S(1)}, u32[]{:S(2)}, u32[]{:S(2)}) collective-permute-start(bf16[4,128,384]{2,1,0:T(8,128)(2,1)S(1)} %slice.14), channel_id=1, source_target_pairs={{0,8},{4,12},{8,0},{12,4},{16,24},{20,28},{24,16},{28,20},{1,9},{5... | collective-permute-start | bytes 1179656 | tf_op jit(solution)/shard_map/ppermute | solution.py:379
  52.1 8.4 %collective-permute-done.22.refs_16_ = bf16[4,96,384]{2,1,0:T(8,128)(2,1)S(1)} collective-permute-done((bf16[4,96,384]{2,1,0:T(8,128)(2,1)S(1)}, bf16[4,96,384]{2,1,0:T(8,128)(2,1)S(1)}, u32[]{:S(2)}, u32[]{:S(2)}) %collective-permute-start.22) | collective-permute-done | bytes 294944 | tf_op jit(solution)/shard_map/ppermute | solution.py:439
  62.3 1.6 %collective-permute-done.23.refs_17_ = bf16[4,96,384]{2,1,0:T(8,128)(2,1)S(1)} collective-permute-done((bf16[4,96,384]{2,1,0:T(8,128)(2,1)S(1)}, bf16[4,96,384]{2,1,0:T(8,128)(2,1)S(1)}, u32[]{:S(2)}, u32[]{:S(2)}) %collective-permute-start.23) | collective-permute-done | bytes 294944 | tf_op jit(solution)/shard_map/ppermute | solution.py:379
  63.9 29.7 %shard_map.50 = (bf16[64,640]{1,0:T(8,128)(2,1)S(1)}, bf16[64,640]{1,0:T(8,128)(2,1)S(1)}, bf16[64,640]{1,0:T(8,128)(2,1)S(1)}, bf16[64,640]{1,0:T(8,128)(2,1)S(...) custom-call(s32[2]{0:T(128)S(1)} %copy-done.2, ...), custom_call_target="tpu_custom_call" | custom-call | tf_op jit(solution)/shard_map/pallas_call | solution.py:481
  93.6 1.4 %collective-permute-start.24 = (bf16[64,640]{1,0:T(8,128)(2,1)S(1)}, bf16[64,640]{1,0:T(8,128)(2,1)S(1)}, u32[]{:S(2)}, u32[]{:S(2)}) collective-permute-start(bf16[64,640]{1,0:T(8,128)(2,1)S(1)} %get-tuple-element.46), channel_id=1, source_target_pairs={{0,12},{4,8},{8,4},{12,0},{16,28},{20,24},{24,20},{28,16},{1,13},{... | collective-permute-start | bytes 245768 | tf_op jit(solution)/shard_map/ppermute | solution.py:379
  94.9 1.5 %collective-permute-start.25 = (bf16[64,640]{1,0:T(8,128)(2,1)S(1)}, bf16[64,640]{1,0:T(8,128)(2,1)S(1)}, u32[]{:S(2)}, u32[]{:S(2)}) collective-permute-start(bf16[64,640]{1,0:T(8,128)(2,1)S(1)} %get-tuple-element.47), channel_id=1, source_target_pairs={{0,4},{4,0},{8,12},{12,8},{16,20},{20,16},{24,28},{28,24},{1,5},{5... | collective-permute-start | bytes 245768 | tf_op jit(solution)/shard_map/ppermute | solution.py:379
  97.3 2.3 %collective-permute-start.28 = (bf16[64,640]{1,0:T(8,128)(2,1)S(1)}, bf16[64,640]{1,0:T(8,128)(2,1)S(1)}, u32[]{:S(2)}, u32[]{:S(2)}) collective-permute-start(bf16[64,640]{1,0:T(8,128)(2,1)S(1)} %get-tuple-element.50), channel_id=1, source_target_pairs={{0,20},{4,16},{8,28},{12,24},{16,4},{20,0},{24,12},{28,8},{1,21},{... | collective-permute-start | bytes 245768 | tf_op jit(solution)/shard_map/ppermute | solution.py:379
  99.8 0.8 collective-permute-done.25.refs_2_
  101.3 1.3 %collective-permute-done.26.refs_3_ = bf16[64,640]{1,0:T(8,128)(2,1)S(1)} collective-permute-done((bf16[64,640]{1,0:T(8,128)(2,1)S(1)}, bf16[64,640]{1,0:T(8,128)(2,1)S(1)}, u32[]{:S(2)}, u32[]{:S(2)}) %collective-permute-start.26) | collective-permute-done | bytes 81952 | tf_op jit(solution)/shard_map/ppermute | solution.py:379
  102.9 1.3 %collective-permute-done.28.refs_5_ = bf16[64,640]{1,0:T(8,128)(2,1)S(1)} collective-permute-done((bf16[64,640]{1,0:T(8,128)(2,1)S(1)}, bf16[64,640]{1,0:T(8,128)(2,1)S(1)}, u32[]{:S(2)}, u32[]{:S(2)}) %collective-permute-start.28) | collective-permute-done | bytes 81952 | tf_op jit(solution)/shard_map/ppermute | solution.py:379
  104.5 1.6 %shard_map.51 = f32[640,512]{1,0:T(8,128)} custom-call(bf16[64,640]{1,0:T(8,128)(2,1)S(1)} %get-tuple-element.45.refs_0_, bf16[64,640]{1,0:T(8,128)(2,1)S(1)} %collective-permute-done.24.refs_1_, bf16[64,640]{1,0:T(8,128)(2,1)S(1)} %collective-permute-done.25.refs_2_, bf16[64,640]{1,0:T(8,128)(2,1)S(1)} %collective-permute-done.26.refs_3_, ...), custom_call_target="tpu_custom_call" | custom-call | tf_op jit(solution)/shard_map/pallas_call | solution.py:511
  (56 shorter events, 7.9 us)
Async XLA Ops:
  5.1 23.6 %collective-permute-start.5 = (bf16[160,1280]{1,0:T(8,128)(2,1)S(1)}, bf16[160,1280]{1,0:T(8,128)(2,1)S(1)}, u32[]{:S(2)}, u32[]{:S(2)}) collective-permute-start(bf16[160,1280]{1,0:T(8,128)(2,1)S(1)} %get-tuple-element.34), channel_id=1, source_target_pairs={{0,4},{4,0},{8,12},{12,8},{16,20},{20,16},{24,28},{28,24},{1,5},{5... | collective-permute-start | bytes 1228808 | tf_op jit(solution)/shard_map/ppermute | solution.py:379
  8.0 20.7 %collective-permute-start.6 = (bf16[160,1280]{1,0:T(8,128)(2,1)S(1)}, bf16[160,1280]{1,0:T(8,128)(2,1)S(1)}, u32[]{:S(2)}, u32[]{:S(2)}) collective-permute-start(bf16[160,1280]{1,0:T(8,128)(2,1)S(1)} %get-tuple-element.35), channel_id=1, source_target_pairs={{0,8},{4,12},{8,0},{12,4},{16,24},{20,28},{24,16},{28,20},{1,9},{5... | collective-permute-start | bytes 1228808 | tf_op jit(solution)/shard_map/ppermute | solution.py:379
  9.5 19.2 %collective-permute-start.7 = (bf16[160,1280]{1,0:T(8,128)(2,1)S(1)}, bf16[160,1280]{1,0:T(8,128)(2,1)S(1)}, u32[]{:S(2)}, u32[]{:S(2)}) collective-permute-start(bf16[160,1280]{1,0:T(8,128)(2,1)S(1)} %get-tuple-element.36), channel_id=1, source_target_pairs={{0,12},{4,8},{8,4},{12,0},{16,28},{20,24},{24,20},{28,16},{1,13},{... | collective-permute-start | bytes 1228808 | tf_op jit(solution)/shard_map/ppermute | solution.py:379
  9.6 9.2 %collective-permute-start.3 = (bf16[240,384]{1,0:T(8,128)(2,1)S(1)}, bf16[240,384]{1,0:T(8,128)(2,1)S(1)}, u32[]{:S(2)}, u32[]{:S(2)}) collective-permute-start(bf16[240,384]{1,0:T(8,128)(2,1)S(1)} %get-tuple-element.37), channel_id=1, source_target_pairs={{0,3},{1,0},{2,1},{3,2},{4,7},{5,4},{6,5},{7,6},{8,11},{9,8},{10,9... | collective-permute-start | bytes 552968 | tf_op jit(solution)/shard_map/ppermute | solution.py:417
  13.6 15.1 %collective-permute-start.2 = (bf16[240,384]{1,0:T(8,128)(2,1)S(1)}, bf16[240,384]{1,0:T(8,128)(2,1)S(1)}, u32[]{:S(2)}, u32[]{:S(2)}) collective-permute-start(bf16[240,384]{1,0:T(8,128)(2,1)S(1)} %get-tuple-element.37), channel_id=1, source_target_pairs={{0,2},{1,3},{2,0},{3,1},{4,6},{5,7},{6,4},{7,5},{8,10},{9,11},{10,... | collective-permute-start | bytes 552968 | tf_op jit(solution)/shard_map/ppermute | solution.py:417
  18.7 10.0 %collective-permute-start.1 = (bf16[240,384]{1,0:T(8,128)(2,1)S(1)}, bf16[240,384]{1,0:T(8,128)(2,1)S(1)}, u32[]{:S(2)}, u32[]{:S(2)}) collective-permute-start(bf16[240,384]{1,0:T(8,128)(2,1)S(1)} %get-tuple-element.37), channel_id=1, source_target_pairs={{0,1},{1,2},{2,3},{3,0},{4,5},{5,6},{6,7},{7,4},{8,9},{9,10},{10,1... | collective-permute-start | bytes 552968 | tf_op jit(solution)/shard_map/ppermute | solution.py:417
  28.9 20.5 %collective-permute-start.9 = (bf16[4,240,384]{2,1,0:T(8,128)(2,1)S(1)}, bf16[4,240,384]{2,1,0:T(8,128)(2,1)S(1)}, u32[]{:S(2)}, u32[]{:S(2)}) collective-permute-start(bf16[4,240,384]{2,1,0:T(8,128)(2,1)S(1)} %pad_maximum_fusion.refs_0_), channel_id=1, source_target_pairs={{0,4},{4,0},{8,12},{12,8},{16,20},{20,16},{24,28},{28,24},{1,5},{5... | collective-permute-start | bytes 2211848 | tf_op jit(solution)/shard_map/ppermute | solution.py:379
  30.4 9.9 %collective-permute-start.18 = (bf16[4,96,384]{2,1,0:T(8,128)(2,1)S(1)}, bf16[4,96,384]{2,1,0:T(8,128)(2,1)S(1)}, u32[]{:S(2)}, u32[]{:S(2)}) collective-permute-start(bf16[4,96,384]{2,1,0:T(8,128)(2,1)S(1)} %shard_map.49.refs_10_), channel_id=1, source_target_pairs={{0,1},{1,2},{2,3},{3,0},{4,5},{5,6},{6,7},{7,4},{8,9},{9,10},{10,1... | collective-permute-start | bytes 884744 | tf_op jit(solution)/shard_map/ppermute | solution.py:439
  31.3 19.6 %collective-permute-start.11 = (bf16[4,240,384]{2,1,0:T(8,128)(2,1)S(1)}, bf16[4,240,384]{2,1,0:T(8,128)(2,1)S(1)}, u32[]{:S(2)}, u32[]{:S(2)}) collective-permute-start(bf16[4,240,384]{2,1,0:T(8,128)(2,1)S(1)} %pad_maximum_fusion.refs_0_), channel_id=1, source_target_pairs={{0,8},{4,12},{8,0},{12,4},{16,24},{20,28},{24,16},{28,20},{1,9},{5... | collective-permute-start | bytes 2211848 | tf_op jit(solution)/shard_map/ppermute | solution.py:379
  32.9 18.7 %collective-permute-start.8 = (bf16[4,240,384]{2,1,0:T(8,128)(2,1)S(1)}, bf16[4,240,384]{2,1,0:T(8,128)(2,1)S(1)}, u32[]{:S(2)}, u32[]{:S(2)}) collective-permute-start(bf16[4,240,384]{2,1,0:T(8,128)(2,1)S(1)} %pad_maximum_fusion.refs_0_), channel_id=1, source_target_pairs={{0,16},{4,20},{8,24},{12,28},{16,0},{20,4},{24,8},{28,12},{1,17},{... | collective-permute-start | bytes 2211848 | tf_op jit(solution)/shard_map/ppermute | solution.py:379
  40.4 8.9 %collective-permute-start.20 = (bf16[4,96,384]{2,1,0:T(8,128)(2,1)S(1)}, bf16[4,96,384]{2,1,0:T(8,128)(2,1)S(1)}, u32[]{:S(2)}, u32[]{:S(2)}) collective-permute-start(bf16[4,96,384]{2,1,0:T(8,128)(2,1)S(1)} %collective-permute-done.18.refs_12_), channel_id=1, source_target_pairs={{0,1},{1,2},{2,3},{3,0},{4,5},{5,6},{6,7},{7,4},{8,9},{9,10},{10,1... | collective-permute-start | bytes 884744 | tf_op jit(solution)/shard_map/ppermute | solution.py:439
  40.4 9.0 %collective-permute-start.17 = (bf16[4,96,384]{2,1,0:T(8,128)(2,1)S(1)}, bf16[4,96,384]{2,1,0:T(8,128)(2,1)S(1)}, u32[]{:S(2)}, u32[]{:S(2)}) collective-permute-start(bf16[4,96,384]{2,1,0:T(8,128)(2,1)S(1)} %shard_map.49.refs_10_), channel_id=1, source_target_pairs={{0,16},{4,20},{8,24},{12,28},{16,0},{20,4},{24,8},{28,12},{1,17},{... | collective-permute-start | bytes 884744 | tf_op jit(solution)/shard_map/ppermute | solution.py:379
  49.3 11.2 %collective-permute-start.22 = (bf16[4,96,384]{2,1,0:T(8,128)(2,1)S(1)}, bf16[4,96,384]{2,1,0:T(8,128)(2,1)S(1)}, u32[]{:S(2)}, u32[]{:S(2)}) collective-permute-start(bf16[4,96,384]{2,1,0:T(8,128)(2,1)S(1)} %collective-permute-done.20.refs_14_), channel_id=1, source_target_pairs={{0,1},{1,2},{2,3},{3,0},{4,5},{5,6},{6,7},{7,4},{8,9},{9,10},{10,1... | collective-permute-start | bytes 884744 | tf_op jit(solution)/shard_map/ppermute | solution.py:439
  49.4 11.6 %collective-permute-start.15 = (bf16[4,128,384]{2,1,0:T(8,128)(2,1)S(1)}, bf16[4,128,384]{2,1,0:T(8,128)(2,1)S(1)}, u32[]{:S(2)}, u32[]{:S(2)}) collective-permute-start(bf16[4,128,384]{2,1,0:T(8,128)(2,1)S(1)} %slice.14), channel_id=1, source_target_pairs={{0,8},{4,12},{8,0},{12,4},{16,24},{20,28},{24,16},{28,20},{1,9},{5... | collective-permute-start | bytes 1179656 | tf_op jit(solution)/shard_map/ppermute | solution.py:379
  51.0 12.9 %collective-permute-start.12 = (bf16[4,240,384]{2,1,0:T(8,128)(2,1)S(1)}, bf16[4,240,384]{2,1,0:T(8,128)(2,1)S(1)}, u32[]{:S(2)}, u32[]{:S(2)}) collective-permute-start(bf16[4,240,384]{2,1,0:T(8,128)(2,1)S(1)} %collective-permute-done.11.refs_4_), channel_id=1, source_target_pairs={{0,16},{4,20},{8,24},{12,28},{16,0},{20,4},{24,8},{28,12},{1,17},{... | collective-permute-start | bytes 2211848 | tf_op jit(solution)/shard_map/ppermute | solution.py:379
  51.2 12.7 %collective-permute-start.10 = (bf16[4,240,384]{2,1,0:T(8,128)(2,1)S(1)}, bf16[4,240,384]{2,1,0:T(8,128)(2,1)S(1)}, u32[]{:S(2)}, u32[]{:S(2)}) collective-permute-start(bf16[4,240,384]{2,1,0:T(8,128)(2,1)S(1)} %collective-permute-done.9.refs_2_), channel_id=1, source_target_pairs={{0,16},{4,20},{8,24},{12,28},{16,0},{20,4},{24,8},{28,12},{1,17},{... | collective-permute-start | bytes 2211848 | tf_op jit(solution)/shard_map/ppermute | solution.py:379
  51.5 10.2 %collective-permute-start.13 = (bf16[4,112,384]{2,1,0:T(8,128)(2,1)S(1)}, bf16[4,112,384]{2,1,0:T(8,128)(2,1)S(1)}, u32[]{:S(2)}, u32[]{:S(2)}) collective-permute-start(bf16[4,112,384]{2,1,0:T(8,128)(2,1)S(1)} %slice.13), channel_id=1, source_target_pairs={{0,4},{4,0},{8,12},{12,8},{16,20},{20,16},{24,28},{28,24},{1,5},{5... | collective-permute-start | bytes 1032200 | tf_op jit(solution)/shard_map/ppermute | solution.py:379
  93.6 6.3 %collective-permute-start.24 = (bf16[64,640]{1,0:T(8,128)(2,1)S(1)}, bf16[64,640]{1,0:T(8,128)(2,1)S(1)}, u32[]{:S(2)}, u32[]{:S(2)}) collective-permute-start(bf16[64,640]{1,0:T(8,128)(2,1)S(1)} %get-tuple-element.46), channel_id=1, source_target_pairs={{0,12},{4,8},{8,4},{12,0},{16,28},{20,24},{24,20},{28,16},{1,13},{... | collective-permute-start | bytes 245768 | tf_op jit(solution)/shard_map/ppermute | solution.py:379
  94.9 5.7 %collective-permute-start.25 = (bf16[64,640]{1,0:T(8,128)(2,1)S(1)}, bf16[64,640]{1,0:T(8,128)(2,1)S(1)}, u32[]{:S(2)}, u32[]{:S(2)}) collective-permute-start(bf16[64,640]{1,0:T(8,128)(2,1)S(1)} %get-tuple-element.47), channel_id=1, source_target_pairs={{0,4},{4,0},{8,12},{12,8},{16,20},{20,16},{24,28},{28,24},{1,5},{5... | collective-permute-start | bytes 245768 | tf_op jit(solution)/shard_map/ppermute | solution.py:379
  96.4 6.1 %collective-permute-start.26 = (bf16[64,640]{1,0:T(8,128)(2,1)S(1)}, bf16[64,640]{1,0:T(8,128)(2,1)S(1)}, u32[]{:S(2)}, u32[]{:S(2)}) collective-permute-start(bf16[64,640]{1,0:T(8,128)(2,1)S(1)} %get-tuple-element.48), channel_id=1, source_target_pairs={{0,8},{4,12},{8,0},{12,4},{16,24},{20,28},{24,16},{28,20},{1,9},{5... | collective-permute-start | bytes 245768 | tf_op jit(solution)/shard_map/ppermute | solution.py:379
  97.1 5.8 %collective-permute-start.27 = (bf16[64,640]{1,0:T(8,128)(2,1)S(1)}, bf16[64,640]{1,0:T(8,128)(2,1)S(1)}, u32[]{:S(2)}, u32[]{:S(2)}) collective-permute-start(bf16[64,640]{1,0:T(8,128)(2,1)S(1)} %get-tuple-element.49), channel_id=1, source_target_pairs={{0,28},{4,24},{8,20},{12,16},{16,12},{20,8},{24,4},{28,0},{1,29},{... | collective-permute-start | bytes 245768 | tf_op jit(solution)/shard_map/ppermute | solution.py:379
  97.3 6.8 %collective-permute-start.28 = (bf16[64,640]{1,0:T(8,128)(2,1)S(1)}, bf16[64,640]{1,0:T(8,128)(2,1)S(1)}, u32[]{:S(2)}, u32[]{:S(2)}) collective-permute-start(bf16[64,640]{1,0:T(8,128)(2,1)S(1)} %get-tuple-element.50), channel_id=1, source_target_pairs={{0,20},{4,16},{8,28},{12,24},{16,4},{20,0},{24,12},{28,8},{1,21},{... | collective-permute-start | bytes 245768 | tf_op jit(solution)/shard_map/ppermute | solution.py:379
  99.8 4.7 %collective-permute-start.29 = (bf16[64,640]{1,0:T(8,128)(2,1)S(1)}, bf16[64,640]{1,0:T(8,128)(2,1)S(1)}, u32[]{:S(2)}, u32[]{:S(2)}) collective-permute-start(bf16[64,640]{1,0:T(8,128)(2,1)S(1)} %get-tuple-element.51), channel_id=1, source_target_pairs={{0,24},{4,28},{8,16},{12,20},{16,8},{20,12},{24,0},{28,4},{1,25},{... | collective-permute-start | bytes 245768 | tf_op jit(solution)/shard_map/ppermute | solution.py:379
  100.6 3.9 %collective-permute-start.30 = (bf16[64,640]{1,0:T(8,128)(2,1)S(1)}, bf16[64,640]{1,0:T(8,128)(2,1)S(1)}, u32[]{:S(2)}, u32[]{:S(2)}) collective-permute-start(bf16[64,640]{1,0:T(8,128)(2,1)S(1)} %get-tuple-element.52), channel_id=1, source_target_pairs={{0,16},{4,20},{8,24},{12,28},{16,0},{20,4},{24,8},{28,12},{1,17},{... | collective-permute-start | bytes 245768 | tf_op jit(solution)/shard_map/ppermute | solution.py:379
  (11 other events, 24.6 us)
